TPU v7x, 32 devices: a whole 2x2x4 slice. The times are simulated.
32 devices in a mesh: grp: 16 (over z, y, x), in: 2 (over core).
Axes of the slice: x: 2, y: 2, z: 4, core: 2. Of those that a mesh axis runs over, the one named last changes fastest.
Arguments:
- inputs: bfloat16 [2, 16, 384, 2048], P(None, 'grp', 'in'), may hold values from -6 to 6
- cotangent: bfloat16 [2, 16, 384, 2048], P(None, 'grp', 'in'), may hold values from -6 to 6
- lengths: int32 [2, 16], P(None, 'grp'), may hold values from 153 to 384, as said below
- w_query: bfloat16 [2048, 2048], P(('grp', 'in')), may hold values from -0.125 to 0.125
- w_key: bfloat16 [2048, 2048], P(('grp', 'in')), may hold values from -0.125 to 0.125
- w_value: bfloat16 [2048, 2048], P(('grp', 'in')), may hold values from -0.125 to 0.125
- w_out: bfloat16 [2048, 2048], P(('grp', 'in')), may hold values from -0.5 to 0.5
- w_gate: bfloat16 [2048, 5632], P(('grp', 'in')), may hold values from -0.125 to 0.125
- w_up: bfloat16 [2048, 5632], P(('grp', 'in')), may hold values from -0.125 to 0.125
- w_down: bfloat16 [5632, 2048], P(('grp', 'in')), may hold values from -0.15625 to 0.15625
- norm_attn: bfloat16 [2048], P(('grp', 'in')), may hold values from 0.5 to 1.5
- norm_head: bfloat16 [2048], P(('grp', 'in')), may hold values from 0.5 to 1.5
- norm_ffn: bfloat16 [2048], P(('grp', 'in')), may hold values from 0.5 to 1.5
- lambda_params: bfloat16 [512], P(('grp', 'in')), may hold values from -0.099609375 to 0.099609375
Outputs:
- output: bfloat16 [2, 16, 384, 2048], P(None, 'grp', 'in')
- input_grad: bfloat16 [2, 16, 384, 2048], P(None, 'grp', 'in')
- grad_w_query: float32 [2048, 2048], P(('grp', 'in'))
- grad_w_key: float32 [2048, 2048], P(('grp', 'in'))
- grad_w_value: float32 [2048, 2048], P(('grp', 'in'))
- grad_w_out: float32 [2048, 2048], P(('grp', 'in'))
- grad_w_gate: float32 [2048, 5632], P(('grp', 'in'))
- grad_w_up: float32 [2048, 5632], P(('grp', 'in'))
- grad_w_down: float32 [5632, 2048], P(('grp', 'in'))
- grad_norm_attn: float32 [2048], P(('grp', 'in'))
- grad_norm_head: float32 [2048], P(('grp', 'in'))
- grad_norm_ffn: float32 [2048], P(('grp', 'in'))
- grad_lambda: float32 [512], P(('grp', 'in'))
Inputs may be any that keep to these rules, and one draw needn't show every extreme that they name: Every slot index s has lengths[m, s] = 384 for at least one micro-batch m.
All inputs are finite; a program needn't handle non-finite values.
Results may differ from a plain program's by a relative error of at most 0.018.
The roundings to bfloat16 on the way count: a program that leaves them out, or rounds other values in their place, can miss the bound.
Values may be sent and summed in bfloat16 or wider, within the bound.
No kernel may reach another device: no remote copies, remote signals or barrier semaphores. Data moves between devices by JAX's collectives and lax.ppermute only.
A program may use at most 448 MiB of HBM per device.

v0:
```python
import math

import jax
import jax.numpy as jnp
from jax import lax
from jax.sharding import PartitionSpec as P

H = 8
DH = 128


epsilon = 1e-05
lambda_init = 0.8 - 0.6 * math.exp(-3.3)
rope_base = 10000.0


def product(left, right):
    return jnp.dot(left, right, preferred_element_type=jnp.float32)


def contract_rows(left, right):
    return lax.dot_general(
        left, right, (((0,), (0,)), ((), ())), preferred_element_type=jnp.float32
    )


def against(left, right):
    return lax.dot_general(
        left, right, (((1,), (1,)), ((), ())), preferred_element_type=jnp.float32
    )


def norm_back(grad_unit, unit_vals, inverse):
    return inverse * (
        grad_unit - unit_vals * jnp.mean(grad_unit * unit_vals, axis=-1, keepdims=True)
    )


def rope_tables(positions, half_width):
    frequency = rope_base ** (-jnp.arange(half_width, dtype=jnp.float32) / half_width)
    angles = positions.astype(jnp.float32)[:, None] * frequency[None, :]
    return (jnp.cos(angles)[:, None, None, :], jnp.sin(angles)[:, None, None, :])


def rotate(values, cos_table, sin_table, direction):
    half_width = values.shape[-1] // 2
    first_half = values[..., :half_width]
    second_half = values[..., half_width:]
    return jnp.concatenate(
        [
            first_half * cos_table - direction * second_half * sin_table,
            second_half * cos_table + direction * first_half * sin_table,
        ],
        axis=-1,
    )


def fetch_weights(
    w_query,
    w_key,
    w_value,
    w_out,
    w_gate,
    w_up,
    w_down,
    norm_attn,
    norm_head,
    norm_ffn,
    lambda_params,
):
    return (
        lax.all_gather(w_query, ("grp", "in"), axis=0, tiled=True),
        lax.all_gather(w_key, ("grp", "in"), axis=0, tiled=True),
        lax.all_gather(w_value, ("grp", "in"), axis=0, tiled=True),
        lax.all_gather(w_out, ("grp", "in"), axis=0, tiled=True),
        lax.all_gather(w_gate, ("grp", "in"), axis=0, tiled=True),
        lax.all_gather(w_up, ("grp", "in"), axis=0, tiled=True),
        lax.all_gather(w_down, ("grp", "in"), axis=0, tiled=True),
        lax.all_gather(norm_attn, ("grp", "in"), axis=0, tiled=True),
        lax.all_gather(norm_head, ("grp", "in"), axis=0, tiled=True),
        lax.all_gather(norm_ffn, ("grp", "in"), axis=0, tiled=True),
        lax.all_gather(lambda_params, ("grp", "in"), axis=0, tiled=True),
    )


def reduce_ffn(group):
    return (
        lax.psum_scatter(group[0], ("grp", "in"), scatter_dimension=0, tiled=True),
        lax.psum_scatter(group[1], ("grp", "in"), scatter_dimension=0, tiled=True),
        lax.psum_scatter(group[2], ("grp", "in"), scatter_dimension=0, tiled=True),
        lax.psum_scatter(group[3], ("grp", "in"), scatter_dimension=0, tiled=True),
    )


def reduce_attn(group):
    return (
        lax.psum_scatter(group[0], ("grp", "in"), scatter_dimension=0, tiled=True),
        lax.psum_scatter(group[1], ("grp", "in"), scatter_dimension=0, tiled=True),
        lax.psum_scatter(group[2], ("grp", "in"), scatter_dimension=0, tiled=True),
        lax.psum_scatter(group[3], ("grp", "in"), scatter_dimension=0, tiled=True),
        lax.psum_scatter(group[4], ("grp", "in"), scatter_dimension=0, tiled=True),
        lax.psum_scatter(group[5], ("grp", "in"), scatter_dimension=0, tiled=True),
        lax.psum_scatter(group[6], ("grp", "in"), scatter_dimension=0, tiled=True),
    )


def forward(weights, seq_in, length, positions, cos_table, sin_table):
    (
        w_query,
        w_key,
        w_value,
        w_out,
        w_gate,
        w_up,
        w_down,
        norm_attn,
        norm_head,
        norm_ffn,
        lambda_params,
    ) = weights
    local_rows, width = seq_in.shape
    score_scale = 1.0 / math.sqrt(DH)
    inverse_one = lax.rsqrt(jnp.mean(seq_in * seq_in, axis=-1, keepdims=True) + epsilon)
    unit_one = seq_in * inverse_one
    normed_one = (unit_one * norm_attn.astype(jnp.float32)).astype(jnp.bfloat16)
    query_raw = product(normed_one, w_query)
    key_raw = product(normed_one, w_key)
    value_low = product(normed_one, w_value).astype(jnp.bfloat16)
    query_rot = rotate(query_raw.reshape(local_rows, H, 2, DH), cos_table, sin_table, 1.0).astype(
        jnp.bfloat16
    )
    key_rot = rotate(key_raw.reshape(local_rows, H, 2, DH), cos_table, sin_table, 1.0).astype(
        jnp.bfloat16
    )
    keys_all, values_all = (
        lax.all_gather(key_rot.reshape(local_rows, width), "in", axis=0, tiled=True),
        lax.all_gather(value_low, "in", axis=0, tiled=True),
    )
    total_rows = keys_all.shape[0]
    key_pos = jnp.arange(total_rows, dtype=jnp.int32)
    allowed = (key_pos[None, :] <= positions[:, None]) & (key_pos[None, :] < length)
    keys_split = keys_all.reshape(total_rows, H, 2, DH)
    values_split = values_all.reshape(total_rows, H, 2 * DH)
    scores = (
        jnp.einsum("qhmd,khmd->hmqk", query_rot, keys_split, preferred_element_type=jnp.float32)
        * score_scale
    )
    masked = jnp.where(allowed, scores, -1e30)
    top_score = jnp.max(masked, axis=-1, keepdims=True)
    exp_terms = jnp.exp(masked - top_score)
    row_total = jnp.sum(exp_terms, axis=-1, keepdims=True)
    probs_all = exp_terms / row_total
    log_total = top_score + jnp.log(row_total)
    lambda_parts = lambda_params.astype(jnp.float32).reshape(4, DH)
    lam_value = (
        jnp.exp(jnp.sum(lambda_parts[0] * lambda_parts[1]))
        - jnp.exp(jnp.sum(lambda_parts[2] * lambda_parts[3]))
        + lambda_init
    )
    combined = (probs_all[:, 0] - lam_value * probs_all[:, 1]).astype(jnp.bfloat16)
    attended = jnp.einsum(
        "hqk,khe->qhe", combined, values_split, preferred_element_type=jnp.float32
    )
    inverse_head = lax.rsqrt(jnp.mean(attended * attended, axis=-1, keepdims=True) + epsilon)
    unit_head = attended * inverse_head
    head_gain = norm_head.astype(jnp.float32).reshape(H, 2 * DH) * (1.0 - lambda_init)
    headed = (unit_head * head_gain).astype(jnp.bfloat16).reshape(local_rows, width)
    residual = seq_in + product(headed, w_out)
    inverse_two = lax.rsqrt(jnp.mean(residual * residual, axis=-1, keepdims=True) + epsilon)
    unit_two = residual * inverse_two
    normed_two = (unit_two * norm_ffn.astype(jnp.float32)).astype(jnp.bfloat16)
    gate_val = product(normed_two, w_gate)
    up_val = product(normed_two, w_up)
    sigmoid_gate = jax.nn.sigmoid(gate_val)
    activation = gate_val * sigmoid_gate
    hidden = (activation * up_val).astype(jnp.bfloat16)
    valid = positions < length
    output = jnp.where(valid[:, None], residual + product(hidden, w_down), 0.0).astype(jnp.bfloat16)
    saved = (
        unit_one,
        inverse_one,
        normed_one,
        query_rot,
        keys_split,
        values_split,
        allowed,
        log_total,
        combined,
        unit_head,
        inverse_head,
        headed,
        unit_two,
        inverse_two,
        normed_two,
        gate_val,
        up_val,
        sigmoid_gate,
        activation,
        hidden,
    )
    return (output, saved)


def backward(weights, saved, seq_ct, length, positions, cos_table, sin_table, handle_ffn):
    (
        w_query,
        w_key,
        w_value,
        w_out,
        w_gate,
        w_up,
        w_down,
        norm_attn,
        norm_head,
        norm_ffn,
        lambda_params,
    ) = weights
    (
        unit_one,
        inverse_one,
        normed_one,
        query_rot,
        keys_split,
        values_split,
        allowed,
        log_total,
        combined,
        unit_head,
        inverse_head,
        headed,
        unit_two,
        inverse_two,
        normed_two,
        gate_val,
        up_val,
        sigmoid_gate,
        activation,
        hidden,
    ) = saved
    local_rows, width = unit_one.shape
    total_rows = keys_split.shape[0]
    score_scale = 1.0 / math.sqrt(DH)
    valid = positions < length
    grad_out = jnp.where(valid[:, None], seq_ct.astype(jnp.float32), 0.0)
    grad_ffn = grad_out.astype(jnp.bfloat16)
    grad_w_down = contract_rows(hidden, grad_ffn)
    grad_hidden = against(grad_ffn, w_down)
    grad_gate = (
        grad_hidden * up_val * sigmoid_gate * (1.0 + gate_val * (1.0 - sigmoid_gate))
    ).astype(jnp.bfloat16)
    grad_up = (grad_hidden * activation).astype(jnp.bfloat16)
    grad_w_gate = contract_rows(normed_two, grad_gate)
    grad_w_up = contract_rows(normed_two, grad_up)
    grad_two = against(grad_gate, w_gate) + against(grad_up, w_up)
    grad_norm_ffn = jnp.sum(grad_two * unit_two, axis=0)
    ffn_part = handle_ffn((grad_w_gate, grad_w_up, grad_w_down, grad_norm_ffn))
    grad_resid = grad_out + norm_back(
        grad_two * norm_ffn.astype(jnp.float32), unit_two, inverse_two
    )
    grad_branch = grad_resid.astype(jnp.bfloat16)
    grad_w_out = contract_rows(headed, grad_branch)
    grad_headed = against(grad_branch, w_out).reshape(local_rows, H, 2 * DH)
    head_gain = norm_head.astype(jnp.float32).reshape(H, 2 * DH) * (1.0 - lambda_init)
    grad_norm_head = (jnp.sum(grad_headed * unit_head, axis=0) * (1.0 - lambda_init)).reshape(width)
    grad_attended = norm_back(grad_headed * head_gain, unit_head, inverse_head).astype(jnp.bfloat16)
    grad_comb = jnp.einsum(
        "qhe,khe->hqk", grad_attended, values_split, preferred_element_type=jnp.float32
    )
    grad_values = jnp.einsum(
        "hqk,qhe->khe", combined, grad_attended, preferred_element_type=jnp.float32
    )
    scores = (
        jnp.einsum("qhmd,khmd->hmqk", query_rot, keys_split, preferred_element_type=jnp.float32)
        * score_scale
    )
    probs_all = jnp.exp(jnp.where(allowed, scores, -1e30) - log_total)
    lambda_parts = lambda_params.astype(jnp.float32).reshape(4, DH)
    first_exp = jnp.exp(jnp.sum(lambda_parts[0] * lambda_parts[1]))
    second_exp = jnp.exp(jnp.sum(lambda_parts[2] * lambda_parts[3]))
    lam_value = first_exp - second_exp + lambda_init
    grad_lam = -jnp.sum(grad_comb * probs_all[:, 1])
    grad_probs = jnp.stack([grad_comb, -lam_value * grad_comb], axis=1)
    grad_scores = (
        probs_all * (grad_probs - jnp.sum(grad_probs * probs_all, axis=-1, keepdims=True))
    ).astype(jnp.bfloat16)
    grad_query_rot = (
        jnp.einsum("hmqk,khmd->qhmd", grad_scores, keys_split, preferred_element_type=jnp.float32)
        * score_scale
    )
    grad_keys = (
        jnp.einsum("hmqk,qhmd->khmd", grad_scores, query_rot, preferred_element_type=jnp.float32)
        * score_scale
    )
    grad_key_mine, grad_value_mine = (
        lax.psum_scatter(
            grad_keys.reshape(total_rows, width).astype(jnp.bfloat16),
            "in",
            scatter_dimension=0,
            tiled=True,
        ).astype(jnp.float32),
        lax.psum_scatter(
            grad_values.reshape(total_rows, width).astype(jnp.bfloat16),
            "in",
            scatter_dimension=0,
            tiled=True,
        ).astype(jnp.float32),
    )
    grad_query_raw = (
        rotate(grad_query_rot, cos_table, sin_table, -1.0)
        .astype(jnp.bfloat16)
        .reshape(local_rows, width)
    )
    grad_key_raw = (
        rotate(grad_key_mine.reshape(local_rows, H, 2, DH), cos_table, sin_table, -1.0)
        .astype(jnp.bfloat16)
        .reshape(local_rows, width)
    )
    grad_value_raw = grad_value_mine.astype(jnp.bfloat16)
    grad_w_query = contract_rows(normed_one, grad_query_raw)
    grad_w_key = contract_rows(normed_one, grad_key_raw)
    grad_w_value = contract_rows(normed_one, grad_value_raw)
    grad_one = (
        against(grad_query_raw, w_query)
        + against(grad_key_raw, w_key)
        + against(grad_value_raw, w_value)
    )
    grad_norm_attn = jnp.sum(grad_one * unit_one, axis=0)
    grad_in = (
        grad_resid + norm_back(grad_one * norm_attn.astype(jnp.float32), unit_one, inverse_one)
    ).astype(jnp.bfloat16)
    grad_lambda = jnp.concatenate(
        [
            grad_lam * first_exp * lambda_parts[1],
            grad_lam * first_exp * lambda_parts[0],
            -grad_lam * second_exp * lambda_parts[3],
            -grad_lam * second_exp * lambda_parts[2],
        ]
    )
    attn_part = (
        grad_w_query,
        grad_w_key,
        grad_w_value,
        grad_w_out,
        grad_norm_attn,
        grad_norm_head,
        grad_lambda,
    )
    return (grad_in, attn_part, ffn_part)


def body(
    inputs,
    cotangent,
    lengths,
    w_query,
    w_key,
    w_value,
    w_out,
    w_gate,
    w_up,
    w_down,
    norm_attn,
    norm_head,
    norm_ffn,
    lambda_params,
):
    batches = inputs.shape[0]
    local_rows = inputs.shape[2]
    positions = lax.axis_index("in") * local_rows + jnp.arange(local_rows, dtype=jnp.int32)
    cos_table, sin_table = rope_tables(positions, DH // 2)
    kept_weights = fetch_weights(
        w_query,
        w_key,
        w_value,
        w_out,
        w_gate,
        w_up,
        w_down,
        norm_attn,
        norm_head,
        norm_ffn,
        lambda_params,
    )
    attn_sum = None
    ffn_sum = None
    output_list = []
    grad_list = []
    for batch_idx in range(batches):
        length = lengths[batch_idx, 0]
        seq_in = inputs[batch_idx, 0].astype(jnp.float32)
        output, saved = forward(kept_weights, seq_in, length, positions, cos_table, sin_table)
        grad_in, attn_part, ffn_part = backward(
            kept_weights,
            saved,
            cotangent[batch_idx, 0],
            length,
            positions,
            cos_table,
            sin_table,
            reduce_ffn,
        )
        attn_part = reduce_attn(attn_part)
        attn_sum = attn_part if attn_sum is None else jax.tree.map(jnp.add, attn_sum, attn_part)
        ffn_sum = ffn_part if ffn_sum is None else jax.tree.map(jnp.add, ffn_sum, ffn_part)
        output_list.append(output)
        grad_list.append(grad_in)
    summed = (
        attn_sum[0],
        attn_sum[1],
        attn_sum[2],
        attn_sum[3],
        ffn_sum[0],
        ffn_sum[1],
        ffn_sum[2],
        attn_sum[4],
        attn_sum[5],
        ffn_sum[3],
        attn_sum[6],
    )
    outputs = jnp.stack(output_list)[:, None]
    input_grads = jnp.stack(grad_list)[:, None]
    return (
        outputs,
        input_grads,
        summed[0],
        summed[1],
        summed[2],
        summed[3],
        summed[4],
        summed[5],
        summed[6],
        summed[7],
        summed[8],
        summed[9],
        summed[10],
    )


def solution(mesh):
    placed = (
        P(None, "grp", "in", None),
        P(None, "grp", "in", None),
        P(None, "grp"),
        P(("grp", "in"), None),
        P(("grp", "in"), None),
        P(("grp", "in"), None),
        P(("grp", "in"), None),
        P(("grp", "in"), None),
        P(("grp", "in"), None),
        P(("grp", "in"), None),
        P(("grp", "in")),
        P(("grp", "in")),
        P(("grp", "in")),
        P(("grp", "in")),
    )
    return jax.shard_map(
        body,
        mesh=mesh,
        in_specs=placed,
        out_specs=(
            P(None, "grp", "in", None),
            P(None, "grp", "in", None),
            P(("grp", "in"), None),
            P(("grp", "in"), None),
            P(("grp", "in"), None),
            P(("grp", "in"), None),
            P(("grp", "in"), None),
            P(("grp", "in"), None),
            P(("grp", "in"), None),
            P(("grp", "in")),
            P(("grp", "in")),
            P(("grp", "in")),
            P(("grp", "in")),
        ),
        check_vma=False,
    )
```

profile of v0, /device:TPU:0, one launch (start us, length us, event | category | flops | bytes accessed | tf_op | source)
XLA Modules:
  0.0 3234.6 jit_solution(14472276834531542081)
XLA Ops:
  12.9 42.6 %all-reduce.9 = (bf16[2048]{0:T(1024)(128)(2,1)S(1)}, bf16[512]{0:T(512)(128)(2,1)S(1)}, bf16[2048]{0:T(1024)(128)(2,1)S(1)}, bf16[2048]{0:T(1024)(128)(2,1)S(1)}) all-reduce(bf16[2048]{0:T(1024)(128)(2,1)S(1)} %dynamic-update-slice, bf16[512]{0:T(512)(128)(2,1)S(1)} %dynamic-update-slice.1, ...), channel_id=1, replica_groups=mesh['grp'=16,'in'=2] {'grp','in'}, use_global_device_ids=true, to_apply=%add | all-reduce | flops 6656 | bytes 26624
  58.4 32.9 %all-gather.18.cloned.1.call-done = bf16[2048,2048]{1,0:T(8,128)(2,1)} async-done(((bf16[64,2048]{1,0:T(8,128)(2,1)}), bf16[2048,2048]{1,0:T(8,128)(2,1)}) %all-gather.18.cloned.1.call-update) | async-done | bytes 8388624 | tf_op jit(solution)/shard_map/all_gather | solution.py:73
  91.3 12.3 copy.162
  103.7 66.6 %all-gather.16.cloned.1.call-done = bf16[2048,2048]{1,0:T(8,128)(2,1)} async-done(((bf16[64,2048]{1,0:T(8,128)(2,1)}), bf16[2048,2048]{1,0:T(8,128)(2,1)}) %all-gather.16.cloned.1.call-update) | async-done | bytes 8388624 | tf_op jit(solution)/shard_map/all_gather | solution.py:72
  170.3 12.4 copy.161
  214.2 35.0 %all-gather.12.cloned.1.call-done = bf16[2048,2048]{1,0:T(8,128)(2,1)} async-done(((bf16[64,2048]{1,0:T(8,128)(2,1)}), bf16[2048,2048]{1,0:T(8,128)(2,1)}) %all-gather.12.cloned.1.call-update) | async-done | bytes 8388624 | tf_op jit(solution)/shard_map/all_gather | solution.py:74
  304.7 74.4 %all-gather.22.cloned.1.call-done = bf16[2048,2048]{1,0:T(8,128)(2,1)} async-done(((bf16[64,2048]{1,0:T(8,128)(2,1)}), bf16[2048,2048]{1,0:T(8,128)(2,1)}) %all-gather.22.cloned.1.call-update) | async-done | bytes 8388624 | tf_op jit(solution)/shard_map/all_gather | solution.py:75
  388.5 136.7 %all-gather.24.cloned.1.call-done = bf16[2048,5632]{1,0:T(8,128)(2,1)} async-done(((bf16[64,5632]{1,0:T(8,128)(2,1)}), bf16[2048,5632]{1,0:T(8,128)(2,1)}) %all-gather.24.cloned.1.call-update) | async-done | bytes 23068688 | tf_op jit(solution)/shard_map/all_gather | solution.py:76
  537.1 133.5 %all-gather.26.cloned.1.call-done = bf16[2048,5632]{1,0:T(8,128)(2,1)} async-done(((bf16[64,5632]{1,0:T(8,128)(2,1)}), bf16[2048,5632]{1,0:T(8,128)(2,1)}) %all-gather.26.cloned.1.call-update) | async-done | bytes 23068688 | tf_op jit(solution)/shard_map/all_gather | solution.py:77
  670.6 12.1 fusion.153
  682.7 133.6 %all-gather.28.cloned.1.call-done = bf16[5632,2048]{1,0:T(8,128)(2,1)} async-done(((bf16[176,2048]{1,0:T(8,128)(2,1)}), bf16[5632,2048]{1,0:T(8,128)(2,1)}) %all-gather.28.cloned.1.call-update) | async-done | bytes 23068688 | tf_op jit(solution)/shard_map/all_gather | solution.py:78
  816.3 16.0 multiply_convert_fusion.4
  832.3 14.0 fusion.156
  846.3 15.3 multiply_reduce_fusion.3
  884.0 14.9 multiply_convert_fusion.2
  898.9 14.6 fusion.158
  913.4 15.2 multiply_reduce_fusion.2
  1008.2 14.3 convolution_add_fusion.4
  1092.0 20.6 fusion.161
  1112.7 29.8 convolution_add_fusion
  1142.6 20.2 fusion.160
  1162.7 29.6 convolution_add_fusion.1
  1194.0 20.4 fusion.118
  1214.4 30.0 convolution_add_fusion.2
  1251.8 13.7 fusion.17
  1297.6 41.8 %all-reduce.8 = (f32[2048]{0:T(1024)S(1)}, f32[2048]{0:T(1024)S(1)}, f32[2048]{0:T(1024)S(1)}, f32[512]{0:T(512)S(1)}) all-reduce(f32[2048]{0:T(1024)S(1)} %add.307, f32[2048]{0:T(1024)S(1)} %bitcast.374, f32[2048]{0:T(1024)S(1)} %add.309, f32[512]{0:T(512)S(1)} %maximum_add_fusion), channel_id=24, replica_groups=mesh['grp'=16,'in'=2] {'grp','in'}, use_global_device_ids=true, to_apply=%region_39.40.clone | all-reduce | flops 6656 | bytes 53248
  1346.3 25.1 reduce-scatter.24.cloned.1.call-done
  1371.4 187.4 %reduce-scatter.22.cloned.1.call-done = f32[64,2048]{1,0:T(8,128)} async-done(((f32[2048,2048]{1,0:T(8,128)}), f32[64,2048]{1,0:T(8,128)}) %reduce-scatter.22.cloned.1.call-update) | async-done | bytes 524304 | tf_op jit(solution)/shard_map/reduce_scatter | solution.py:98
  1558.7 187.2 %reduce-scatter.20.cloned.1.call-done = f32[64,2048]{1,0:T(8,128)} async-done(((f32[2048,2048]{1,0:T(8,128)}), f32[64,2048]{1,0:T(8,128)}) %reduce-scatter.20.cloned.1.call-update) | async-done | bytes 524304 | tf_op jit(solution)/shard_map/reduce_scatter | solution.py:97
  1746.0 489.4 %reduce-scatter.30.cloned.1.call-done = f32[64,5632]{1,0:T(8,128)} async-done(((f32[2048,5632]{1,0:T(8,128)}), f32[64,5632]{1,0:T(8,128)}) %reduce-scatter.30.cloned.1.call-update) | async-done | bytes 1441808 | tf_op jit(solution)/shard_map/reduce_scatter | solution.py:89
  2235.4 496.0 %reduce-scatter.28.cloned.1.call-done = f32[64,5632]{1,0:T(8,128)} async-done(((f32[2048,5632]{1,0:T(8,128)}), f32[64,5632]{1,0:T(8,128)}) %reduce-scatter.28.cloned.1.call-update) | async-done | bytes 1441808 | tf_op jit(solution)/shard_map/reduce_scatter | solution.py:88
  2731.4 496.0 %reduce-scatter.32.cloned.1.call-done = f32[176,2048]{1,0:T(8,128)} async-done(((f32[5632,2048]{1,0:T(8,128)}), f32[176,2048]{1,0:T(8,128)}) %reduce-scatter.32.cloned.1.call-update) | async-done | bytes 1441808 | tf_op jit(solution)/shard_map/reduce_scatter | solution.py:90
  (414 shorter events, 330.7 us)
Async XLA Ops:
  7.2 84.1 %all-gather.18.cloned.1.call-start = ((), (), s32[]{:S(2)}) async-start(), calls=%async_computation.14 | async-start | bytes 8650752 | tf_op jit(solution)/shard_map/all_gather | solution.py:73
  7.9 162.3 %all-gather.16.cloned.1.call-start = ((), (), s32[]{:S(2)}) async-start(), calls=%async_computation.13 | async-start | bytes 8650752 | tf_op jit(solution)/shard_map/all_gather | solution.py:72
  8.7 240.6 %all-gather.12.cloned.1.call-start = ((), (), s32[]{:S(2)}) async-start(), calls=%async_computation.11 | async-start | bytes 8650752 | tf_op jit(solution)/shard_map/all_gather | solution.py:74
  9.4 261.7 %all-gather.20.cloned.1.call-start = ((), (), s32[]{:S(2)}) async-start(), calls=%async_computation.15 | async-start | bytes 2359296 | tf_op jit(solution)/shard_map/all_gather | solution.py:136
  55.5 199.9 %copy-start.61 = (f32[2048]{0:T(1024)}, f32[2048]{0:T(1024)S(1)}, u32[]{:S(2)}) copy-start(f32[2048]{0:T(1024)S(1)} %convert_element_type.285) | copy-start | bytes 24580
  57.3 198.1 %copy-start.79 = (f32[192]{0:T(256)}, f32[192]{0:T(256)S(1)}, u32[]{:S(2)}) copy-start(f32[192]{0:T(256)S(1)} %add_rsqrt_fusion.5) | copy-start | bytes 2308
  57.3 191.9 %copy-start.76 = (f32[192]{0:T(256)}, f32[192]{0:T(256)S(1)}, u32[]{:S(2)}) copy-start(f32[192]{0:T(256)S(1)} %add_rsqrt_fusion.3) | copy-start | bytes 2308
  58.4 139.9 %copy-start.65 = (f32[192,64]{1,0:T(8,128)}, f32[192,64]{1,0:T(8,128)S(1)}, u32[]{:S(2)}) copy-start(f32[192,64]{1,0:T(8,128)S(1)} %get-tuple-element.166) | copy-start | bytes 147460
  202.1 71.6 %copy-start.32 = (bf16[192,8,2,64]{3,0,2,1:T(8,128)(2,1)}, bf16[192,8,2,64]{3,0,2,1:T(8,128)(2,1)S(1)}, u32[]{:S(2)}) copy-start(bf16[192,8,2,64]{3,0,2,1:T(8,128)(2,1)S(1)} %get-tuple-element.124) | copy-start | bytes 1179652
  207.4 71.3 %all-gather.32.cloned.1.call-start = ((), (), s32[]{:S(2)}) async-start(), calls=%async_computation.21 | async-start | bytes 2359296 | tf_op jit(solution)/shard_map/all_gather | solution.py:136
  214.1 76.4 %all-gather.30.cloned.1.call-start = ((), (), s32[]{:S(2)}) async-start(), calls=%async_computation.20 | async-start | bytes 2359296 | tf_op jit(solution)/shard_map/all_gather | solution.py:137
  255.4 44.5 %all-gather.14.cloned.1.call-start = ((), (), s32[]{:S(2)}) async-start(), calls=%async_computation.12 | async-start | bytes 2359296 | tf_op jit(solution)/shard_map/all_gather | solution.py:137
  262.2 116.9 %all-gather.22.cloned.1.call-start = ((), (), s32[]{:S(2)}) async-start(), calls=%async_computation.16 | async-start | bytes 8650752 | tf_op jit(solution)/shard_map/all_gather | solution.py:75
  263.0 262.2 %all-gather.24.cloned.1.call-start = ((), (), s32[]{:S(2)}) async-start(), calls=%async_computation.17 | async-start | bytes 23789568 | tf_op jit(solution)/shard_map/all_gather | solution.py:76
  263.7 406.9 %all-gather.26.cloned.1.call-start = ((), (), s32[]{:S(2)}) async-start(), calls=%async_computation.18 | async-start | bytes 23789568 | tf_op jit(solution)/shard_map/all_gather | solution.py:77
  264.3 552.0 %all-gather.28.cloned.1.call-start = ((), (), s32[]{:S(2)}) async-start(), calls=%async_computation.19 | async-start | bytes 23789568 | tf_op jit(solution)/shard_map/all_gather | solution.py:78
  265.0 732.3 %reduce-scatter.34.cloned.1.call-start = ((), (), s32[]{:S(2)}) async-start(), calls=%async_computation.31 | async-start | bytes 2359296
  270.9 657.8 %copy-start.88 = (pred[192]{0:T(512)(128)(4,1)}, pred[192]{0:T(512)(128)(4,1)S(1)}, u32[]{:S(2)}) copy-start(pred[192]{0:T(512)(128)(4,1)S(1)} %get-tuple-element.189) | copy-start | bytes 580
  270.9 657.8 %copy-start.90 = (pred[192]{0:T(512)(128)(4,1)}, pred[192]{0:T(512)(128)(4,1)S(1)}, u32[]{:S(2)}) copy-start(pred[192]{0:T(512)(128)(4,1)S(1)} %get-tuple-element.188) | copy-start | bytes 580
  304.7 80.1 %copy-start.41 = (bf16[8,24,8,256]{3,2,0,1:T(8,128)(2,1)}, bf16[8,24,8,256]{3,2,0,1:T(8,128)(2,1)S(1)}, u32[]{:S(2)}) copy-start(bf16[8,24,8,256]{3,2,0,1:T(8,128)(2,1)S(1)} %copy.224) | copy-start | bytes 2359300
  388.5 282.2 %copy-start.26 = (bf16[192,2048]{1,0:T(8,128)(2,1)}, bf16[192,2048]{1,0:T(8,128)(2,1)S(1)}, u32[]{:S(2)}) copy-start(bf16[192,2048]{1,0:T(8,128)(2,1)S(1)} %multiply_convert_fusion.14) | copy-start | bytes 2359300
  537.1 279.2 %copy-start.36 = (bf16[2,1,192,2048]{3,2,1,0:T(8,128)(2,1)S(1)}, bf16[2,1,192,2048]{3,2,1,0:T(8,128)(2,1)}, u32[]{:S(2)}) copy-start(bf16[2,1,192,2048]{3,2,1,0:T(8,128)(2,1)} %param.15) | copy-start | bytes 4718596
  951.1 57.1 %reduce-scatter.36.cloned.1.call-start = ((), (), s32[]{:S(2)}) async-start(), calls=%async_computation.32 | async-start | bytes 2359296
  958.5 69.6 %reduce-scatter.18.cloned.1.call-start = ((), (), s32[]{:S(2)}) async-start(), calls=%async_computation.23 | async-start | bytes 2359296 | tf_op jit(solution)/shard_map/reduce_scatter | solution.py:295
  970.4 61.4 %reduce-scatter.16.cloned.1.call-start = ((), (), s32[]{:S(2)}) async-start(), calls=%async_computation.22 | async-start | bytes 2359296 | tf_op jit(solution)/shard_map/reduce_scatter | solution.py:295
  983.2 363.1 %reduce-scatter.26.cloned.1.call-start = ((), (), s32[]{:S(2)}) async-start(), calls=%async_computation.27 | async-start | bytes 17301504 | tf_op jit(solution)/shard_map/reduce_scatter | solution.py:100
  997.2 374.1 %reduce-scatter.24.cloned.1.call-start = ((), (), s32[]{:S(2)}) async-start(), calls=%async_computation.26 | async-start | bytes 17301504 | tf_op jit(solution)/shard_map/reduce_scatter | solution.py:99
  1022.5 536.2 %reduce-scatter.22.cloned.1.call-start = ((), (), s32[]{:S(2)}) async-start(), calls=%async_computation.25 | async-start | bytes 17301504 | tf_op jit(solution)/shard_map/reduce_scatter | solution.py:98
  1067.8 678.1 %reduce-scatter.20.cloned.1.call-start = ((), (), s32[]{:S(2)}) async-start(), calls=%async_computation.24 | async-start | bytes 17301504 | tf_op jit(solution)/shard_map/reduce_scatter | solution.py:97
  1090.9 1144.5 %reduce-scatter.30.cloned.1.call-start = ((), (), s32[]{:S(2)}) async-start(), calls=%async_computation.29 | async-start | bytes 47579136 | tf_op jit(solution)/shard_map/reduce_scatter | solution.py:89
  1142.5 1588.9 %reduce-scatter.28.cloned.1.call-start = ((), (), s32[]{:S(2)}) async-start(), calls=%async_computation.28 | async-start | bytes 47579136 | tf_op jit(solution)/shard_map/reduce_scatter | solution.py:88
  1192.4 2034.9 %reduce-scatter.32.cloned.1.call-start = ((), (), s32[]{:S(2)}) async-start(), calls=%async_computation.30 | async-start | bytes 47579136 | tf_op jit(solution)/shard_map/reduce_scatter | solution.py:90
  (97 other events, 628.4 us)
Sparse Core Ops, SparseCore 0:
  10.9 80.4 all-gather.17
  94.2 76.0 all-gather.15
  173.1 76.0 all-gather.11
  251.2 8.3 all-gather.19
  261.6 10.9 all-gather.31
  274.0 10.9 all-gather.29
  286.5 10.9 all-gather.13
  300.4 78.6 all-gather.21
  381.9 143.1 all-gather.23
  527.8 142.7 all-gather.25
  673.5 142.7 all-gather.27
  951.2 7.2 reduce-scatter.33
  960.8 10.2 reduce-scatter.35
  973.2 10.2 reduce-scatter.17
  985.7 10.2 reduce-scatter.15
  998.7 183.8 reduce-scatter.25
  1185.4 185.9 reduce-scatter.23
  1374.1 184.5 reduce-scatter.21
  1561.6 184.3 reduce-scatter.19
  1748.7 486.6 reduce-scatter.29
  2238.3 493.0 reduce-scatter.27
  2734.2 493.0 reduce-scatter.31
where the time goes:
time: 3250 us; the launch traced here: 3230 us
  waiting for transfers between devices  2500 us (77%)
  matrix products  471 us (14%)
  local copies, waits for them, and re-layouts  101 us (3%)
  blocking collectives  84.4 us (3%)
  other arithmetic  57.7 us (2%)
    reduce_scatter x1, waiting for transfers between devices, reduce_ffn(): lax.psum_scatter(group[2], ('grp', 'in'), scatter_dimension=0, tiled=True)  496 us
    reduce_scatter x1, waiting for transfers between devices, reduce_ffn(): lax.psum_scatter(group[0], ('grp', 'in'), scatter_dimension=0, tiled=True)  496 us
    reduce_scatter x1, waiting for transfers between devices, reduce_ffn(): lax.psum_scatter(group[1], ('grp', 'in'), scatter_dimension=0, tiled=True)  489 us
    dot_general x14, matrix products, contract_rows(): lax.dot_general(left, right, (((0,), (0,)), ((), ())), preferred_element_...  210 us
    reduce_scatter x1, waiting for transfers between devices, reduce_attn(): lax.psum_scatter(group[1], ('grp', 'in'), scatter_dimension=0, tiled=True)  187 us
    reduce_scatter x1, waiting for transfers between devices, reduce_attn(): lax.psum_scatter(group[0], ('grp', 'in'), scatter_dimension=0, tiled=True)  187 us
    all_gather x1, waiting for transfers between devices, fetch_weights(): lax.all_gather(w_gate, ('grp', 'in'), axis=0, tiled=True)  137 us
    all_gather x1, waiting for transfers between devices, fetch_weights(): lax.all_gather(w_down, ('grp', 'in'), axis=0, tiled=True)  134 us
  transfers between devices with their start and end apart: 22, of which 13 were waited for; matrix products, arithmetic and copies ran while one was open for 15% of the time, Pallas kernels for 0%

commit v1 on v0

v1 whole, which is shorter than its diff:
```python
import functools
import math

import jax
import jax.numpy as jnp
from jax import lax
from jax.experimental import pallas as pl
from jax.experimental.pallas import tpu as pltpu
from jax.sharding import Mesh
from jax.sharding import PartitionSpec as P

H = 8
DH = 128
TEAM = ("y", "x", "c")
ROWS = ("c", "y", "x")
EVERY = ("z", "y", "x", "c")

epsilon = 1e-05
lambda_init = 0.8 - 0.6 * math.exp(-3.3)
rope_base = 10000.0
score_scale = 1.0 / math.sqrt(DH)
bf16 = jnp.bfloat16
f32 = jnp.float32


def product(left, right):
    return jnp.dot(left, right, preferred_element_type=f32)


def contract_rows(left, right):
    return lax.dot_general(left, right, (((0,), (0,)), ((), ())), preferred_element_type=f32)


def against(left, right):
    return lax.dot_general(left, right, (((1,), (1,)), ((), ())), preferred_element_type=f32)


def inverse_rms(values):
    return lax.rsqrt(jnp.mean(values * values, axis=-1, keepdims=True) + epsilon)


def norm_back(grad_unit, unit_vals, inverse):
    return inverse * (
        grad_unit - unit_vals * jnp.mean(grad_unit * unit_vals, axis=-1, keepdims=True)
    )


def turn(values, cos_table, sin_table):
    return values * cos_table + pltpu.roll(values, DH // 2, 1) * sin_table


def softmax_block(query, key, allowed):
    scores = jnp.where(allowed, against(query, key) * score_scale, -1e30)
    terms = jnp.exp(scores - jnp.max(scores, axis=-1, keepdims=True))
    return terms / jnp.sum(terms, axis=-1, keepdims=True)


def allowed_block(start, rows, keys, length):
    row = start + lax.broadcasted_iota(jnp.int32, (rows, keys), 0)
    col = lax.broadcasted_iota(jnp.int32, (rows, keys), 1)
    return (col <= row) & (col < length)


def attend_kernel(len_ref, lam_ref, raw_ref, cos_ref, sin_ref, gain_ref, rot_ref, headed_ref):
    length = len_ref[pl.program_id(0), pl.program_id(1)]
    lam = lam_ref[0]
    halves, rows = raw_ref.shape[0], raw_ref.shape[3]
    total = halves * rows
    raw = raw_ref[:, 0, 0].reshape(total, 6 * DH)
    cos_table, sin_table = cos_ref[...], sin_ref[...]
    turned = [
        turn(raw[:, part * DH : (part + 1) * DH], cos_table, sin_table).astype(bf16)
        for part in range(4)
    ]
    value = raw[:, 4 * DH :].astype(bf16)
    rot_ref[:, 0, 0] = jnp.concatenate(turned + [value], axis=1).reshape(halves, rows, 6 * DH)
    gain = gain_ref[...]
    step = 128
    parts = []
    for start in range(0, total, step):
        keys = start + step
        mask = allowed_block(start, step, keys, length)
        first = softmax_block(turned[0][start:keys], turned[2][:keys], mask)
        second = softmax_block(turned[1][start:keys], turned[3][:keys], mask)
        combined = (first - lam * second).astype(bf16)
        attended = product(combined, value[:keys])
        parts.append((attended * inverse_rms(attended) * gain).astype(bf16))
    headed_ref[:, 0, 0] = jnp.concatenate(parts, axis=0).reshape(halves, rows, 2 * DH)


def attend_back_kernel(
    len_ref, lam_ref, rot_ref, grad_ref, cos_ref, sin_ref, gain_ref,
    out_ref, head_ref, lam_out_ref, grad_key, grad_value,
):
    first_step = (pl.program_id(0) == 0) & (pl.program_id(1) == 0)

    @pl.when(first_step)
    def _():
        head_ref[...] = jnp.zeros_like(head_ref)
        lam_out_ref[...] = jnp.zeros_like(lam_out_ref)

    length = len_ref[pl.program_id(0), pl.program_id(1)]
    lam = lam_ref[0]
    halves, rows = rot_ref.shape[0], rot_ref.shape[3]
    total = halves * rows
    rot = rot_ref[:, 0, 0].reshape(total, 6 * DH)
    grad_headed = grad_ref[:, 0, 0].reshape(total, 2 * DH).astype(f32)
    cos_table, sin_table = cos_ref[...], sin_ref[...]
    query = [rot[:, :DH], rot[:, DH : 2 * DH]]
    key = [rot[:, 2 * DH : 3 * DH], rot[:, 3 * DH : 4 * DH]]
    value = rot[:, 4 * DH :]
    gain = gain_ref[...]
    step = 128
    grad_query = [[], []]
    for start in reversed(range(0, total, step)):
        keys = start + step
        mask = allowed_block(start, step, keys, length)
        first = softmax_block(query[0][start:keys], key[0][:keys], mask)
        second = softmax_block(query[1][start:keys], key[1][:keys], mask)
        combined = (first - lam * second).astype(bf16)
        attended = product(combined, value[:keys])
        inverse = inverse_rms(attended)
        unit = attended * inverse
        grad_head = grad_headed[start:keys]
        head_ref[...] += jnp.sum(grad_head * unit, axis=0, keepdims=True)
        grad_attended = norm_back(grad_head * gain, unit, inverse).astype(bf16)
        grad_comb = against(grad_attended, value[:keys])
        value_part = contract_rows(combined, grad_attended)
        inner = [
            jnp.sum(grad_comb * first, axis=-1, keepdims=True),
            jnp.sum(grad_comb * second, axis=-1, keepdims=True),
        ]
        lam_out_ref[...] -= jnp.sum(inner[1], axis=0, keepdims=True)
        grad_scores = [
            (first * (grad_comb - inner[0])).astype(bf16),
            (-lam * second * (grad_comb - inner[1])).astype(bf16),
        ]
        if keys == total:
            grad_value[...] = value_part
        else:
            grad_value[:keys] += value_part
        for k in range(2):
            key_part = contract_rows(grad_scores[k], query[k][start:keys])
            cols = slice(k * DH, (k + 1) * DH)
            if keys == total:
                grad_key[:, cols] = key_part
            else:
                grad_key[:keys, cols] += key_part
            grad_query[k].append(product(grad_scores[k], key[k][:keys]) * score_scale)
    turned = [
        turn(jnp.concatenate(grad_query[k][::-1], axis=0), cos_table, sin_table).astype(bf16)
        for k in range(2)
    ] + [
        turn(grad_key[:, k * DH : (k + 1) * DH] * score_scale, cos_table, sin_table).astype(bf16)
        for k in range(2)
    ]
    out_ref[:, 0, 0] = jnp.concatenate(
        turned + [grad_value[...].astype(bf16)], axis=1
    ).reshape(halves, rows, 6 * DH)


def row_spec(halves, rows, cols):
    return pl.BlockSpec((halves, 1, 1, rows, cols), lambda j, m: (0, j, m, 0, 0))


def whole_spec(shape):
    return pl.BlockSpec(shape, lambda j, m: (0,) * len(shape))


def attend(lengths, lam, raw, cos_table, sin_table, gain, dims):
    halves, slots, batches, rows = dims
    smem = pl.BlockSpec(memory_space=pltpu.SMEM)
    rot, headed = pl.pallas_call(
        attend_kernel,
        grid=(slots, batches),
        in_specs=[
            smem, smem, row_spec(halves, rows, 6 * DH),
            whole_spec(cos_table.shape), whole_spec(sin_table.shape), whole_spec(gain.shape),
        ],
        out_specs=[row_spec(halves, rows, 6 * DH), row_spec(halves, rows, 2 * DH)],
        out_shape=[
            jax.ShapeDtypeStruct(dims + (6 * DH,), bf16),
            jax.ShapeDtypeStruct(dims + (2 * DH,), bf16),
        ],
        compiler_params=pltpu.CompilerParams(vmem_limit_bytes=48 * 1024 * 1024),
    )(lengths, lam, raw.reshape(dims + (6 * DH,)), cos_table, sin_table, gain)
    return rot, headed


def attend_back(lengths, lam, rot, grad_headed, cos_table, sin_table, gain, dims):
    halves, slots, batches, rows = dims
    smem = pl.BlockSpec(memory_space=pltpu.SMEM)
    return pl.pallas_call(
        attend_back_kernel,
        grid=(slots, batches),
        in_specs=[
            smem, smem, row_spec(halves, rows, 6 * DH), row_spec(halves, rows, 2 * DH),
            whole_spec(cos_table.shape), whole_spec(sin_table.shape), whole_spec(gain.shape),
        ],
        out_specs=[
            row_spec(halves, rows, 6 * DH), whole_spec((1, 2 * DH)), whole_spec((1, 128)),
        ],
        out_shape=[
            jax.ShapeDtypeStruct(dims + (6 * DH,), bf16),
            jax.ShapeDtypeStruct((1, 2 * DH), f32),
            jax.ShapeDtypeStruct((1, 128), f32),
        ],
        scratch_shapes=[
            pltpu.VMEM((halves * rows, 2 * DH), f32),
            pltpu.VMEM((halves * rows, 2 * DH), f32),
        ],
        compiler_params=pltpu.CompilerParams(vmem_limit_bytes=48 * 1024 * 1024),
    )(lengths, lam, rot, grad_headed.reshape(dims + (2 * DH,)), cos_table, sin_table, gain)


def shift(depth, step):
    return [(i, (i + step) % depth) for i in range(depth)]


def after(value, *others):
    return lax.optimization_barrier((value, *others))[0]


def permute(value, depth, step):
    return lax.ppermute(value, "z", shift(depth, step))


class Gather:
    def __init__(self, block, depth, hold=None):
        self.block, self.depth = block, depth
        self.near = [(block, block)]
        for _ in range((depth - 1) // 2):
            above, below = self.near[-1]
            pair = (permute(above, depth, -1), permute(below, depth, 1))
            self.near.append(pair if hold is None else hold(pair))
        self.far = None
        if depth % 2 == 0:
            above, below = self.near[-1]
            half = block.shape[0] // 2
            self.far = (permute(above[:half], depth, -1), permute(below[half:], depth, 1))

    def joined(self, axis, *others):
        near, far = self.near[1:], self.far
        if others:
            near, far, _ = lax.optimization_barrier((near, far, others))
        middle = [] if far is None else [jnp.concatenate(far, axis=0)]
        above = [pair[0] for pair in near]
        below = [pair[1] for pair in near[::-1]]
        return jnp.concatenate([self.block] + above + middle + below, axis=axis)

    def first(self):
        return self.near[-1]

    def last(self):
        return self.near[-1] if self.far is None else self.far


class Scatter:
    def __init__(self, blocks):
        depth = len(blocks)
        half = blocks[0].shape[0] // 2
        self.pairs = [
            [(blocks[k][:half], blocks[-k % depth][half:]) for k in range(depth // 2 + 1)],
            [(blocks[k][half:], blocks[-k % depth][:half]) for k in range((depth - 1) // 2 + 1)],
        ]
        self.depth = depth
        self.first = self.move(self.pairs[0][-1]) if depth > 1 else None

    def move(self, pair):
        return (permute(pair[0], self.depth, 1), permute(pair[1], self.depth, -1))

    def chain(self, pairs, moved):
        for pair in pairs[-2:0:-1]:
            moved = self.move(
                tuple((a.astype(f32) + b.astype(f32)).astype(bf16) for a, b in zip(pair, moved))
            )
        return moved

    def plain(self):
        pairs = self.pairs[1]
        self.second = self.chain(pairs, self.move(pairs[-1])) if len(pairs) > 1 else None
        return self.second

    def added(self, *others):
        pairs = self.pairs[0]
        self.third = self.chain(pairs, after(self.first, *others)) if self.depth > 1 else None
        return self.third

    def total(self, *others):
        (top, _), (bottom, _) = self.pairs[0][0], self.pairs[1][0]
        bottom = self.pairs[0][0][1]
        top, bottom = top.astype(f32), bottom.astype(f32)
        third, second, _ = lax.optimization_barrier((self.third, self.second, others))
        for pair, swap in ((third, False), (second, True)):
            if pair is not None:
                up, down = pair[::-1] if swap else pair
                top, bottom = top + up.astype(f32), bottom + down.astype(f32)
        return jnp.concatenate([top, bottom], axis=0)


def turn_blocks(values, depth, axis, forth=True):
    size = values.shape[axis]
    here = lax.axis_index("z")
    start = (here if forth else (depth - here) % depth) * (size // depth)
    return lax.dynamic_slice_in_dim(
        jnp.concatenate([values, values], axis=axis), start, size, axis
    )


def gather_rows(block):
    return lax.all_gather(block, ROWS, axis=0, tiled=True)


def exchange(values, split, joined, order=ROWS):
    return lax.all_to_all(values, order, split_axis=split, concat_axis=joined, tiled=True)


def split_cores(values, axis=0):
    count = values.shape[axis] // 2
    mine = lax.axis_index("c")
    return [
        lax.dynamic_slice_in_dim(values, core * count, count, axis) for core in (1 - mine, mine)
    ]


def across(values):
    values = values.astype(bf16)
    return values, lax.ppermute(values, "c", [(0, 1), (1, 0)])


def over_cores(compute, theirs, mine):
    return compute(mine) + across(compute(theirs))[1].astype(f32)


def over_chips(total):
    return lax.psum_scatter(total.astype(bf16), ("y", "x"), scatter_dimension=0, tiled=True)


def body(
    inputs, cotangent, lengths, w_query, w_key, w_value, w_out, w_gate, w_up, w_down,
    norm_attn, norm_head, norm_ffn, lambda_params, *, depth,
):
    batches, _, rows, width = inputs.shape
    team = H
    chips = team // 2
    shard = w_query.shape[0]
    hidden_shard = w_down.shape[0]
    own_rows = batches * rows
    dims = (2, chips, batches, rows)
    total_rows = 2 * rows
    places = depth * team
    units = depth * hidden_shard
    turned = functools.partial(turn_blocks, depth=depth)

    def natural(blocks):
        shape = blocks.shape
        blocks = blocks.reshape((2, chips, shape[0] // team) + shape[1:])
        return jnp.swapaxes(blocks, 0, 1).reshape(shape)

    def by_core(blocks):
        shape = blocks.shape
        blocks = blocks.reshape((chips, 2, shape[0] // team) + shape[1:])
        return jnp.swapaxes(blocks, 0, 1).reshape(shape)

    x_own = inputs.reshape(own_rows, width)
    x_all = gather_rows(turned(x_own, axis=1))

    qkv = jnp.concatenate(
        [w.reshape(shard, H, 2 * DH) for w in (w_query, w_key, w_value)], axis=2
    )
    qkv = exchange(qkv.transpose(1, 0, 2).reshape(H * shard, 6 * DH), 0, 0)

    small = jnp.concatenate(
        [
            norm_attn.astype(f32), norm_head.astype(f32), norm_ffn.astype(f32),
            lambda_params.astype(f32), lengths[:, 0].astype(f32),
        ]
    )[None]
    small = lax.all_gather(after(small, qkv), TEAM, axis=0, tiled=True)
    length_all = small[:, -batches:].reshape(chips, 2, batches)[:, 0].astype(jnp.int32)
    far_small = [permute(small, depth, -k) for k in range(1, depth)]
    qkv_ring = Gather(natural(qkv), depth, lambda near: after(near, far_small))
    small = jnp.concatenate([small] + far_small, axis=0).reshape(depth, team, -1)
    small = turned(small, axis=0, forth=False)
    qkv_near = qkv_ring.first()
    out_w = lax.all_gather(w_out, EVERY, axis=0, tiled=True)

    def by_units(w):
        w = w.reshape(shard, depth, team, hidden_shard).transpose(2, 0, 1, 3)
        return w.reshape(team * shard, units)

    gate_up = jnp.concatenate([by_units(w_gate), by_units(w_up)], axis=1)
    def to_units(grad):
        grad = grad.reshape(team, shard, depth, hidden_shard).transpose(1, 2, 0, 3)
        return grad.reshape(shard, places * hidden_shard)

    n_lam = lambda_params.shape[0]
    gain_attn = small[:, :, :shard].reshape(1, width)
    gain_head = small[:, :, shard : 2 * shard].reshape(H, 2 * DH)
    gain_ffn = small[:, :, 2 * shard : 3 * shard].reshape(1, width)
    lam_parts = small[:, :, 3 * shard : 3 * shard + n_lam].reshape(4, DH)
    first_exp = jnp.exp(jnp.sum(lam_parts[0] * lam_parts[1]))
    second_exp = jnp.exp(jnp.sum(lam_parts[2] * lam_parts[3]))
    lam = (first_exp - second_exp + lambda_init)[None]
    head = lax.axis_index(ROWS)
    gain_mine = lax.dynamic_index_in_dim(gain_head, head, 0) * (1.0 - lambda_init)

    frequency = rope_base ** (-jnp.arange(DH // 2, dtype=f32) / (DH // 2))
    angles = jnp.arange(total_rows, dtype=f32)[:, None] * frequency[None, :]
    cos_table = jnp.concatenate([jnp.cos(angles)] * 2, axis=1)
    sine = jnp.sin(angles)
    sin_table = jnp.concatenate([-sine, sine], axis=1)

    x_float = after(x_all, *qkv_near).astype(f32)
    inverse_all = inverse_rms(x_float)
    normed_one = (x_float * inverse_all * turned(gain_attn, axis=1)).astype(bf16)
    qkv_w = qkv_ring.joined(0, normed_one)
    gate_up = exchange(after(gate_up, normed_one), 0, 0, TEAM).T
    gate_up_ring = Gather(gate_up, depth)
    gate_up_w = gate_up_ring.joined(1)
    down_ring = Gather(after(w_down, *gate_up_ring.first()), depth)
    raw = product(normed_one, qkv_w)
    rot, headed = attend(length_all, lam, after(raw, gate_up), cos_table, sin_table, gain_mine, dims)
    headed_own = exchange(headed.reshape(team * own_rows, 2 * DH), 0, 1)
    headed_own = after(headed_own, *gate_up_ring.first())

    x_own = x_own.astype(f32)
    residual = x_own + product(headed_own, out_w)
    inverse_two = inverse_rms(residual)
    unit_two = residual * inverse_two
    normed_two = gather_rows(turned((unit_two * gain_ffn).astype(bf16), axis=1))

    positions = lax.axis_index("c") * rows + jnp.arange(rows, dtype=jnp.int32)
    valid = (positions[None, :] < lengths).reshape(own_rows, 1)
    grad_own = jnp.where(valid, cotangent.reshape(own_rows, width), 0)
    grad_all = gather_rows(grad_own)

    gate_up_val = against(gate_up_w, normed_two)
    gate_val, up_val = gate_up_val[:units], gate_up_val[units:]
    down_w = turned(down_ring.joined(0, gate_up_val), axis=0, forth=False)
    sigmoid_gate = jax.nn.sigmoid(gate_val)
    activation = gate_val * sigmoid_gate
    hidden = (activation * up_val).astype(bf16)

    def over_units(weight):
        return lambda values: contract_rows(values, weight)

    out_rows = over_cores(over_units(down_w), *split_cores(hidden, 1)).astype(bf16)
    grad_hidden = against(down_w, after(grad_all, out_rows))
    grad_gate = grad_hidden * up_val * sigmoid_gate * (1.0 + gate_val * (1.0 - sigmoid_gate))
    grad_up = grad_hidden * activation
    grad_gate_up = jnp.concatenate([grad_gate.astype(bf16), grad_up.astype(bf16)], axis=0)

    out_rows = over_chips(out_rows)
    theirs, mine = split_cores(grad_gate_up, 1)
    sent = across(over_units(gate_up_w)(theirs))
    grad_w_down = product(hidden, after(grad_all, sent[0])).astype(bf16)
    down_blocks = grad_w_down.reshape(depth, hidden_shard, width)
    down_back = Scatter(
        [
            lax.dynamic_index_in_dim(down_blocks, (lax.axis_index("z") + k) % depth, 0, False)
            for k in range(depth)
        ]
    )
    grad_two = over_units(gate_up_w)(after(mine, grad_w_down))
    grad_two = (grad_two + sent[1].astype(f32)).astype(bf16)
    down_back.plain()
    grad_w_gate_up = product(after(grad_gate_up, grad_two), normed_two).astype(bf16)
    down_back.added(*down_back.second, grad_w_gate_up)
    gate_up_back = Scatter(jnp.split(grad_w_gate_up, depth, axis=1))
    gate_up_back.plain()
    gate_up_back.added()
    grad_w_down = down_back.total()
    grad_two = after(over_chips(after(grad_two, out_rows)), grad_w_down, *gate_up_back.first)
    grad_two = turned(grad_two, axis=1, forth=False).astype(f32)

    grad_norm_ffn = jnp.sum(grad_two * unit_two, axis=0)
    grad_resid = grad_own.astype(f32) + norm_back(grad_two * gain_ffn, unit_two, inverse_two)
    grad_branch = grad_resid.astype(bf16)
    grad_headed = exchange(against(grad_branch, out_w).astype(bf16), 1, 0)
    headed_cores = headed_own.reshape(own_rows, depth, chips, 2, shard).transpose(0, 3, 2, 1, 4)
    headed_cores = turned(headed_cores, axis=3).reshape(own_rows, width)
    grad_w_out = over_cores(lambda v: contract_rows(v, grad_branch), *split_cores(headed_cores, 1))
    grad_w_out = grad_w_out.astype(bf16)
    grad_headed = after(grad_headed, grad_w_out, *gate_up_back.second)
    grad_w_out = over_chips(grad_w_out)
    grad_raw, grad_head, grad_lam = attend_back(
        length_all, lam, rot, grad_headed, cos_table, -sin_table, gain_mine, dims
    )
    grad_raw = grad_raw.reshape(team * own_rows, 6 * DH)
    out_rows = after(out_rows, grad_raw)
    output = jnp.where(valid, residual + out_rows.astype(f32), 0.0).astype(bf16)
    theirs, mine = split_cores(grad_raw)
    sent = across(against(theirs, qkv_w))
    grad_qkv = contract_rows(normed_one, after(grad_raw, sent[0], *gate_up_back.third)).astype(bf16)
    qkv_back = Scatter(jnp.split(grad_qkv, depth, axis=0))
    grad_w_gate_up = gate_up_back.total(grad_qkv)
    grad_w_gate_up = exchange(grad_w_gate_up.astype(bf16).T, 0, 0, TEAM).astype(f32)
    grad_one = against(after(mine, grad_qkv), qkv_w) + sent[1].astype(f32)
    unit_mine = split_cores(x_all)[1].astype(f32) * split_cores(inverse_all)[1]
    grad_norm_attn = turned(jnp.sum(grad_one * unit_mine, axis=0), axis=0, forth=False)
    grad_one = over_chips(grad_one)
    grad_w_gate = to_units(grad_w_gate_up[:, :units])
    grad_w_up = to_units(grad_w_gate_up[:, units:])
    qkv_back.plain()
    qkv_back.added(grad_w_gate_up)
    out_back = Scatter(jnp.split(after(grad_w_out, *qkv_back.first), depth, axis=0))
    out_back.plain()
    out_back.added()
    grad_w_out = out_back.total()
    grad_lam = grad_lam[0, 0]
    grad_lambda = jnp.concatenate(
        [
            grad_lam * first_exp * lam_parts[1],
            grad_lam * first_exp * lam_parts[0],
            -grad_lam * second_exp * lam_parts[3],
            -grad_lam * second_exp * lam_parts[2],
        ]
    )
    grad_head = grad_head * (1.0 - lambda_init)
    head_full = lax.dynamic_update_slice(jnp.zeros((H, 2 * DH), f32), grad_head, (head, 0))
    small_grads = jnp.concatenate(
        [
            grad_norm_attn.reshape(places, shard),
            head_full.reshape(places, shard),
            grad_norm_ffn.reshape(places, shard),
            grad_lambda.reshape(places, n_lam),
        ],
        axis=1,
    )
    small_grads = small_grads.reshape(depth, team, -1).swapaxes(0, 1).reshape(places, -1)
    small_grads = exchange(small_grads, 0, 0, TEAM).reshape(team, depth, -1).sum(axis=0)
    small_grads = lax.all_to_all(small_grads, "z", 0, 0, tiled=True).sum(axis=0)

    grad_qkv = exchange(by_core(qkv_back.total(small_grads, grad_w_gate, grad_w_up)).astype(bf16), 0, 0).astype(f32)
    grad_qkv = grad_qkv.reshape(H, shard, 3, 2 * DH).transpose(2, 1, 0, 3)
    grad_qkv = grad_qkv.reshape(3, shard, width)

    inverse_one = inverse_rms(x_own)
    grad_one = after(grad_one, small_grads, grad_w_gate, grad_w_up, grad_w_out)
    grad_one = turned(grad_one, axis=1, forth=False).astype(f32)
    unit_one = x_own * inverse_one
    input_grad = (
        grad_resid + norm_back(grad_one * gain_attn, unit_one, inverse_one)
    ).astype(bf16)

    return (
        output.reshape(inputs.shape),
        input_grad.reshape(inputs.shape),
        grad_qkv[0],
        grad_qkv[1],
        grad_qkv[2],
        grad_w_out,
        grad_w_gate,
        grad_w_up,
        grad_w_down,
        small_grads[:shard],
        small_grads[shard : 2 * shard],
        small_grads[2 * shard : 3 * shard],
        small_grads[3 * shard :],
    )


def solution(mesh):
    cores = mesh.shape["in"]
    depth = mesh.shape["grp"] * cores // H
    split = Mesh(mesh.devices.reshape(depth, 2, H // (2 * cores), cores), EVERY)
    group = ("z", "y", "x")
    data = P(None, group, "c", None)
    matrix = P(EVERY, None)
    vector = P(EVERY)
    return jax.shard_map(
        functools.partial(body, depth=depth),
        mesh=split,
        in_specs=(data, data, P(None, group)) + (matrix,) * 7 + (vector,) * 4,
        out_specs=(data, data) + (matrix,) * 7 + (vector,) * 4,
        check_vma=False,
    )
```

time: 3250 us -> 868 us (0.27)
  waiting for transfers between devices: 2500 us -> 289 us
  matrix products: 471 us -> 215 us
  starting transfers between devices: 1.27 us -> 101 us
  blocking collectives: 84.4 us -> 19.5 us
  Pallas kernels: 0 us -> 43.3 us
    reduce_scatter x9 -> x4, waiting for transfers between devices: 1880 us -> 0.03 us  [over_chips(): lax.psum_scatter(total.astype(bf16), ('y', 'x'), scatter_dimension=0, til...]
    all_gather x11 -> x4, waiting for transfers between devices: 613 us -> 3.47 us  [the longest x3 3.47 us: gather_rows(): return lax.all_gather(block, ROWS, axis=0, tiled=True)]
    ppermute x0 -> x43, waiting for transfers between devices: none -> 233 us  [the longest x39 223 us: permute(): return lax.ppermute(value, 'z', shift(depth, step))]
    dot_general x14 -> x7, matrix products: 210 us -> 85.3 us  [contract_rows(): lax.dot_general(left, right, (((0,), (0,)), ((), ())), preferred_element_...]
    unnamed x2 -> x0, blocking collectives: 84.4 us -> none
    dot_general x26 -> x4, matrix products: 141 us -> 57.3 us  [product(): return jnp.dot(left, right, preferred_element_type=f32)]
    ppermute x0 -> x43, starting transfers between devices: none -> 67.9 us  [the longest x39 67.5 us: permute(): return lax.ppermute(value, 'z', shift(depth, step))]
    all_to_all x0 -> x8, waiting for transfers between devices: none -> 51.7 us  [the longest x7 51.7 us: exchange(): lax.all_to_all(values, order, split_axis=split, concat_axis=joined, tiled...]
  transfers between devices with their start and end apart: 22 -> 59, of which waited for: 13 -> 25; matrix products, arithmetic and copies ran while one was open for 15% -> 42% of each run, Pallas kernels for 0% -> 5%
where the time goes in v1:
time: 868 us; the launch traced here: 860 us
  waiting for transfers between devices  289 us (33%)
  matrix products  215 us (25%)
  starting transfers between devices  101 us (12%)
  local copies, waits for them, and re-layouts  89.1 us (10%)
  other arithmetic  86.3 us (10%)
  Pallas kernels  43.3 us (5%)
  blocking collectives  19.5 us (2%)
  between operations  17 us (2%)
    ppermute x39, waiting for transfers between devices, permute(): return lax.ppermute(value, 'z', shift(depth, step))  223 us
    dot_general x7, matrix products, contract_rows(): lax.dot_general(left, right, (((0,), (0,)), ((), ())), preferred_element_...  85.3 us
    dot_general x5, matrix products, against(): lax.dot_general(left, right, (((1,), (1,)), ((), ())), preferred_element_...  72.3 us
    ppermute x39, starting transfers between devices, permute(): return lax.ppermute(value, 'z', shift(depth, step))  67.5 us
    dot_general x4, matrix products, product(): return jnp.dot(left, right, preferred_element_type=f32)  57.3 us
    all_to_all x7, waiting for transfers between devices, exchange(): lax.all_to_all(values, order, split_axis=split, concat_axis=joined, tiled...  51.7 us
    pallas_call x1, Pallas kernels, attend_back(): pl.pallas_call(attend_back_kernel, grid=(slots, batches), in_specs=[smem,...  28.8 us
    all_to_all x7, starting transfers between devices, exchange(): lax.all_to_all(values, order, split_axis=split, concat_axis=joined, tiled...  28.4 us
  transfers between devices with their start and end apart: 59, of which 25 were waited for; matrix products, arithmetic and copies ran while one was open for 42% of the time, Pallas kernels for 5%

profile of v1, /device:TPU:0, one launch (start us, length us, event | category | flops | bytes accessed | tf_op | source)
XLA Modules:
  0.0 860.2 jit_solution(6575099459315703098)
XLA Ops:
  18.1 19.5 %all-gather = f32[8,1,210]{2,1,0:T(1,128)S(1)} all-gather(f32[1,1,210]{2,1,0:T(1,128)S(1)} %bitcast.207), channel_id=1, replica_groups=mesh['z'=4,'y'=2,'x'=2,'c'=2] {'y','x','c'}, dimensions={0}, use_global_device_ids=true | all-gather | bytes 7560 | tf_op jit(solution)/shard_map/all_gather | solution.py:379
  57.8 15.3 %collective-permute-done.3 = bf16[512,768]{1,0:T(8,128)(2,1)} collective-permute-done((bf16[512,768]{1,0:T(8,128)(2,1)S(1)}, bf16[512,768]{1,0:T(8,128)(2,1)}, u32[]{:S(2)}, u32[]{:S(2)}) %collective-permute-start.3) | collective-permute-done | bytes 786464 | tf_op jit(solution)/shard_map/ppermute | solution.py:225
  73.1 15.3 %collective-permute-done.4 = bf16[512,768]{1,0:T(8,128)(2,1)S(1)} collective-permute-done((bf16[512,768]{1,0:T(8,128)(2,1)S(1)}, bf16[512,768]{1,0:T(8,128)(2,1)S(1)}, u32[]{:S(2)}, u32[]{:S(2)}) %collective-permute-start.4) | collective-permute-done | bytes 786464 | tf_op jit(solution)/shard_map/ppermute | solution.py:225
  97.6 11.8 %fusion.2 = bf16[3072,2048]{1,0:T(8,128)(2,1)} fusion(bf16[3072,2048]{1,0:T(8,128)(2,1)} %all-gather.6.cloned.1.call-done, f32[2048]{0:T(1024)S(1)} %bitcast.205, f32[3072]{0:T(1024)S(1)} %add_rsqrt_fusion), kind=kLoop, calls=%fused_computation.4 | loop fusion | flops 25165824 | bytes 25186304 | tf_op jit(solution)/shard_map/convert_element_type | solution.py:416
  123.8 11.7 %collective-permute-done.5 = bf16[256,768]{1,0:T(8,128)(2,1)S(1)} collective-permute-done((bf16[256,768]{1,0:T(8,128)(2,1)}, bf16[256,768]{1,0:T(8,128)(2,1)S(1)}, u32[]{:S(2)}, u32[]{:S(2)}) %collective-permute-start.5) | collective-permute-done | bytes 393248 | tf_op jit(solution)/shard_map/ppermute | solution.py:225
  135.6 14.5 %collective-permute-done.6 = bf16[256,768]{1,0:T(8,128)(2,1)} collective-permute-done((bf16[256,768]{1,0:T(8,128)(2,1)}, bf16[256,768]{1,0:T(8,128)(2,1)}, u32[]{:S(2)}, u32[]{:S(2)}) %collective-permute-start.6) | collective-permute-done | bytes 393248 | tf_op jit(solution)/shard_map/ppermute | solution.py:225
  157.9 16.1 %fusion.78 = f32[3072,768]{1,0:T(8,128)} fusion(bf16[3072,2048]{1,0:T(8,128)(2,1)} %fusion.2, bf16[2048,768]{1,0:T(8,128)(2,1)} %constant_dynamic-update-slice_fusion), kind=kOutput, calls=%fused_computation.194 | convolution fusion | flops 9663676416 | bytes 25165824 | tf_op jit(solution)/shard_map/dot_general | solution.py:27
  174.0 14.5 %shard_map.237 = (bf16[2,4,2,192,768]{4,3,2,1,0:T(8,128)(2,1)}, bf16[2,4,2,192,256]{4,3,2,1,0:T(8,128)(2,1)S(1)}) custom-call(s32[4,2]{1,0:T(4,128)S(1)} %bitcast.154, f32[1]{0:T(128)} %bitcast.6.lam_ref, f32[2,4,2,192,768]{4,3,2,1,0:T(8,128)} %bitcast.166, f32[384,128]{1,0:T(8,128)S(1)} %get-tuple-element.266.cos_ref, ...), custom_call_target="tpu_custom_call" | custom-call | tf_op jit(solution)/shard_map/pallas_call | solution.py:173
  194.6 20.0 %all-to-all-done.2 = bf16[8,384,256]{1,2,0:T(8,128)(2,1)S(1)} async-done(((bf16[8,384,256]{1,2,0:T(8,128)(2,1)}), bf16[8,384,256]{1,2,0:T(8,128)(2,1)S(1)}, u32[]{:S(2)}, u32[]{:S(2)}) %all-to-all-start.2) | async-done | bytes 1572896 | tf_op jit(solution)/shard_map/all_to_all | solution.py:315
  214.8 27.1 %collective-permute-done.8 = bf16[1408,512]{0,1:T(8,128)(2,1)} collective-permute-done((bf16[1408,512]{0,1:T(8,128)(2,1)}, bf16[1408,512]{0,1:T(8,128)(2,1)}, u32[]{:S(2)}, u32[]{:S(2)}) %collective-permute-start.8) | collective-permute-done | bytes 1441824 | tf_op jit(solution)/shard_map/ppermute | solution.py:225
  265.9 38.0 %collective-permute-done.11 = bf16[176,2048]{1,0:T(8,128)(2,1)S(1)} collective-permute-done((bf16[176,2048]{1,0:T(8,128)(2,1)S(1)}, bf16[176,2048]{1,0:T(8,128)(2,1)S(1)}, u32[]{:S(2)}, u32[]{:S(2)}) %collective-permute-start.11) | collective-permute-done | bytes 720928 | tf_op jit(solution)/shard_map/ppermute | solution.py:225
  309.0 10.4 %collective-permute-done.9 = bf16[704,512]{1,0:T(8,128)(2,1)} collective-permute-done((bf16[704,512]{1,0:T(8,128)(2,1)}, bf16[704,512]{1,0:T(8,128)(2,1)}, u32[]{:S(2)}, u32[]{:S(2)}) %collective-permute-start.9) | collective-permute-done | bytes 720928 | tf_op jit(solution)/shard_map/ppermute | solution.py:225
  322.5 29.6 %fusion.67 = f32[1408,3072]{1,0:T(8,128)} fusion(bf16[3072,2048]{1,0:T(8,128)(2,1)} %all-gather.10.cloned.1.call-done, bf16[704,512]{0,1:T(8,128)(2,1)} %copy.113, bf16[704,512]{0,1:T(8,128)(2,1)} %copy.112, bf16[1408,512]{0,1:T(8,128)(2,1)} %collective-permute-done.8, bf16[1408,512]{0,1:T(8,128)(2,1)} %collective-permute-done.7, ...), kind=kOutput, calls=%fused_computation.185 | convolution fusion | flops 17745575936 | bytes 35651584 | tf_op jit(solution)/shard_map/dot_general | solution.py:35
  359.9 8.0 multiply_convert_fusion.2
  375.7 10.2 %collective-permute-done.15 = bf16[1536,2048]{1,0:T(8,128)(2,1)} collective-permute-done((bf16[1536,2048]{1,0:T(8,128)(2,1)}, bf16[1536,2048]{1,0:T(8,128)(2,1)}, u32[]{:S(2)}, u32[]{:S(2)}) %collective-permute-start.15) | collective-permute-done | bytes 6291488 | tf_op jit(solution)/shard_map/ppermute | solution.py:328
  385.9 10.4 %add_convert_fusion.1 = bf16[1536,2048]{1,0:T(8,128)(2,1)} fusion(bf16[1536,2048]{1,0:T(8,128)(2,1)} %collective-permute-done.15, bf16[1408,2048]{1,0:T(8,128)(2,1)} %constant_dynamic-update-slice_fusion.5, s32[]{:T(128)S(6)} %select_n.99, bf16[704,3072]{1,0:T(8,128)(2,1)} %copy-done.17, s32[]{:T(128)S(6)} %select_n.98), kind=kOutput, calls=%fused_computation.8 | convolution fusion | flops 4438622208 | bytes 17629192 | tf_op jit(solution)/shard_map/dot_general | solution.py:31
  397.0 21.1 %multiply_convert_fusion = (bf16[704,3072]{1,0:T(8,128)(2,1)}, bf16[704,3072]{1,0:T(8,128)(2,1)}) fusion(f32[1408,3072]{1,0:T(8,128)} %fusion.67, bf16[3072,2048]{1,0:T(8,128)(2,1)} %all-gather.12.cloned.1.call-done, bf16[1408,2048]{1,0:T(8,128)(2,1)} %constant_dynamic-update-slice_fusion.5, s32[]{:T(128)S(6)} %select_n.99), kind=kOutput, calls=%fused_computation.15 | convolution fusion | flops 8886484992 | bytes 41418756 | tf_op jit(solution)/shard_map/dot_general | solution.py:35
  418.1 22.1 %convolution_convert_fusion.2 = bf16[1536,2048]{1,0:T(8,128)(2,1)} fusion(s32[]{:T(128)S(6)} %select_n.100, bf16[704,3072]{1,0:T(8,128)(2,1)} %get-tuple-element.211, bf16[704,3072]{1,0:T(8,128)(2,1)} %get-tuple-element.210, bf16[704,512]{0,1:T(8,128)(2,1)S(1)} %copy-done.24, bf16[704,512]{0,1:T(8,128)(2,1)S(1)} %copy-done.25, ...), kind=kOutput, calls=%fused_computation.23 | convolution fusion | flops 8899002368 | bytes 20709380 | tf_op jit(solution)/shard_map/dot_general | solution.py:31
  447.1 11.5 %convolution_convert_fusion.6 = bf16[704,2048]{1,0:T(8,128)(2,1)S(1)} fusion(bf16[704,3072]{1,0:T(8,128)(2,1)} %copy-done.17, bf16[3072,2048]{1,0:T(8,128)(2,1)S(1)} %copy-done.48), kind=kOutput, calls=%fused_computation.40 | convolution fusion | flops 8859811840 | bytes 19791872 | tf_op jit(solution)/shard_map/dot_general | solution.py:27
  458.6 19.2 %add_convert_fusion = bf16[1536,2048]{1,0:T(8,128)(2,1)} fusion(bf16[1536,2048]{1,0:T(8,128)(2,1)} %collective-permute-done.16, bf16[1408,1536]{1,0:T(8,128)(2,1)S(1)} %copy-done.16, bf16[704,512]{0,1:T(8,128)(2,1)} %copy.113, bf16[704,512]{0,1:T(8,128)(2,1)} %copy.112, bf16[1408,512]{0,1:T(8,128)(2,1)} %collective-permute-done.8, ...), kind=kOutput, calls=%fused_computation.7 | convolution fusion | flops 8896643072 | bytes 22675456 | tf_op jit(solution)/shard_map/dot_general | solution.py:31
  494.4 23.6 %convolution_convert_fusion.1 = bf16[1408,2048]{1,0:T(8,128)(2,1)S(1)} fusion(bf16[1408,3072]{1,0:T(8,128)(2,1)} %pad_maximum_fusion, bf16[3072,2048]{1,0:T(8,128)(2,1)} %all-gather.10.cloned.1.call-done), kind=kOutput, calls=%fused_computation.22 | convolution fusion | flops 17719623680 | bytes 27000832 | tf_op jit(solution)/shard_map/dot_general | solution.py:27
  533.1 8.1 collective-permute-done.22
  544.2 12.3 %collective-permute-done.23 = bf16[704,512]{1,0:T(8,128)(2,1)} collective-permute-done((bf16[704,512]{1,0:T(8,128)(2,1)S(1)}, bf16[704,512]{1,0:T(8,128)(2,1)}, u32[]{:S(2)}, u32[]{:S(2)}) %collective-permute-start.23) | collective-permute-done | bytes 720928 | tf_op jit(solution)/shard_map/ppermute | solution.py:225
  556.5 11.6 %collective-permute-done.24 = bf16[704,512]{1,0:T(8,128)(2,1)} collective-permute-done((bf16[704,512]{1,0:T(8,128)(2,1)S(1)}, bf16[704,512]{1,0:T(8,128)(2,1)}, u32[]{:S(2)}, u32[]{:S(2)}) %collective-permute-start.24) | collective-permute-done | bytes 720928 | tf_op jit(solution)/shard_map/ppermute | solution.py:225
  597.3 9.3 %collective-permute-done.26 = bf16[704,512]{1,0:T(8,128)(2,1)} collective-permute-done((bf16[704,512]{1,0:T(8,128)(2,1)}, bf16[704,512]{1,0:T(8,128)(2,1)}, u32[]{:S(2)}, u32[]{:S(2)}) %collective-permute-start.26) | collective-permute-done | bytes 720928 | tf_op jit(solution)/shard_map/ppermute | solution.py:225
  606.5 14.0 %collective-permute-done.27 = bf16[704,512]{1,0:T(8,128)(2,1)} collective-permute-done((bf16[704,512]{1,0:T(8,128)(2,1)}, bf16[704,512]{1,0:T(8,128)(2,1)}, u32[]{:S(2)}, u32[]{:S(2)}) %collective-permute-start.27) | collective-permute-done | bytes 720928 | tf_op jit(solution)/shard_map/ppermute | solution.py:225
  620.6 28.8 %shard_map.238 = (bf16[2,4,2,192,768]{4,3,2,1,0:T(8,128)(2,1)}, f32[1,256]{1,0:T(1,128)S(1)}, f32[1,128]{1,0:T(1,128)S(1)}) custom-call(s32[4,2]{1,0:T(4,128)S(1)} %bitcast.155, f32[1]{0:T(128)} %bitcast.6.lam_ref, bf16[2,4,2,192,768]{4,3,2,1,0:T(8,128)(2,1)} %get-tuple-element.85.rot_ref, bf16[2,4,2,192,256]{4,3,2,1,0:T(8,128)(2,1)S(1)} %bitcast.152, ...), custom_call_target="tpu_custom_call" | custom-call | tf_op jit(solution)/shard_map/pallas_call | solution.py:193
  663.4 16.9 %collective-permute-done.28 = bf16[704,512]{1,0:T(8,128)(2,1)S(1)} collective-permute-done((bf16[704,512]{1,0:T(8,128)(2,1)S(1)}, bf16[704,512]{1,0:T(8,128)(2,1)S(1)}, u32[]{:S(2)}, u32[]{:S(2)}) %collective-permute-start.28) | collective-permute-done | bytes 720928 | tf_op jit(solution)/shard_map/ppermute | solution.py:225
  680.3 14.4 %collective-permute-done.29 = bf16[704,512]{1,0:T(8,128)(2,1)S(1)} collective-permute-done((bf16[704,512]{1,0:T(8,128)(2,1)S(1)}, bf16[704,512]{1,0:T(8,128)(2,1)S(1)}, u32[]{:S(2)}, u32[]{:S(2)}) %collective-permute-start.29) | collective-permute-done | bytes 720928 | tf_op jit(solution)/shard_map/ppermute | solution.py:225
  694.9 14.6 %convolution_convert_fusion.5 = bf16[2048,768]{1,0:T(8,128)(2,1)} fusion(bf16[3072,2048]{1,0:T(8,128)(2,1)} %fusion.2, bf16[3072,768]{1,0:T(8,128)(2,1)S(1)} %bitcast.190), kind=kOutput, calls=%fused_computation.39 | convolution fusion | flops 9665249280 | bytes 20447232 | tf_op jit(solution)/shard_map/dot_general | solution.py:31
  709.5 10.4 %multiply_reduce_fusion = (f32[2048]{0:T(1024)S(1)}, bf16[1536,2048]{1,0:T(8,128)(2,1)}) fusion(bf16[1536,2048]{1,0:T(8,128)(2,1)} %collective-permute-done.30, f32[1536]{0:T(1024)S(1)} %dynamic-slice.3, bf16[3072,2048]{1,0:T(8,128)(2,1)S(1)} %bitcast.159, s32[]{:T(128)S(6)} %select_n.98, bf16[1536,768]{1,0:T(8,128)(2,1)S(1)} %constant_dynamic-slice_fusion, ...), kind=kOutput, calls=%fused_computation.5 | convolution fusion | flops 4853856256 | bytes 24393732 | tf_op jit(solution)/shard_map/dot_general | solution.py:35
  739.6 24.2 %all-to-all-done.6 = bf16[8,64,1408]{2,1,0:T(8,128)(2,1)} async-done(((bf16[8,64,1408]{2,1,0:T(8,128)(2,1)}), bf16[8,64,1408]{2,1,0:T(8,128)(2,1)}, u32[]{:S(2)}, u32[]{:S(2)}) %all-to-all-start.6) | async-done | bytes 1441824 | tf_op jit(solution)/shard_map/all_to_all | solution.py:315
  (362 shorter events, 308.4 us)
Async XLA Ops:
  7.2 83.2 %all-gather.6.cloned.1.call-start = ((), (), s32[]{:S(2)}) async-start(), calls=%async_computation.12 | async-start | bytes 14155776 | tf_op jit(solution)/shard_map/all_gather | solution.py:311
  10.6 231.2 %all-gather.8.cloned.1.call-start = ((), (), s32[]{:S(2)}) async-start(), calls=%async_computation.13 | async-start | bytes 8650752 | tf_op jit(solution)/shard_map/all_gather | solution.py:386
  12.7 39.8 %all-to-all-start = ((bf16[8,64,768]{2,1,0:T(8,128)(2,1)}), bf16[8,64,768]{2,1,0:T(8,128)(2,1)S(1)}, u32[]{:S(2)}, u32[]{:S(2)}) async-start(bf16[8,64,768]{2,1,0:T(8,128)(2,1)} %copy.104), calls=%async_computation | async-start | bytes 1572864 | tf_op jit(solution)/shard_map/all_to_all | solution.py:315
  53.1 35.4 %collective-permute-start.4 = (bf16[512,768]{1,0:T(8,128)(2,1)S(1)}, bf16[512,768]{1,0:T(8,128)(2,1)S(1)}, u32[]{:S(2)}, u32[]{:S(2)}) collective-permute-start(bf16[512,768]{1,0:T(8,128)(2,1)S(1)} %bitcast.175), channel_id=1, source_target_pairs={{0,8},{8,16},{16,24},{24,0},{1,9},{9,17},{17,25},{25,1},{2,10},{10... | collective-permute-start | bytes 2359304 | tf_op jit(solution)/shard_map/ppermute | solution.py:225
  109.3 46.5 %all-to-all-start.1 = ((bf16[8,64,1408]{2,1,0:T(8,128)(2,1)}), bf16[8,64,1408]{2,1,0:T(8,128)(2,1)}, u32[]{:S(2)}, u32[]{:S(2)}) async-start(bf16[8,64,1408]{2,1,0:T(8,128)(2,1)} %bitcast.14), calls=%async_computation.1 | async-start | bytes 2883584 | tf_op jit(solution)/shard_map/all_to_all | solution.py:315
  155.8 58.9 %collective-permute-start.7 = (bf16[1408,512]{0,1:T(8,128)(2,1)}, bf16[1408,512]{0,1:T(8,128)(2,1)}, u32[]{:S(2)}, u32[]{:S(2)}) collective-permute-start(bf16[1408,512]{0,1:T(8,128)(2,1)} %bitcast.16), channel_id=1, source_target_pairs={{0,24},{8,0},{16,8},{24,16},{1,25},{9,1},{17,9},{25,17},{2,26},{10... | collective-permute-start | bytes 4325384 | tf_op jit(solution)/shard_map/ppermute | solution.py:225
  157.5 84.4 %collective-permute-start.8 = (bf16[1408,512]{0,1:T(8,128)(2,1)}, bf16[1408,512]{0,1:T(8,128)(2,1)}, u32[]{:S(2)}, u32[]{:S(2)}) collective-permute-start(bf16[1408,512]{0,1:T(8,128)(2,1)} %bitcast.16), channel_id=1, source_target_pairs={{0,8},{8,16},{16,24},{24,0},{1,9},{9,17},{17,25},{25,1},{2,10},{10... | collective-permute-start | bytes 4325384 | tf_op jit(solution)/shard_map/ppermute | solution.py:225
  194.1 128.4 %all-gather.10.cloned.1.call-start = ((), (), s32[]{:S(2)}) async-start(), calls=%async_computation.14 | async-start | bytes 14155776 | tf_op jit(solution)/shard_map/all_gather | solution.py:311
  252.1 144.9 %all-gather.12.cloned.1.call-start = ((), (), s32[]{:S(2)}) async-start(), calls=%async_computation.16 | async-start | bytes 14155776 | tf_op jit(solution)/shard_map/all_gather | solution.py:311
  253.8 224.0 %reduce-scatter.5.cloned.1.call-start = ((), (), s32[]{:S(2)}) async-start(), calls=%async_computation.15 | async-start | bytes 7864320 | tf_op jit(solution)/shard_map/reduce_scatter | solution.py:336
  253.9 50.0 %collective-permute-start.11 = (bf16[176,2048]{1,0:T(8,128)(2,1)S(1)}, bf16[176,2048]{1,0:T(8,128)(2,1)S(1)}, u32[]{:S(2)}, u32[]{:S(2)}) collective-permute-start(bf16[176,2048]{1,0:T(8,128)(2,1)S(1)} %copy-done.22), channel_id=1, source_target_pairs={{0,24},{8,0},{16,8},{24,16},{1,25},{9,1},{17,9},{25,17},{2,26},{10... | collective-permute-start | bytes 2162696 | tf_op jit(solution)/shard_map/ppermute | solution.py:225
  254.4 49.5 %collective-permute-start.12 = (bf16[176,2048]{1,0:T(8,128)(2,1)S(1)}, bf16[176,2048]{1,0:T(8,128)(2,1)S(1)}, u32[]{:S(2)}, u32[]{:S(2)}) collective-permute-start(bf16[176,2048]{1,0:T(8,128)(2,1)S(1)} %copy-done.22), channel_id=1, source_target_pairs={{0,8},{8,16},{16,24},{24,0},{1,9},{9,17},{17,25},{25,1},{2,10},{10... | collective-permute-start | bytes 2162696 | tf_op jit(solution)/shard_map/ppermute | solution.py:225
  258.7 48.0 %collective-permute-start.10 = (bf16[704,512]{1,0:T(8,128)(2,1)}, bf16[704,512]{1,0:T(8,128)(2,1)}, u32[]{:S(2)}, u32[]{:S(2)}) collective-permute-start(bf16[704,512]{1,0:T(8,128)(2,1)} %copy.111), channel_id=1, source_target_pairs={{0,8},{8,16},{16,24},{24,0},{1,9},{9,17},{17,25},{25,1},{2,10},{10... | collective-permute-start | bytes 2162696 | tf_op jit(solution)/shard_map/ppermute | solution.py:225
  261.1 58.3 %collective-permute-start.9 = (bf16[704,512]{1,0:T(8,128)(2,1)}, bf16[704,512]{1,0:T(8,128)(2,1)}, u32[]{:S(2)}, u32[]{:S(2)}) collective-permute-start(bf16[704,512]{1,0:T(8,128)(2,1)} %copy.110), channel_id=1, source_target_pairs={{0,24},{8,0},{16,8},{24,16},{1,25},{9,1},{17,9},{25,17},{2,26},{10... | collective-permute-start | bytes 2162696 | tf_op jit(solution)/shard_map/ppermute | solution.py:225
  303.9 48.3 %collective-permute-start.13 = (bf16[88,2048]{1,0:T(8,128)(2,1)S(1)}, bf16[88,2048]{1,0:T(8,128)(2,1)S(1)}, u32[]{:S(2)}, u32[]{:S(2)}) collective-permute-start(bf16[88,2048]{1,0:T(8,128)(2,1)S(1)} %slice.309), channel_id=1, source_target_pairs={{0,24},{8,0},{16,8},{24,16},{1,25},{9,1},{17,9},{25,17},{2,26},{10... | collective-permute-start | bytes 1081352 | tf_op jit(solution)/shard_map/ppermute | solution.py:225
  304.7 47.4 %collective-permute-start.14 = (bf16[88,2048]{1,0:T(8,128)(2,1)}, bf16[88,2048]{1,0:T(8,128)(2,1)S(1)}, u32[]{:S(2)}, u32[]{:S(2)}) collective-permute-start(bf16[88,2048]{1,0:T(8,128)(2,1)} %slice.310), channel_id=1, source_target_pairs={{0,8},{8,16},{16,24},{24,0},{1,9},{9,17},{17,25},{25,1},{2,10},{10... | collective-permute-start | bytes 1081352 | tf_op jit(solution)/shard_map/ppermute | solution.py:225
  396.3 171.8 %reduce-scatter.7.cloned.1.call-start = ((), (), s32[]{:S(2)}) async-start(), calls=%async_computation.17 | async-start | bytes 7864320 | tf_op jit(solution)/shard_map/reduce_scatter | solution.py:336
  479.0 39.0 %collective-permute-start.17 = (bf16[88,2048]{1,0:T(8,128)(2,1)}, bf16[88,2048]{1,0:T(8,128)(2,1)S(1)}, u32[]{:S(2)}, u32[]{:S(2)}) collective-permute-start(bf16[88,2048]{1,0:T(8,128)(2,1)} %get-tuple-element.237), channel_id=1, source_target_pairs={{0,8},{8,16},{16,24},{24,0},{1,9},{9,17},{17,25},{25,1},{2,10},{10... | collective-permute-start | bytes 1081352 | tf_op jit(solution)/shard_map/ppermute | solution.py:225
  480.5 37.6 %collective-permute-start.18 = (bf16[88,2048]{1,0:T(8,128)(2,1)}, bf16[88,2048]{1,0:T(8,128)(2,1)}, u32[]{:S(2)}, u32[]{:S(2)}) collective-permute-start(bf16[88,2048]{1,0:T(8,128)(2,1)} %get-tuple-element.238), channel_id=1, source_target_pairs={{0,24},{8,0},{16,8},{24,16},{1,25},{9,1},{17,9},{25,17},{2,26},{10... | collective-permute-start | bytes 1081352 | tf_op jit(solution)/shard_map/ppermute | solution.py:225
  482.9 35.2 %collective-permute-start.19 = (bf16[88,2048]{1,0:T(8,128)(2,1)}, bf16[88,2048]{1,0:T(8,128)(2,1)}, u32[]{:S(2)}, u32[]{:S(2)}) collective-permute-start(bf16[88,2048]{1,0:T(8,128)(2,1)} %get-tuple-element.239), channel_id=1, source_target_pairs={{0,8},{8,16},{16,24},{24,0},{1,9},{9,17},{17,25},{25,1},{2,10},{10... | collective-permute-start | bytes 1081352 | tf_op jit(solution)/shard_map/ppermute | solution.py:225
  482.9 35.3 %collective-permute-start.20 = (bf16[88,2048]{1,0:T(8,128)(2,1)}, bf16[88,2048]{1,0:T(8,128)(2,1)}, u32[]{:S(2)}, u32[]{:S(2)}) collective-permute-start(bf16[88,2048]{1,0:T(8,128)(2,1)} %get-tuple-element.236), channel_id=1, source_target_pairs={{0,24},{8,0},{16,8},{24,16},{1,25},{9,1},{17,9},{25,17},{2,26},{10... | collective-permute-start | bytes 1081352 | tf_op jit(solution)/shard_map/ppermute | solution.py:225
  527.1 41.0 %collective-permute-start.24 = (bf16[704,512]{1,0:T(8,128)(2,1)S(1)}, bf16[704,512]{1,0:T(8,128)(2,1)}, u32[]{:S(2)}, u32[]{:S(2)}) collective-permute-start(bf16[704,512]{1,0:T(8,128)(2,1)S(1)} %get-tuple-element.220), channel_id=1, source_target_pairs={{0,24},{8,0},{16,8},{24,16},{1,25},{9,1},{17,9},{25,17},{2,26},{10... | collective-permute-start | bytes 2162696 | tf_op jit(solution)/shard_map/ppermute | solution.py:225
  581.7 38.8 %all-to-all-start.3 = ((bf16[384,8,256]{2,0,1:T(8,128)(2,1)}), bf16[384,8,256]{2,0,1:T(8,128)(2,1)S(1)}, u32[]{:S(2)}, u32[]{:S(2)}) async-start(bf16[384,8,256]{2,0,1:T(8,128)(2,1)} %bitcast.147), calls=%async_computation.5 | async-start | bytes 3145728 | tf_op jit(solution)/shard_map/all_to_all | solution.py:315
  585.3 229.9 %reduce-scatter.11.cloned.1.call-start = ((), (), s32[]{:S(2)}) async-start(), calls=%async_computation.19 | async-start | bytes 5242880 | tf_op jit(solution)/shard_map/reduce_scatter | solution.py:336
  596.8 249.0 %reduce-scatter.9.cloned.1.call-start = ((), (), s32[]{:S(2)}) async-start(), calls=%async_computation.18 | async-start | bytes 7864320 | tf_op jit(solution)/shard_map/reduce_scatter | solution.py:336
  657.0 52.4 %collective-permute-start.30 = (bf16[1536,2048]{1,0:T(8,128)(2,1)S(1)}, bf16[1536,2048]{1,0:T(8,128)(2,1)}, u32[]{:S(2)}, u32[]{:S(2)}) collective-permute-start(bf16[1536,2048]{1,0:T(8,128)(2,1)S(1)} %convolution_convert_fusion), channel_id=1, source_target_pairs={{0,1},{1,0},{2,3},{3,2},{4,5},{5,4},{6,7},{7,6},{8,9},{9,8},{10,11... | collective-permute-start | bytes 18874376 | tf_op jit(solution)/shard_map/ppermute | solution.py:328
  724.0 39.9 %all-to-all-start.6 = ((bf16[8,64,1408]{2,1,0:T(8,128)(2,1)}), bf16[8,64,1408]{2,1,0:T(8,128)(2,1)}, u32[]{:S(2)}, u32[]{:S(2)}) async-start(bf16[8,64,1408]{2,1,0:T(8,128)(2,1)} %bitcast.49), calls=%async_computation.9 | async-start | bytes 2883584 | tf_op jit(solution)/shard_map/all_to_all | solution.py:315
  731.9 35.2 %collective-permute-start.31 = (bf16[256,768]{1,0:T(8,128)(2,1)}, bf16[256,768]{1,0:T(8,128)(2,1)}, u32[]{:S(2)}, u32[]{:S(2)}) collective-permute-start(bf16[256,768]{1,0:T(8,128)(2,1)} %get-tuple-element.227), channel_id=1, source_target_pairs={{0,8},{8,16},{16,24},{24,0},{1,9},{9,17},{17,25},{25,1},{2,10},{10... | collective-permute-start | bytes 1179656 | tf_op jit(solution)/shard_map/ppermute | solution.py:225
  735.7 73.1 %collective-permute-start.41 = (bf16[256,768]{1,0:T(8,128)(2,1)}, bf16[256,768]{1,0:T(8,128)(2,1)}, u32[]{:S(2)}, u32[]{:S(2)}) collective-permute-start(bf16[256,768]{1,0:T(8,128)(2,1)} %get-tuple-element.225), channel_id=1, source_target_pairs={{0,8},{8,16},{16,24},{24,0},{1,9},{9,17},{17,25},{25,1},{2,10},{10... | collective-permute-start | bytes 1179656 | tf_op jit(solution)/shard_map/ppermute | solution.py:225
  735.7 73.1 %collective-permute-start.42 = (bf16[256,768]{1,0:T(8,128)(2,1)}, bf16[256,768]{1,0:T(8,128)(2,1)}, u32[]{:S(2)}, u32[]{:S(2)}) collective-permute-start(bf16[256,768]{1,0:T(8,128)(2,1)} %get-tuple-element.224), channel_id=1, source_target_pairs={{0,24},{8,0},{16,8},{24,16},{1,25},{9,1},{17,9},{25,17},{2,26},{10... | collective-permute-start | bytes 1179656 | tf_op jit(solution)/shard_map/ppermute | solution.py:225
  769.5 39.3 %collective-permute-start.39 = (bf16[256,768]{1,0:T(8,128)(2,1)}, bf16[256,768]{1,0:T(8,128)(2,1)}, u32[]{:S(2)}, u32[]{:S(2)}) collective-permute-start(bf16[256,768]{1,0:T(8,128)(2,1)} %get-tuple-element.229), channel_id=1, source_target_pairs={{0,8},{8,16},{16,24},{24,0},{1,9},{9,17},{17,25},{25,1},{2,10},{10... | collective-permute-start | bytes 1179656 | tf_op jit(solution)/shard_map/ppermute | solution.py:225
  770.1 38.7 %collective-permute-start.40 = (bf16[256,768]{1,0:T(8,128)(2,1)}, bf16[256,768]{1,0:T(8,128)(2,1)}, u32[]{:S(2)}, u32[]{:S(2)}) collective-permute-start(bf16[256,768]{1,0:T(8,128)(2,1)} %get-tuple-element.228), channel_id=1, source_target_pairs={{0,24},{8,0},{16,8},{24,16},{1,25},{9,1},{17,9},{25,17},{2,26},{10... | collective-permute-start | bytes 1179656 | tf_op jit(solution)/shard_map/ppermute | solution.py:225
  (81 other events, 1502.0 us)
Sparse Core Ops, SparseCore 0:
  10.8 79.6 all-gather.5
  93.3 100.8 all-gather.7
  252.2 70.2 all-gather.9
  324.8 72.1 all-gather.11
  399.8 70.2 reduce-scatter.4
  478.0 70.3 reduce-scatter.6
  596.9 51.5 reduce-scatter.10
  720.1 85.4 reduce-scatter.8

commit v2 on v1

--- a/solution.py
+++ b/solution.py
@@ -183,6 +183,7 @@
             jax.ShapeDtypeStruct(dims + (2 * DH,), bf16),
         ],
         compiler_params=pltpu.CompilerParams(vmem_limit_bytes=48 * 1024 * 1024),
+        cost_estimate=pl.CostEstimate(flops=1, bytes_accessed=1, transcendentals=0),
     )(lengths, lam, raw.reshape(dims + (6 * DH,)), cos_table, sin_table, gain)
     return rot, headed
 
@@ -210,7 +211,195 @@
             pltpu.VMEM((halves * rows, 2 * DH), f32),
         ],
         compiler_params=pltpu.CompilerParams(vmem_limit_bytes=48 * 1024 * 1024),
+        cost_estimate=pl.CostEstimate(flops=1, bytes_accessed=1, transcendentals=0),
     )(lengths, lam, rot, grad_headed.reshape(dims + (2 * DH,)), cos_table, sin_table, gain)
+
+
+TILE = 256
+
+
+def tile_rows(rows):
+    return next(t for t in (TILE, 128, 64, 32, 16) if rows % t == 0)
+
+
+def row_call(
+    kernel, cores, rows_in, whole_in, half_in, rows_out, half_out, shared=(), sums=()
+):
+    total = rows_in[0].shape[0]
+    count = total if cores is None else total // 2
+    tile = tile_rows(count)
+    steps = count // tile
+    first = jnp.zeros((1,), jnp.int32) if cores is None else cores * steps
+    params = dict(memory_space=pltpu.VMEM)
+
+    def of_all(cols):
+        return pl.BlockSpec((tile, cols), lambda i, first: (first[0] + i, 0), **params)
+
+    def of_half(cols):
+        return pl.BlockSpec((tile, cols), lambda i, first: (i, 0), **params)
+
+    n_in = len(rows_in) + len(whole_in) + len(half_in)
+
+    def body_kernel(first, *refs):
+        kernel(*refs[:n_in], *refs[n_in + len(shared) :])
+
+    return pl.pallas_call(
+        body_kernel,
+        grid_spec=pltpu.PrefetchScalarGridSpec(
+            num_scalar_prefetch=1,
+            grid=(steps,),
+            in_specs=[of_all(v.shape[1]) for v in rows_in]
+            + [pl.BlockSpec(v.shape, lambda i, first: (0, 0), **params) for v in whole_in]
+            + [of_half(v.shape[1]) for v in half_in]
+            + [pl.BlockSpec(memory_space=pl.ANY) for _ in shared],
+            out_specs=[of_all(c) for c, _ in rows_out]
+            + [of_half(c) for c, _ in half_out]
+            + [pl.BlockSpec(shape, lambda i, first: (0, 0), **params) for shape, _ in sums],
+        ),
+        out_shape=[jax.ShapeDtypeStruct((total, c), d) for c, d in rows_out]
+        + [jax.ShapeDtypeStruct((count, c), d) for c, d in half_out]
+        + [jax.ShapeDtypeStruct(shape, d) for shape, d in sums],
+        input_output_aliases={1 + n_in + i: i for i in range(len(shared))},
+        compiler_params=pltpu.CompilerParams(vmem_limit_bytes=56 * 1024 * 1024),
+        cost_estimate=pl.CostEstimate(flops=1, bytes_accessed=1, transcendentals=0),
+    )(first, *rows_in, *whole_in, *half_in, *shared)
+
+
+def norm_product_kernel(x_ref, gain_ref, weight_ref, inverse_ref, normed_ref, out_ref):
+    values = x_ref[...].astype(f32)
+    inverse = inverse_rms(values)
+    normed = (values * inverse * gain_ref[...]).astype(bf16)
+    inverse_ref[...] = inverse
+    normed_ref[...] = normed
+    out_ref[...] = product(normed, weight_ref[...])
+
+
+def column_pieces(refs, units):
+    column = 0
+    found, late = [], None
+    for ref in refs:
+        cols = ref.shape[1]
+        if ref.shape[0] == units:
+            if late is None:
+                late = ref
+                continue
+            found.append((column, late[...], ref[...]))
+            late = None
+        else:
+            found.append((column, ref[:units], ref[units:]))
+        column += cols
+    return found
+
+
+def gate_up_kernel(x_ref, *refs):
+    *pieces, gate_ref, up_ref, hidden_ref = refs
+    gate = up = 0.0
+    for start, gate_part, up_part in column_pieces(pieces, gate_ref.shape[1]):
+        values = x_ref[:, start : start + gate_part.shape[1]]
+        gate += against(values, gate_part)
+        up += against(values, up_part)
+    gate_ref[...] = gate
+    up_ref[...] = up
+    hidden_ref[...] = (gate * jax.nn.sigmoid(gate) * up).astype(bf16)
+
+
+def add_other(value, other):
+    return value + other[0][...].astype(f32) if other else value
+
+
+def product_kernel(x_ref, weight_ref, *refs):
+    refs[-1][...] = add_other(product(x_ref[...], weight_ref[...]), refs[:-1]).astype(bf16)
+
+
+def gate_up_back_kernel(n_pieces, grad_ref, gate_ref, up_ref, down_ref, *refs):
+    pieces, other, (gate_out, up_out, out_ref) = refs[:n_pieces], refs[n_pieces:-3], refs[-3:]
+    grad_hidden = against(grad_ref[...], down_ref[...])
+    gate = gate_ref[...]
+    share = jax.nn.sigmoid(gate)
+    grad_gate = grad_hidden * up_ref[...] * share * (1.0 + gate * (1.0 - share))
+    grad_gate = grad_gate.astype(bf16)
+    grad_up = (grad_hidden * (gate * share)).astype(bf16)
+    gate_out[...] = grad_gate
+    up_out[...] = grad_up
+    for start, gate_part, up_part in column_pieces(pieces, gate_ref.shape[1]):
+        cols = slice(start, start + gate_part.shape[1])
+        grad = product(grad_gate, gate_part) + product(grad_up, up_part)
+        if other:
+            grad += other[0][:, cols].astype(f32)
+        out_ref[:, cols] = grad.astype(bf16)
+
+
+def place_units_kernel(depth, team, grad_ref, gate_ref, up_ref):
+    shard = gate_ref.shape[0]
+    units = grad_ref.shape[1] // 2
+    part = units // depth
+    for source in range(team):
+        rows = grad_ref[source * shard : (source + 1) * shard, :].astype(f32)
+        for first, out_ref in ((0, gate_ref), (units, up_ref)):
+            for z in range(depth):
+                column = (z * team + source) * part
+                start = first + z * part
+                out_ref[:, column : column + part] = rows[:, start : start + part]
+
+
+def place_units(grad, depth, team):
+    shape = (grad.shape[0] // team, team * grad.shape[1] // 2)
+    return pl.pallas_call(
+        functools.partial(place_units_kernel, depth, team),
+        out_shape=[jax.ShapeDtypeStruct(shape, f32)] * 2,
+        compiler_params=pltpu.CompilerParams(vmem_limit_bytes=40 * 1024 * 1024),
+        cost_estimate=pl.CostEstimate(flops=1, bytes_accessed=1, transcendentals=0),
+    )(grad)
+
+
+def against_kernel(grad_ref, weight_ref, out_ref):
+    out_ref[...] = against(grad_ref[...], weight_ref[...]).astype(bf16)
+
+
+def inputs_back_kernel(grad_ref, x_ref, inverse_ref, weight_ref, other_ref, out_ref, sum_ref):
+    @pl.when(pl.program_id(0) == 0)
+    def _():
+        sum_ref[...] = jnp.zeros_like(sum_ref)
+
+    grad = against(grad_ref[...], weight_ref[...]) + other_ref[...].astype(f32)
+    out_ref[...] = grad.astype(bf16)
+    part = grad * (x_ref[...].astype(f32) * inverse_ref[...])
+    sum_ref[...] += part.reshape(-1, 8, part.shape[1]).sum(axis=0)
+
+
+def columns_kernel(left_ref, right_ref, *refs):
+    *other, out_ref, total = refs
+    step = pl.program_id(0)
+
+    @pl.when(step == 0)
+    def _():
+        total[...] = contract_rows(left_ref[...], right_ref[...])
+
+    @pl.when(step > 0)
+    def _():
+        total[...] += contract_rows(left_ref[...], right_ref[...])
+
+    @pl.when(step == pl.num_programs(0) - 1)
+    def _():
+        out_ref[...] = add_other(total[...], other).astype(bf16)
+
+
+def columns_call(left, right, *other):
+    rows = left.shape[0]
+    tile = next(t for t in (1024, 512, 384, 256, 192, 128, 64, 32, 16) if rows % t == 0)
+    shape = (left.shape[1], right.shape[1])
+    whole = pl.BlockSpec(shape, lambda k: (0, 0))
+    return pl.pallas_call(
+        columns_kernel,
+        grid=(rows // tile,),
+        in_specs=[pl.BlockSpec((tile, v.shape[1]), lambda k: (k, 0)) for v in (left, right)]
+        + [whole] * len(other),
+        out_specs=whole,
+        out_shape=jax.ShapeDtypeStruct(shape, bf16),
+        scratch_shapes=[pltpu.VMEM(shape, f32)],
+        compiler_params=pltpu.CompilerParams(vmem_limit_bytes=56 * 1024 * 1024),
+        cost_estimate=pl.CostEstimate(flops=1, bytes_accessed=1, transcendentals=0),
+    )(left, right, *other)
 
 
 def shift(depth, step):
@@ -239,6 +428,11 @@
             half = block.shape[0] // 2
             self.far = (permute(above[:half], depth, -1), permute(below[half:], depth, 1))
 
+    def pieces(self):
+        above = [pair[0] for pair in self.near[1:]]
+        below = [pair[1] for pair in self.near[:0:-1]]
+        return [self.block] + above + list(self.far or ()) + below
+
     def joined(self, axis, *others):
         near, far = self.near[1:], self.far
         if others:
@@ -256,12 +450,11 @@
 
 
 class Scatter:
-    def __init__(self, blocks):
-        depth = len(blocks)
-        half = blocks[0].shape[0] // 2
+    def __init__(self, tops, bottoms):
+        depth = len(tops)
         self.pairs = [
-            [(blocks[k][:half], blocks[-k % depth][half:]) for k in range(depth // 2 + 1)],
-            [(blocks[k][half:], blocks[-k % depth][:half]) for k in range((depth - 1) // 2 + 1)],
+            [(tops[k], bottoms[-k % depth]) for k in range(depth // 2 + 1)],
+            [(bottoms[k], tops[-k % depth]) for k in range((depth - 1) // 2 + 1)],
         ]
         self.depth = depth
         self.first = self.move(self.pairs[0][-1]) if depth > 1 else None
@@ -287,15 +480,25 @@
         return self.third
 
     def total(self, *others):
-        (top, _), (bottom, _) = self.pairs[0][0], self.pairs[1][0]
-        bottom = self.pairs[0][0][1]
+        top, bottom = self.pairs[0][0]
         top, bottom = top.astype(f32), bottom.astype(f32)
         third, second, _ = lax.optimization_barrier((self.third, self.second, others))
         for pair, swap in ((third, False), (second, True)):
             if pair is not None:
                 up, down = pair[::-1] if swap else pair
                 top, bottom = top + up.astype(f32), bottom + down.astype(f32)
-        return jnp.concatenate([top, bottom], axis=0)
+        return top, bottom
+
+
+def scatter_straight(blocks):
+    depth = len(blocks)
+    moved = [permute(blocks[k], depth, k) for k in range(1, depth)]
+    return sum((v.astype(f32) for v in moved), blocks[0].astype(f32))
+
+
+def halves(blocks):
+    half = blocks[0].shape[0] // 2
+    return [block[:half] for block in blocks], [block[half:] for block in blocks]
 
 
 def turn_blocks(values, depth, axis, forth=True):
@@ -324,16 +527,11 @@
 
 
 def across(values):
-    values = values.astype(bf16)
-    return values, lax.ppermute(values, "c", [(0, 1), (1, 0)])
-
-
-def over_cores(compute, theirs, mine):
-    return compute(mine) + across(compute(theirs))[1].astype(f32)
+    return lax.ppermute(values, "c", [(0, 1), (1, 0)])
 
 
 def over_chips(total):
-    return lax.psum_scatter(total.astype(bf16), ("y", "x"), scatter_dimension=0, tiled=True)
+    return lax.psum_scatter(total, ("y", "x"), scatter_dimension=0, tiled=True)
 
 
 def body(
@@ -376,24 +574,27 @@
             lambda_params.astype(f32), lengths[:, 0].astype(f32),
         ]
     )[None]
-    small = lax.all_gather(after(small, qkv), TEAM, axis=0, tiled=True)
+    small = lax.all_gather(after(small, natural(qkv)), TEAM, axis=0, tiled=True)
     length_all = small[:, -batches:].reshape(chips, 2, batches)[:, 0].astype(jnp.int32)
     far_small = [permute(small, depth, -k) for k in range(1, depth)]
-    qkv_ring = Gather(natural(qkv), depth, lambda near: after(near, far_small))
+    out_ring = Gather(w_out, depth, lambda near: after(near, natural(qkv)))
+    qkv_ring = Gather(
+        natural(qkv),
+        depth,
+        lambda near: after(near, far_small, out_ring.last()),
+    )
     small = jnp.concatenate([small] + far_small, axis=0).reshape(depth, team, -1)
     small = turned(small, axis=0, forth=False)
     qkv_near = qkv_ring.first()
-    out_w = lax.all_gather(w_out, EVERY, axis=0, tiled=True)
+    out_w = out_ring.joined(0).reshape(depth, shard, width)
+    out_w = lax.all_gather(out_w, TEAM, axis=1, tiled=False)
+    out_w = turned(out_w, axis=0, forth=False).reshape(width, width)
 
     def by_units(w):
         w = w.reshape(shard, depth, team, hidden_shard).transpose(2, 0, 1, 3)
         return w.reshape(team * shard, units)
 
     gate_up = jnp.concatenate([by_units(w_gate), by_units(w_up)], axis=1)
-    def to_units(grad):
-        grad = grad.reshape(team, shard, depth, hidden_shard).transpose(1, 2, 0, 3)
-        return grad.reshape(shard, places * hidden_shard)
-
     n_lam = lambda_params.shape[0]
     gain_attn = small[:, :, :shard].reshape(1, width)
     gain_head = small[:, :, shard : 2 * shard].reshape(H, 2 * DH)
@@ -411,16 +612,14 @@
     sine = jnp.sin(angles)
     sin_table = jnp.concatenate([-sine, sine], axis=1)
 
-    x_float = after(x_all, *qkv_near).astype(f32)
-    inverse_all = inverse_rms(x_float)
-    normed_one = (x_float * inverse_all * turned(gain_attn, axis=1)).astype(bf16)
-    qkv_w = qkv_ring.joined(0, normed_one)
-    gate_up = exchange(after(gate_up, normed_one), 0, 0, TEAM).T
+    gate_up = exchange(after(gate_up, *qkv_near), 0, 0, TEAM).T
+    x_all = after(x_all, *qkv_ring.last(), gate_up)
+    inverse_all, normed_one, raw = row_call(
+        norm_product_kernel, None, [x_all], [turned(gain_attn, axis=1), qkv_ring.joined(0)], [],
+        [(1, f32), (width, bf16), (6 * DH, f32)], [],
+    )
     gate_up_ring = Gather(gate_up, depth)
-    gate_up_w = gate_up_ring.joined(1)
-    down_ring = Gather(after(w_down, *gate_up_ring.first()), depth)
-    raw = product(normed_one, qkv_w)
-    rot, headed = attend(length_all, lam, after(raw, gate_up), cos_table, sin_table, gain_mine, dims)
+    rot, headed = attend(length_all, lam, raw, cos_table, sin_table, gain_mine, dims)
     headed_own = exchange(headed.reshape(team * own_rows, 2 * DH), 0, 1)
     headed_own = after(headed_own, *gate_up_ring.first())
 
@@ -435,79 +634,98 @@
     grad_own = jnp.where(valid, cotangent.reshape(own_rows, width), 0)
     grad_all = gather_rows(grad_own)
 
-    gate_up_val = against(gate_up_w, normed_two)
-    gate_val, up_val = gate_up_val[:units], gate_up_val[units:]
-    down_w = turned(down_ring.joined(0, gate_up_val), axis=0, forth=False)
-    sigmoid_gate = jax.nn.sigmoid(gate_val)
-    activation = gate_val * sigmoid_gate
-    hidden = (activation * up_val).astype(bf16)
-
-    def over_units(weight):
-        return lambda values: contract_rows(values, weight)
-
-    out_rows = over_cores(over_units(down_w), *split_cores(hidden, 1)).astype(bf16)
-    grad_hidden = against(down_w, after(grad_all, out_rows))
-    grad_gate = grad_hidden * up_val * sigmoid_gate * (1.0 + gate_val * (1.0 - sigmoid_gate))
-    grad_up = grad_hidden * activation
-    grad_gate_up = jnp.concatenate([grad_gate.astype(bf16), grad_up.astype(bf16)], axis=0)
-
+    mine = lax.axis_index("c")[None].astype(jnp.int32)
+    gate_up_w = gate_up_ring.pieces()
+    gate_val, up_val, hidden = row_call(
+        gate_up_kernel, None, [normed_two], gate_up_w, [],
+        [(units, f32), (units, f32), (units, bf16)], [],
+    )
+    down_ring = Gather(
+        after(w_down, *gate_up_ring.last()), depth, lambda near: after(near, hidden)
+    )
+    down_w = turned(down_ring.joined(0), axis=0, forth=False)
+
+    (sent,) = row_call(product_kernel, 1 - mine, [hidden], [down_w], [], [], [(width, bf16)])
+    (out_rows,) = row_call(
+        product_kernel, mine, [hidden], [down_w], [across(sent)], [], [(width, bf16)]
+    )
+    grad_all = after(grad_all, out_rows)
     out_rows = over_chips(out_rows)
-    theirs, mine = split_cores(grad_gate_up, 1)
-    sent = across(over_units(gate_up_w)(theirs))
-    grad_w_down = product(hidden, after(grad_all, sent[0])).astype(bf16)
+
+    grads = [(units, bf16), (units, bf16)]
+    back_kernel = functools.partial(gate_up_back_kernel, len(gate_up_w))
+    back_in = [grad_all, gate_val, up_val]
+    *grad_gate_up, sent = row_call(
+        back_kernel, 1 - mine, back_in, [down_w, *gate_up_w], [], grads, [(width, bf16)]
+    )
+    grad_w_down = columns_call(hidden, after(grad_all, sent))
+    *grad_gate_up, grad_two = row_call(
+        back_kernel, mine, back_in, [down_w, *gate_up_w],
+        [after(across(sent), grad_w_down)], grads, [(width, bf16)], grad_gate_up,
+    )
     down_blocks = grad_w_down.reshape(depth, hidden_shard, width)
     down_back = Scatter(
-        [
-            lax.dynamic_index_in_dim(down_blocks, (lax.axis_index("z") + k) % depth, 0, False)
-            for k in range(depth)
-        ]
-    )
-    grad_two = over_units(gate_up_w)(after(mine, grad_w_down))
-    grad_two = (grad_two + sent[1].astype(f32)).astype(bf16)
+        *halves(
+            [
+                lax.dynamic_index_in_dim(down_blocks, (lax.axis_index("z") + k) % depth, 0, False)
+                for k in range(depth)
+            ]
+        )
+    )
+    grad_two = after(grad_two, *down_back.first)
     down_back.plain()
-    grad_w_gate_up = product(after(grad_gate_up, grad_two), normed_two).astype(bf16)
-    down_back.added(*down_back.second, grad_w_gate_up)
-    gate_up_back = Scatter(jnp.split(grad_w_gate_up, depth, axis=1))
+    grad_w_gate, grad_w_up = (
+        columns_call(after(v, grad_two), normed_two) for v in grad_gate_up
+    )
+    down_back.added(*down_back.second, grad_w_gate)
+    gate_up_back = Scatter(
+        *(jnp.split(v, depth, axis=1) for v in (grad_w_gate, grad_w_up))
+    )
     gate_up_back.plain()
     gate_up_back.added()
-    grad_w_down = down_back.total()
-    grad_two = after(over_chips(after(grad_two, out_rows)), grad_w_down, *gate_up_back.first)
+    grad_two = after(
+        over_chips(after(grad_two, out_rows)), grad_w_gate, grad_w_up, *gate_up_back.first,
+        *down_back.second, *down_back.third,
+    )
     grad_two = turned(grad_two, axis=1, forth=False).astype(f32)
+    grad_w_down = jnp.concatenate(down_back.total(), axis=0)
 
     grad_norm_ffn = jnp.sum(grad_two * unit_two, axis=0)
     grad_resid = grad_own.astype(f32) + norm_back(grad_two * gain_ffn, unit_two, inverse_two)
     grad_branch = grad_resid.astype(bf16)
-    grad_headed = exchange(against(grad_branch, out_w).astype(bf16), 1, 0)
+    sent_heads = against(grad_branch, out_w).astype(bf16)
+    grad_headed = exchange(sent_heads, 1, 0)
     headed_cores = headed_own.reshape(own_rows, depth, chips, 2, shard).transpose(0, 3, 2, 1, 4)
     headed_cores = turned(headed_cores, axis=3).reshape(own_rows, width)
-    grad_w_out = over_cores(lambda v: contract_rows(v, grad_branch), *split_cores(headed_cores, 1))
-    grad_w_out = grad_w_out.astype(bf16)
-    grad_headed = after(grad_headed, grad_w_out, *gate_up_back.second)
-    grad_w_out = over_chips(grad_w_out)
+    theirs, own = split_cores(headed_cores, 1)
+    branch = after(grad_branch, sent_heads)
+    sent = across(columns_call(theirs, branch))
+    grad_w_out = columns_call(own, branch, after(sent, grad_headed))
+    grad_headed = after(grad_headed, grad_w_out)
+    grad_w_out = over_chips(after(grad_w_out, *gate_up_back.second))
     grad_raw, grad_head, grad_lam = attend_back(
         length_all, lam, rot, grad_headed, cos_table, -sin_table, gain_mine, dims
     )
     grad_raw = grad_raw.reshape(team * own_rows, 6 * DH)
     out_rows = after(out_rows, grad_raw)
     output = jnp.where(valid, residual + out_rows.astype(f32), 0.0).astype(bf16)
-    theirs, mine = split_cores(grad_raw)
-    sent = across(against(theirs, qkv_w))
-    grad_qkv = contract_rows(normed_one, after(grad_raw, sent[0], *gate_up_back.third)).astype(bf16)
-    qkv_back = Scatter(jnp.split(grad_qkv, depth, axis=0))
-    grad_w_gate_up = gate_up_back.total(grad_qkv)
-    grad_w_gate_up = exchange(grad_w_gate_up.astype(bf16).T, 0, 0, TEAM).astype(f32)
-    grad_one = against(after(mine, grad_qkv), qkv_w) + sent[1].astype(f32)
-    unit_mine = split_cores(x_all)[1].astype(f32) * split_cores(inverse_all)[1]
-    grad_norm_attn = turned(jnp.sum(grad_one * unit_mine, axis=0), axis=0, forth=False)
-    grad_one = over_chips(grad_one)
-    grad_w_gate = to_units(grad_w_gate_up[:, :units])
-    grad_w_up = to_units(grad_w_gate_up[:, units:])
+    qkv_w = qkv_ring.joined(0)
+    (sent,) = row_call(against_kernel, 1 - mine, [grad_raw], [qkv_w], [], [], [(width, bf16)])
+    sent = after(sent, *gate_up_back.third)
+    grad_w_gate_up = jnp.concatenate([v.astype(bf16).T for v in gate_up_back.total()], axis=1)
+    grad_w_gate_up = exchange(grad_w_gate_up, 0, 0, TEAM)
+    grad_qkv = columns_call(normed_one, after(grad_raw, sent))
+    qkv_back = Scatter(*halves(jnp.split(grad_qkv, depth, axis=0)))
+    grad_one, norm_sums = row_call(
+        inputs_back_kernel, mine, [grad_raw, x_all, inverse_all], [qkv_w],
+        [after(across(sent), grad_qkv)], [], [(width, bf16)], sums=[((8, width), f32)],
+    )
+    grad_norm_attn = turned(jnp.sum(norm_sums, axis=0), axis=0, forth=False)
+    grad_one = over_chips(after(grad_one, grad_w_gate_up, *qkv_back.first))
+    grad_w_gate, grad_w_up = place_units(grad_w_gate_up, depth, team)
     qkv_back.plain()
     qkv_back.added(grad_w_gate_up)
-    out_back = Scatter(jnp.split(after(grad_w_out, *qkv_back.first), depth, axis=0))
-    out_back.plain()
-    out_back.added()
-    grad_w_out = out_back.total()
+    grad_w_out = scatter_straight(jnp.split(grad_w_out, depth, axis=0))
     grad_lam = grad_lam[0, 0]
     grad_lambda = jnp.concatenate(
         [
@@ -532,7 +750,7 @@
     small_grads = exchange(small_grads, 0, 0, TEAM).reshape(team, depth, -1).sum(axis=0)
     small_grads = lax.all_to_all(small_grads, "z", 0, 0, tiled=True).sum(axis=0)
 
-    grad_qkv = exchange(by_core(qkv_back.total(small_grads, grad_w_gate, grad_w_up)).astype(bf16), 0, 0).astype(f32)
+    grad_qkv = exchange(by_core(jnp.concatenate(qkv_back.total(small_grads, grad_w_gate, grad_w_up, grad_w_out), axis=0)).astype(bf16), 0, 0).astype(f32)
     grad_qkv = grad_qkv.reshape(H, shard, 3, 2 * DH).transpose(2, 1, 0, 3)
     grad_qkv = grad_qkv.reshape(3, shard, width)
 

time: 868 us -> 767 us (0.88)
  Pallas kernels: 43.3 us -> 254 us
  matrix products: 215 us -> 15.6 us
  waiting for transfers between devices: 289 us -> 222 us
  other arithmetic: 86.3 us -> 57.2 us
  local copies, waits for them, and re-layouts: 89.1 us -> 74.2 us
  blocking collectives: 19.5 us -> 7.96 us
    pallas_call x0 -> x15, Pallas kernels: none -> 211 us  [the longest x8 137 us: row_call(): pl.pallas_call(body_kernel, grid_spec=pltpu.PrefetchScalarGridSpec(num_sc...]
    ppermute x39 -> x40, waiting for transfers between devices: 223 us -> 133 us  [permute(): return lax.ppermute(value, 'z', shift(depth, step))]
    dot_general x7 -> x0, matrix products: 85.3 us -> none  [contract_rows(): lax.dot_general(left, right, (((0,), (0,)), ((), ())), preferred_element_...]
    dot_general x5 -> x1, matrix products: 72.3 us -> 7.39 us  [against(): lax.dot_general(left, right, (((1,), (1,)), ((), ())), preferred_element_...]
    dot_general x4 -> x1, matrix products: 57.3 us -> 8.17 us  [product(): return jnp.dot(left, right, preferred_element_type=f32)]
    convert_element_type x4 -> x1, other arithmetic: 25.9 us -> 1.89 us  [body(): grad_branch = grad_resid.astype(bf16)]
    all_gather x3, waiting for transfers between devices: 3.47 us -> 25.2 us  [gather_rows(): return lax.all_gather(block, ROWS, axis=0, tiled=True)]
    all_to_all x7, waiting for transfers between devices: 51.7 us -> 37.5 us  [exchange(): lax.all_to_all(values, order, split_axis=split, concat_axis=joined, tiled...]
  transfers between devices with their start and end apart: 59 -> 60, of which waited for: 25 -> 28; matrix products, arithmetic and copies ran while one was open for 42% -> 14% of each run, Pallas kernels for 5% -> 33%
where the time goes in v2:
time: 767 us; the launch traced here: 752 us
  Pallas kernels  254 us (33%)
  waiting for transfers between devices  222 us (29%)
  starting transfers between devices  104 us (14%)
  local copies, waits for them, and re-layouts  74.2 us (10%)
  other arithmetic  57.2 us (7%)
  between operations  17 us (2%)
  matrix products  15.6 us (2%)
  blocking collectives  7.96 us (1%)
    pallas_call x8, Pallas kernels, row_call(): pl.pallas_call(body_kernel, grid_spec=pltpu.PrefetchScalarGridSpec(num_sc...  137 us
    ppermute x40, waiting for transfers between devices, permute(): return lax.ppermute(value, 'z', shift(depth, step))  133 us
    pallas_call x6, Pallas kernels, columns_call(): pl.pallas_call(columns_kernel, grid=(rows // tile,), in_specs=[pl.BlockSp...  71.9 us
    ppermute x40, starting transfers between devices, permute(): return lax.ppermute(value, 'z', shift(depth, step))  70.5 us
    all_to_all x7, waiting for transfers between devices, exchange(): lax.all_to_all(values, order, split_axis=split, concat_axis=joined, tiled...  37.5 us
    pallas_call x1, Pallas kernels, attend_back(): pl.pallas_call(attend_back_kernel, grid=(slots, batches), in_specs=[smem,...  28.9 us
    all_to_all x7, starting transfers between devices, exchange(): lax.all_to_all(values, order, split_axis=split, concat_axis=joined, tiled...  27.8 us
    all_gather x3, waiting for transfers between devices, gather_rows(): return lax.all_gather(block, ROWS, axis=0, tiled=True)  25.2 us
  transfers between devices with their start and end apart: 60, of which 28 were waited for; matrix products, arithmetic and copies ran while one was open for 14% of the time, Pallas kernels for 33%

profile of v2, /device:TPU:0, one launch (start us, length us, event | category | flops | bytes accessed | tf_op | source)
XLA Modules:
  0.0 752.1 jit_solution(7510421737823619200)
XLA Ops:
  21.0 12.1 %all-to-all-done = bf16[8,64,768]{2,1,0:T(8,128)(2,1)S(1)} async-done(((bf16[8,64,768]{2,1,0:T(8,128)(2,1)}), bf16[8,64,768]{2,1,0:T(8,128)(2,1)S(1)}, u32[]{:S(2)}, u32[]{:S(2)}) %all-to-all-start) | async-done | bytes 786464 | tf_op jit(solution)/shard_map/all_to_all | solution.py:518
  63.2 8.0 %all-gather = f32[8,1,210]{2,1,0:T(1,128)S(1)} all-gather(f32[1,1,210]{2,1,0:T(1,128)S(1)} %bitcast.190), channel_id=1, replica_groups=mesh['z'=4,'y'=2,'x'=2,'c'=2] {'y','x','c'}, dimensions={0}, use_global_device_ids=true | all-gather | bytes 7560 | tf_op jit(solution)/shard_map/all_gather | solution.py:577
  101.1 8.1 %collective-permute-done.10 = bf16[256,768]{1,0:T(8,128)(2,1)S(1)} collective-permute-done((bf16[256,768]{1,0:T(8,128)(2,1)}, bf16[256,768]{1,0:T(8,128)(2,1)S(1)}, u32[]{:S(2)}, u32[]{:S(2)}) %collective-permute-start.10) | collective-permute-done | bytes 393248 | tf_op jit(solution)/shard_map/ppermute | solution.py:414
  117.6 20.8 %shard_map.237 = (f32[3072,1]{1,0:T(8,128)}, bf16[3072,2048]{1,0:T(8,128)(2,1)}, f32[3072,768]{1,0:T(8,128)}) custom-call(s32[1]{0:T(128)} %constant.102.clone.1.first, bf16[3072,2048]{1,0:T(8,128)(2,1)} %all-gather.6.cloned.1.call-done.refs_0_.refs_1_, f32[1,2048]{1,0:T(1,128)} %fusion.29.refs_1_, ...), custom_call_target="tpu_custom_call" | custom-call | flops 1 | bytes 1 | tf_op jit(solution)/shard_map/pallas_call | solution.py:246
  138.4 14.5 %shard_map.238 = (bf16[2,4,2,192,768]{4,3,2,1,0:T(8,128)(2,1)}, bf16[2,4,2,192,256]{4,3,2,1,0:T(8,128)(2,1)S(1)}) custom-call(s32[4,2]{1,0:T(4,128)S(1)} %bitcast.140, f32[1]{0:T(128)} %bitcast.10.lam_ref, f32[2,4,2,192,768]{4,3,2,1,0:T(8,128)} %bitcast.156, f32[384,128]{1,0:T(8,128)S(1)} %get-tuple-element.266.cos_ref, ...), custom_call_target="tpu_custom_call" | custom-call | flops 1 | bytes 1 | tf_op jit(solution)/shard_map/pallas_call | solution.py:173
  158.4 8.3 %fusion = bf16[4,8,64,2048]{3,2,1,0:T(8,128)(2,1)} fusion(s32[]{:T(128)S(6)} %select_n.86, bf16[4,8,64,2048]{3,2,1,0:T(8,128)(2,1)} %all-gather.8.cloned.1.call-done), kind=kLoop, calls=%fused_computation.2 | loop fusion | flops 4194304 | bytes 16777220 | tf_op jit(solution)/shard_map/concatenate | solution.py:509
  166.7 10.9 %collective-permute-done.11.refs_2_.refs_5_ = bf16[1408,512]{1,0:T(8,128)(2,1)} collective-permute-done((bf16[1408,512]{1,0:T(8,128)(2,1)}, bf16[1408,512]{1,0:T(8,128)(2,1)}, u32[]{:S(2)}, u32[]{:S(2)}) %collective-permute-start.11) | collective-permute-done | bytes 1441824 | tf_op jit(solution)/shard_map/ppermute | solution.py:414
  179.9 8.2 %multiply_reduce_fusion.1 = (f32[384]{0:T(512)S(1)}, f32[384,2048]{1,0:T(8,128)S(1)}) fusion(bf16[384,2048]{0,1:T(8,128)(2,1)} %bitcast.151, bf16[2048,2048]{1,0:T(8,128)(2,1)} %bitcast.149, bf16[384,2048]{1,0:T(8,128)(2,1)} %bitcast.148), kind=kOutput, calls=%fused_computation.34 | convolution fusion | flops 3224370688 | bytes 14681600 | tf_op jit(solution)/shard_map/dot_general | solution.py:27
  203.0 15.8 %collective-permute-done.14.refs_4_.refs_7_ = bf16[704,512]{1,0:T(8,128)(2,1)} collective-permute-done((bf16[704,512]{1,0:T(8,128)(2,1)S(1)}, bf16[704,512]{1,0:T(8,128)(2,1)}, u32[]{:S(2)}, u32[]{:S(2)}) %collective-permute-start.14) | collective-permute-done | bytes 720928 | tf_op jit(solution)/shard_map/ppermute | solution.py:414
  218.8 14.3 %collective-permute-done.13.refs_3_.refs_6_ = bf16[704,512]{1,0:T(8,128)(2,1)} collective-permute-done((bf16[704,512]{1,0:T(8,128)(2,1)S(1)}, bf16[704,512]{1,0:T(8,128)(2,1)}, u32[]{:S(2)}, u32[]{:S(2)}) %collective-permute-start.13) | collective-permute-done | bytes 720928 | tf_op jit(solution)/shard_map/ppermute | solution.py:414
  237.0 25.1 %all-gather.10.cloned.1.call-done.refs_0_.right_ref = bf16[3072,2048]{1,0:T(8,128)(2,1)} async-done(((bf16[384,2048]{1,0:T(8,128)(2,1)}), bf16[3072,2048]{1,0:T(8,128)(2,1)}) %all-gather.10.cloned.1.call-update) | async-done | bytes 12582928 | tf_op jit(solution)/shard_map/all_gather | solution.py:514
  262.1 26.6 %shard_map.239 = (f32[3072,704]{1,0:T(8,128)}, f32[3072,704]{1,0:T(8,128)}, bf16[3072,704]{1,0:T(8,128)(2,1)}) custom-call(s32[1]{0:T(128)} %constant.102.clone.1.first, bf16[3072,2048]{1,0:T(8,128)(2,1)} %all-gather.10.cloned.1.call-done.refs_0_.right_ref, bf16[1408,512]{1,0:T(8,128)(2,1)} %bitcast.15.refs_1_.refs_4_, ...), custom_call_target="tpu_custom_call" | custom-call | flops 1 | bytes 1 | tf_op jit(solution)/shard_map/pallas_call | solution.py:246
  302.0 8.0 %collective-permute-done.18 = bf16[88,2048]{1,0:T(8,128)(2,1)S(1)} collective-permute-done((bf16[88,2048]{1,0:T(8,128)(2,1)S(1)}, bf16[88,2048]{1,0:T(8,128)(2,1)S(1)}, u32[]{:S(2)}, u32[]{:S(2)}) %collective-permute-start.18) | collective-permute-done | bytes 360480 | tf_op jit(solution)/shard_map/ppermute | solution.py:414
  315.3 9.6 %shard_map.240 = bf16[1536,2048]{1,0:T(8,128)(2,1)} custom-call(s32[1]{0:T(128)} %bitcast.23.first, bf16[3072,704]{1,0:T(8,128)(2,1)} %get-tuple-element.91.refs_0_.left_ref, bf16[704,2048]{1,0:T(8,128)(2,1)} %constant_dynamic-slice_fusion.2.refs_1_.refs_3_), custom_call_target="tpu_custom_call" | custom-call | flops 1 | bytes 1 | tf_op jit(solution)/shard_map/pallas_call | solution.py:246
  324.9 11.3 %collective-permute-done.19.refs_2_ = bf16[1536,2048]{1,0:T(8,128)(2,1)} collective-permute-done((bf16[1536,2048]{1,0:T(8,128)(2,1)}, bf16[1536,2048]{1,0:T(8,128)(2,1)}, u32[]{:S(2)}, u32[]{:S(2)}) %collective-permute-start.19) | collective-permute-done | bytes 6291488 | tf_op jit(solution)/shard_map/ppermute | solution.py:530
  336.2 10.9 %shard_map.241 = bf16[1536,2048]{1,0:T(8,128)(2,1)} custom-call(s32[1]{0:T(128)} %bitcast.22.first, bf16[3072,704]{1,0:T(8,128)(2,1)} %get-tuple-element.91.refs_0_.left_ref, bf16[704,2048]{1,0:T(8,128)(2,1)} %constant_dynamic-slice_fusion.2.refs_1_.refs_3_, bf16[1536,2048]{1,0:T(8,128)(2,1)} %collective-permute-done.19.refs_2_), custom_call_target="tpu_custom_call" | custom-call | flops 1 | bytes 1 | tf_op jit(solution)/shard_map/pallas_call | solution.py:246
  347.2 22.7 %shard_map.242 = (bf16[3072,704]{1,0:T(8,128)(2,1)}, bf16[3072,704]{1,0:T(8,128)(2,1)}, bf16[1536,2048]{1,0:T(8,128)(2,1)}) custom-call(s32[1]{0:T(128)} %bitcast.23.first, bf16[3072,2048]{1,0:T(8,128)(2,1)} %all-gather.12.cloned.1.call-done.refs_0_.right_ref, f32[3072,704]{1,0:T(8,128)} %get-tuple-element.97.refs_1_, ...), custom_call_target="tpu_custom_call" | custom-call | flops 1 | bytes 1 | tf_op jit(solution)/shard_map/pallas_call | solution.py:246
  370.1 14.3 %shard_map.243 = bf16[704,2048]{1,0:T(8,128)(2,1)} custom-call(bf16[3072,704]{1,0:T(8,128)(2,1)} %get-tuple-element.91.refs_0_.left_ref, bf16[3072,2048]{1,0:T(8,128)(2,1)} %all-gather.12.cloned.1.call-done.refs_0_.right_ref), custom_call_target="tpu_custom_call" | custom-call | flops 1 | bytes 1 | tf_op jit(solution)/shard_map/pallas_call | solution.py:392
  390.6 23.1 %shard_map.244 = (bf16[3072,704]{1,0:T(8,128)(2,1)}, bf16[3072,704]{1,0:T(8,128)(2,1)}, bf16[1536,2048]{1,0:T(8,128)(2,1)}) custom-call(s32[1]{0:T(128)} %bitcast.22.first, bf16[3072,2048]{1,0:T(8,128)(2,1)} %all-gather.12.cloned.1.call-done.refs_0_.right_ref, ...), custom_call_target="tpu_custom_call", output_to_operand_aliasing={{0}: (11, {}), {1}: (12, {})} | custom-call | flops 1 | bytes 1 | tf_op jit(solution)/shard_map/pallas_call | solution.py:246
  421.3 14.2 %shard_map.245 = bf16[704,2048]{1,0:T(8,128)(2,1)} custom-call(bf16[3072,704]{1,0:T(8,128)(2,1)} %get-tuple-element.108.left_ref, bf16[3072,2048]{1,0:T(8,128)(2,1)} %all-gather.10.cloned.1.call-done.refs_0_.right_ref), custom_call_target="tpu_custom_call" | custom-call | flops 1 | bytes 1 | tf_op jit(solution)/shard_map/pallas_call | solution.py:392
  441.7 14.5 %shard_map.246 = bf16[704,2048]{1,0:T(8,128)(2,1)} custom-call(bf16[3072,704]{1,0:T(8,128)(2,1)} %get-tuple-element.110.left_ref, bf16[3072,2048]{1,0:T(8,128)(2,1)} %all-gather.10.cloned.1.call-done.refs_0_.right_ref), custom_call_target="tpu_custom_call" | custom-call | flops 1 | bytes 1 | tf_op jit(solution)/shard_map/pallas_call | solution.py:392
  471.3 14.1 %collective-permute-done.28 = bf16[88,2048]{1,0:T(8,128)(2,1)} collective-permute-done((bf16[88,2048]{1,0:T(8,128)(2,1)}, bf16[88,2048]{1,0:T(8,128)(2,1)}, u32[]{:S(2)}, u32[]{:S(2)}) %collective-permute-start.28) | collective-permute-done | bytes 360480 | tf_op jit(solution)/shard_map/ppermute | solution.py:414
  498.6 7.4 convolution_convert_fusion
  521.2 16.0 %all-to-all-done.3 = bf16[384,8,256]{2,0,1:T(8,128)(2,1)S(1)} async-done(((bf16[384,8,256]{2,0,1:T(8,128)(2,1)}), bf16[384,8,256]{2,0,1:T(8,128)(2,1)S(1)}, u32[]{:S(2)}, u32[]{:S(2)}) %all-to-all-start.3) | async-done | bytes 1572896 | tf_op jit(solution)/shard_map/all_to_all | solution.py:518
  544.6 8.3 %collective-permute-done.33 = bf16[704,512]{1,0:T(8,128)(2,1)} collective-permute-done((bf16[704,512]{1,0:T(8,128)(2,1)}, bf16[704,512]{1,0:T(8,128)(2,1)}, u32[]{:S(2)}, u32[]{:S(2)}) %collective-permute-start.33) | collective-permute-done | bytes 720928 | tf_op jit(solution)/shard_map/ppermute | solution.py:414
  558.2 28.9 %shard_map.249 = (bf16[2,4,2,192,768]{4,3,2,1,0:T(8,128)(2,1)}, f32[1,256]{1,0:T(1,128)S(1)}, f32[1,128]{1,0:T(1,128)S(1)}) custom-call(s32[4,2]{1,0:T(4,128)S(1)} %bitcast.141, f32[1]{0:T(128)} %bitcast.10.lam_ref, bf16[2,4,2,192,768]{4,3,2,1,0:T(8,128)(2,1)} %get-tuple-element.95.rot_ref, bf16[2,4,2,192,256]{4,3,2,1,0:T(8,128)(2,1)S(1)} %bitcast.137, ...), custom_call_target="tpu_custom_call" | custom-call | flops 1 | bytes 1 | tf_op jit(solution)/shard_map/pallas_call | solution.py:194
  587.1 9.7 %shard_map.250 = bf16[1536,2048]{1,0:T(8,128)(2,1)} custom-call(s32[1]{0:T(128)} %bitcast.23.first, bf16[3072,768]{1,0:T(8,128)(2,1)} %bitcast.144, bf16[2048,768]{1,0:T(8,128)(2,1)} %constant_dynamic-update-slice_fusion.refs_2_.refs_1_.refs_3_), custom_call_target="tpu_custom_call" | custom-call | flops 1 | bytes 1 | tf_op jit(solution)/shard_map/pallas_call | solution.py:246
  605.8 15.6 %shard_map.251 = bf16[2048,768]{1,0:T(8,128)(2,1)} custom-call(bf16[3072,2048]{1,0:T(8,128)(2,1)} %get-tuple-element.123.left_ref, bf16[3072,768]{1,0:T(8,128)(2,1)} %bitcast.145), custom_call_target="tpu_custom_call" | custom-call | flops 1 | bytes 1 | tf_op jit(solution)/shard_map/pallas_call | solution.py:392
  627.6 13.0 %shard_map.252 = (bf16[1536,2048]{1,0:T(8,128)(2,1)}, f32[8,2048]{1,0:T(8,128)}) custom-call(s32[1]{0:T(128)} %bitcast.22.first, bf16[3072,768]{1,0:T(8,128)(2,1)} %bitcast.146, bf16[3072,2048]{1,0:T(8,128)(2,1)} %all-gather.6.cloned.1.call-done.refs_0_.refs_1_, f32[3072,1]{1,0:T(8,128)} %get-tuple-element.119.refs_2_, ...), custom_call_target="tpu_custom_call" | custom-call | flops 1 | bytes 1 | tf_op jit(solution)/shard_map/pallas_call | solution.py:246
  672.1 11.5 %all-to-all-done.6 = f32[4,1,208]{2,1,0:T(1,128)S(1)} async-done(((f32[4,1,208]{2,1,0:T(1,128)}), f32[4,1,208]{2,1,0:T(1,128)S(1)}, u32[]{:S(2)}, u32[]{:S(2)}) %all-to-all-start.6) | async-done | bytes 3360 | tf_op jit(solution)/shard_map/all_to_all | solution.py:751
  702.5 8.3 %collective-permute-done.40 = bf16[256,768]{1,0:T(8,128)(2,1)S(1)} collective-permute-done((bf16[256,768]{1,0:T(8,128)(2,1)S(1)}, bf16[256,768]{1,0:T(8,128)(2,1)S(1)}, u32[]{:S(2)}, u32[]{:S(2)}) %collective-permute-start.40) | collective-permute-done | bytes 393248 | tf_op jit(solution)/shard_map/ppermute | solution.py:414
  721.2 8.0 %all-to-all-done.7 = bf16[8,64,768]{2,1,0:T(8,128)(2,1)S(1)} async-done(((bf16[8,64,768]{2,1,0:T(8,128)(2,1)}), bf16[8,64,768]{2,1,0:T(8,128)(2,1)S(1)}, u32[]{:S(2)}, u32[]{:S(2)}) %all-to-all-start.7) | async-done | bytes 786464 | tf_op jit(solution)/shard_map/all_to_all | solution.py:518
  (333 shorter events, 293.2 us)
Async XLA Ops:
  7.2 110.4 %all-gather.6.cloned.1.call-start = ((), (), s32[]{:S(2)}) async-start(), calls=%async_computation.12 | async-start | bytes 14155776 | tf_op jit(solution)/shard_map/all_gather | solution.py:514
  17.2 141.2 %all-gather.8.cloned.1.call-start = ((), (), s32[]{:S(2)}) async-start(), calls=%async_computation.13 | async-start | bytes 9437184 | tf_op jit(solution)/shard_map/all_gather | solution.py:590
  45.1 38.3 %collective-permute-start.4 = (bf16[512,768]{1,0:T(8,128)(2,1)S(1)}, bf16[512,768]{1,0:T(8,128)(2,1)}, u32[]{:S(2)}, u32[]{:S(2)}) collective-permute-start(bf16[512,768]{1,0:T(8,128)(2,1)S(1)} %bitcast.163), channel_id=1, source_target_pairs={{0,8},{8,16},{16,24},{24,0},{1,9},{9,17},{17,25},{25,1},{2,10},{10... | collective-permute-start | bytes 2359304 | tf_op jit(solution)/shard_map/ppermute | solution.py:414
  46.4 37.0 %collective-permute-start.3 = (bf16[512,768]{1,0:T(8,128)(2,1)S(1)}, bf16[512,768]{1,0:T(8,128)(2,1)}, u32[]{:S(2)}, u32[]{:S(2)}) collective-permute-start(bf16[512,768]{1,0:T(8,128)(2,1)S(1)} %bitcast.164), channel_id=1, source_target_pairs={{0,24},{8,0},{16,8},{24,16},{1,25},{9,1},{17,9},{25,17},{2,26},{10... | collective-permute-start | bytes 2359304 | tf_op jit(solution)/shard_map/ppermute | solution.py:414
  83.4 26.6 %all-to-all-start.1 = ((bf16[8,64,1408]{2,1,0:T(8,128)(2,1)}), bf16[8,64,1408]{2,1,0:T(8,128)(2,1)S(1)}, u32[]{:S(2)}, u32[]{:S(2)}) async-start(bf16[8,64,1408]{2,1,0:T(8,128)(2,1)} %bitcast.13), calls=%async_computation.1 | async-start | bytes 2883584 | tf_op jit(solution)/shard_map/all_to_all | solution.py:518
  111.5 55.2 %collective-permute-start.12 = (bf16[1408,512]{1,0:T(8,128)(2,1)}, bf16[1408,512]{1,0:T(8,128)(2,1)}, u32[]{:S(2)}, u32[]{:S(2)}) collective-permute-start(bf16[1408,512]{1,0:T(8,128)(2,1)} %bitcast.15.refs_1_.refs_4_), channel_id=1, source_target_pairs={{0,8},{8,16},{16,24},{24,0},{1,9},{9,17},{17,25},{25,1},{2,10},{10... | collective-permute-start | bytes 4325384 | tf_op jit(solution)/shard_map/ppermute | solution.py:414
  113.1 64.4 %collective-permute-start.11 = (bf16[1408,512]{1,0:T(8,128)(2,1)}, bf16[1408,512]{1,0:T(8,128)(2,1)}, u32[]{:S(2)}, u32[]{:S(2)}) collective-permute-start(bf16[1408,512]{1,0:T(8,128)(2,1)} %bitcast.15.refs_1_.refs_4_), channel_id=1, source_target_pairs={{0,24},{8,0},{16,8},{24,16},{1,25},{9,1},{17,9},{25,17},{2,26},{10... | collective-permute-start | bytes 4325384 | tf_op jit(solution)/shard_map/ppermute | solution.py:414
  158.3 103.8 %all-gather.10.cloned.1.call-start = ((), (), s32[]{:S(2)}) async-start(), calls=%async_computation.14 | async-start | bytes 14155776 | tf_op jit(solution)/shard_map/all_gather | solution.py:514
  191.1 156.1 %all-gather.12.cloned.1.call-start = ((), (), s32[]{:S(2)}) async-start(), calls=%async_computation.16 | async-start | bytes 14155776 | tf_op jit(solution)/shard_map/all_gather | solution.py:514
  196.5 221.0 %reduce-scatter.5.cloned.1.call-start = ((), (), s32[]{:S(2)}) async-start(), calls=%async_computation.15 | async-start | bytes 7864320 | tf_op jit(solution)/shard_map/reduce_scatter | solution.py:534
  199.2 34.0 %collective-permute-start.13 = (bf16[704,512]{1,0:T(8,128)(2,1)S(1)}, bf16[704,512]{1,0:T(8,128)(2,1)}, u32[]{:S(2)}, u32[]{:S(2)}) collective-permute-start(bf16[704,512]{1,0:T(8,128)(2,1)S(1)} %slice.217), channel_id=1, source_target_pairs={{0,24},{8,0},{16,8},{24,16},{1,25},{9,1},{17,9},{25,17},{2,26},{10... | collective-permute-start | bytes 2162696 | tf_op jit(solution)/shard_map/ppermute | solution.py:414
  233.1 55.6 %collective-permute-start.16 = (bf16[176,2048]{1,0:T(8,128)(2,1)}, bf16[176,2048]{1,0:T(8,128)(2,1)}, u32[]{:S(2)}, u32[]{:S(2)}) collective-permute-start(bf16[176,2048]{1,0:T(8,128)(2,1)} %param.23), channel_id=1, source_target_pairs={{0,8},{8,16},{16,24},{24,0},{1,9},{9,17},{17,25},{25,1},{2,10},{10... | collective-permute-start | bytes 2162696 | tf_op jit(solution)/shard_map/ppermute | solution.py:414
  234.2 54.6 %collective-permute-start.15 = (bf16[176,2048]{1,0:T(8,128)(2,1)}, bf16[176,2048]{1,0:T(8,128)(2,1)}, u32[]{:S(2)}, u32[]{:S(2)}) collective-permute-start(bf16[176,2048]{1,0:T(8,128)(2,1)} %param.23), channel_id=1, source_target_pairs={{0,24},{8,0},{16,8},{24,16},{1,25},{9,1},{17,9},{25,17},{2,26},{10... | collective-permute-start | bytes 2162696 | tf_op jit(solution)/shard_map/ppermute | solution.py:414
  347.2 144.6 %reduce-scatter.7.cloned.1.call-start = ((), (), s32[]{:S(2)}) async-start(), calls=%async_computation.17 | async-start | bytes 7864320 | tf_op jit(solution)/shard_map/reduce_scatter | solution.py:534
  386.8 27.0 %collective-permute-start.21 = (bf16[88,2048]{1,0:T(8,128)(2,1)S(1)}, bf16[88,2048]{1,0:T(8,128)(2,1)}, u32[]{:S(2)}, u32[]{:S(2)}) collective-permute-start(bf16[88,2048]{1,0:T(8,128)(2,1)S(1)} %get-tuple-element.241), channel_id=1, source_target_pairs={{0,8},{8,16},{16,24},{24,0},{1,9},{9,17},{17,25},{25,1},{2,10},{10... | collective-permute-start | bytes 1081352 | tf_op jit(solution)/shard_map/ppermute | solution.py:414
  388.3 25.5 %collective-permute-start.22 = (bf16[88,2048]{1,0:T(8,128)(2,1)S(1)}, bf16[88,2048]{1,0:T(8,128)(2,1)}, u32[]{:S(2)}, u32[]{:S(2)}) collective-permute-start(bf16[88,2048]{1,0:T(8,128)(2,1)S(1)} %get-tuple-element.242), channel_id=1, source_target_pairs={{0,24},{8,0},{16,8},{24,16},{1,25},{9,1},{17,9},{25,17},{2,26},{10... | collective-permute-start | bytes 1081352 | tf_op jit(solution)/shard_map/ppermute | solution.py:414
  440.2 51.6 %collective-permute-start.23 = (bf16[704,512]{1,0:T(8,128)(2,1)}, bf16[704,512]{1,0:T(8,128)(2,1)}, u32[]{:S(2)}, u32[]{:S(2)}) collective-permute-start(bf16[704,512]{1,0:T(8,128)(2,1)} %get-tuple-element.234), channel_id=1, source_target_pairs={{0,8},{8,16},{16,24},{24,0},{1,9},{9,17},{17,25},{25,1},{2,10},{10... | collective-permute-start | bytes 2162696 | tf_op jit(solution)/shard_map/ppermute | solution.py:414
  458.8 33.0 %collective-permute-start.24 = (bf16[704,512]{1,0:T(8,128)(2,1)}, bf16[704,512]{1,0:T(8,128)(2,1)}, u32[]{:S(2)}, u32[]{:S(2)}) collective-permute-start(bf16[704,512]{1,0:T(8,128)(2,1)} %get-tuple-element.236), channel_id=1, source_target_pairs={{0,24},{8,0},{16,8},{24,16},{1,25},{9,1},{17,9},{25,17},{2,26},{10... | collective-permute-start | bytes 2162696 | tf_op jit(solution)/shard_map/ppermute | solution.py:414
  463.4 28.4 %collective-permute-start.27 = (bf16[88,2048]{1,0:T(8,128)(2,1)}, bf16[88,2048]{1,0:T(8,128)(2,1)}, u32[]{:S(2)}, u32[]{:S(2)}) collective-permute-start(bf16[88,2048]{1,0:T(8,128)(2,1)} %get-tuple-element.238), channel_id=1, source_target_pairs={{0,8},{8,16},{16,24},{24,0},{1,9},{9,17},{17,25},{25,1},{2,10},{10... | collective-permute-start | bytes 1081352 | tf_op jit(solution)/shard_map/ppermute | solution.py:414
  511.9 25.3 %collective-permute-start.29 = (bf16[1024,2048]{1,0:T(8,128)(2,1)}, bf16[1024,2048]{1,0:T(8,128)(2,1)}, u32[]{:S(2)}, u32[]{:S(2)}) collective-permute-start(bf16[1024,2048]{1,0:T(8,128)(2,1)} %shard_map.247), channel_id=1, source_target_pairs={{0,1},{1,0},{2,3},{3,2},{4,5},{5,4},{6,7},{7,6},{8,9},{9,8},{10,11... | collective-permute-start | bytes 12582920 | tf_op jit(solution)/shard_map/ppermute | solution.py:530
  516.8 147.0 %reduce-scatter.11.cloned.1.call-start = ((), (), s32[]{:S(2)}) async-start(), calls=%async_computation.19 | async-start | bytes 5242880 | tf_op jit(solution)/shard_map/reduce_scatter | solution.py:534
  516.8 27.8 %collective-permute-start.34 = (bf16[704,512]{1,0:T(8,128)(2,1)}, bf16[704,512]{1,0:T(8,128)(2,1)}, u32[]{:S(2)}, u32[]{:S(2)}) collective-permute-start(bf16[704,512]{1,0:T(8,128)(2,1)} %get-tuple-element.233), channel_id=1, source_target_pairs={{0,24},{8,0},{16,8},{24,16},{1,25},{9,1},{17,9},{25,17},{2,26},{10... | collective-permute-start | bytes 2162696 | tf_op jit(solution)/shard_map/ppermute | solution.py:414
  520.0 32.8 %collective-permute-start.33 = (bf16[704,512]{1,0:T(8,128)(2,1)}, bf16[704,512]{1,0:T(8,128)(2,1)}, u32[]{:S(2)}, u32[]{:S(2)}) collective-permute-start(bf16[704,512]{1,0:T(8,128)(2,1)} %get-tuple-element.235), channel_id=1, source_target_pairs={{0,8},{8,16},{16,24},{24,0},{1,9},{9,17},{17,25},{25,1},{2,10},{10... | collective-permute-start | bytes 2162696 | tf_op jit(solution)/shard_map/ppermute | solution.py:414
  555.9 40.9 %collective-permute-start.31 = (bf16[704,512]{1,0:T(8,128)(2,1)S(1)}, bf16[704,512]{1,0:T(8,128)(2,1)S(1)}, u32[]{:S(2)}, u32[]{:S(2)}) collective-permute-start(bf16[704,512]{1,0:T(8,128)(2,1)S(1)} %add_convert_fusion.2), channel_id=1, source_target_pairs={{0,24},{8,0},{16,8},{24,16},{1,25},{9,1},{17,9},{25,17},{2,26},{10... | collective-permute-start | bytes 2162696 | tf_op jit(solution)/shard_map/ppermute | solution.py:414
  557.7 39.1 %collective-permute-start.30 = (bf16[704,512]{1,0:T(8,128)(2,1)S(1)}, bf16[704,512]{1,0:T(8,128)(2,1)S(1)}, u32[]{:S(2)}, u32[]{:S(2)}) collective-permute-start(bf16[704,512]{1,0:T(8,128)(2,1)S(1)} %add_convert_fusion.3), channel_id=1, source_target_pairs={{0,8},{8,16},{16,24},{24,0},{1,9},{9,17},{17,25},{25,1},{2,10},{10... | collective-permute-start | bytes 2162696 | tf_op jit(solution)/shard_map/ppermute | solution.py:414
  596.9 30.7 %collective-permute-start.32 = (bf16[1536,2048]{1,0:T(8,128)(2,1)}, bf16[1536,2048]{1,0:T(8,128)(2,1)}, u32[]{:S(2)}, u32[]{:S(2)}) collective-permute-start(bf16[1536,2048]{1,0:T(8,128)(2,1)} %shard_map.250), channel_id=1, source_target_pairs={{0,1},{1,0},{2,3},{3,2},{4,5},{5,4},{6,7},{7,6},{8,9},{9,8},{10,11... | collective-permute-start | bytes 18874376 | tf_op jit(solution)/shard_map/ppermute | solution.py:530
  602.0 38.6 %all-to-all-start.4 = ((bf16[8,64,1408]{2,1,0:T(8,128)(2,1)}), bf16[8,64,1408]{2,1,0:T(8,128)(2,1)S(1)}, u32[]{:S(2)}, u32[]{:S(2)}) async-start(bf16[8,64,1408]{2,1,0:T(8,128)(2,1)} %bitcast.44), calls=%async_computation.6 | async-start | bytes 2883584 | tf_op jit(solution)/shard_map/all_to_all | solution.py:518
  605.7 129.7 %reduce-scatter.9.cloned.1.call-start = ((), (), s32[]{:S(2)}) async-start(), calls=%async_computation.18 | async-start | bytes 7864320 | tf_op jit(solution)/shard_map/reduce_scatter | solution.py:534
  656.1 46.3 %collective-permute-start.43 = (bf16[256,768]{1,0:T(8,128)(2,1)}, bf16[256,768]{1,0:T(8,128)(2,1)S(1)}, u32[]{:S(2)}, u32[]{:S(2)}) collective-permute-start(bf16[256,768]{1,0:T(8,128)(2,1)} %get-tuple-element.223), channel_id=1, source_target_pairs={{0,24},{8,0},{16,8},{24,16},{1,25},{9,1},{17,9},{25,17},{2,26},{10... | collective-permute-start | bytes 1179656 | tf_op jit(solution)/shard_map/ppermute | solution.py:414
  658.1 44.3 %collective-permute-start.42 = (bf16[256,768]{1,0:T(8,128)(2,1)}, bf16[256,768]{1,0:T(8,128)(2,1)S(1)}, u32[]{:S(2)}, u32[]{:S(2)}) collective-permute-start(bf16[256,768]{1,0:T(8,128)(2,1)} %get-tuple-element.224), channel_id=1, source_target_pairs={{0,8},{8,16},{16,24},{24,0},{1,9},{9,17},{17,25},{25,1},{2,10},{10... | collective-permute-start | bytes 1179656 | tf_op jit(solution)/shard_map/ppermute | solution.py:414
  659.0 24.6 %all-to-all-start.6 = ((f32[4,1,208]{2,1,0:T(1,128)}), f32[4,1,208]{2,1,0:T(1,128)S(1)}, u32[]{:S(2)}, u32[]{:S(2)}) async-start(f32[4,1,208]{2,1,0:T(1,128)} %all_to_all.77), calls=%async_computation.9 | async-start | bytes 8192 | tf_op jit(solution)/shard_map/all_to_all | solution.py:751
  669.6 30.9 %collective-permute-start.38 = (bf16[64,2048]{1,0:T(8,128)(2,1)S(1)}, bf16[64,2048]{1,0:T(8,128)(2,1)S(1)}, u32[]{:S(2)}, u32[]{:S(2)}) collective-permute-start(bf16[64,2048]{1,0:T(8,128)(2,1)S(1)} %get-tuple-element.250), channel_id=1, source_target_pairs={{0,16},{8,24},{16,0},{24,8},{1,17},{9,25},{17,1},{25,9},{2,18},{10... | collective-permute-start | bytes 786440 | tf_op jit(solution)/shard_map/ppermute | solution.py:414
  (70 other events, 1068.4 us)
Sparse Core Ops, SparseCore 0:
  10.8 78.9 all-gather.5
  92.2 55.5 all-gather.7
  191.2 70.8 all-gather.9
  263.8 73.2 all-gather.11
  347.3 70.2 reduce-scatter.4
  420.4 70.2 reduce-scatter.6
  553.0 52.0 reduce-scatter.10
  646.4 70.3 reduce-scatter.8

commit v3 on v2

--- a/solution.py
+++ b/solution.py
@@ -61,145 +61,157 @@
     return (col <= row) & (col < length)
 
 
-def attend_kernel(len_ref, lam_ref, raw_ref, cos_ref, sin_ref, gain_ref, rot_ref, headed_ref):
-    length = len_ref[pl.program_id(0), pl.program_id(1)]
-    lam = lam_ref[0]
-    halves, rows = raw_ref.shape[0], raw_ref.shape[3]
-    total = halves * rows
-    raw = raw_ref[:, 0, 0].reshape(total, 6 * DH)
-    cos_table, sin_table = cos_ref[...], sin_ref[...]
-    turned = [
-        turn(raw[:, part * DH : (part + 1) * DH], cos_table, sin_table).astype(bf16)
-        for part in range(4)
-    ]
-    value = raw[:, 4 * DH :].astype(bf16)
-    rot_ref[:, 0, 0] = jnp.concatenate(turned + [value], axis=1).reshape(halves, rows, 6 * DH)
-    gain = gain_ref[...]
-    step = 128
-    parts = []
-    for start in range(0, total, step):
-        keys = start + step
-        mask = allowed_block(start, step, keys, length)
-        first = softmax_block(turned[0][start:keys], turned[2][:keys], mask)
-        second = softmax_block(turned[1][start:keys], turned[3][:keys], mask)
-        combined = (first - lam * second).astype(bf16)
-        attended = product(combined, value[:keys])
-        parts.append((attended * inverse_rms(attended) * gain).astype(bf16))
-    headed_ref[:, 0, 0] = jnp.concatenate(parts, axis=0).reshape(halves, rows, 2 * DH)
+def attend_kernel(len_ref, lam_ref, raw_ref, cos_ref, sin_ref, gain_ref, rot_ref, headed_ref, probs_ref, kept_ref):
+    for batch in range(raw_ref.shape[2]):
+        length = len_ref[pl.program_id(0), batch]
+        lam = lam_ref[0]
+        halves, rows = raw_ref.shape[0], raw_ref.shape[3]
+        total = halves * rows
+        raw = raw_ref[:, 0, batch].reshape(total, 6 * DH)
+        cos_table, sin_table = cos_ref[...], sin_ref[...]
+        turned = [
+            turn(raw[:, part * DH : (part + 1) * DH], cos_table, sin_table).astype(bf16)
+            for part in range(4)
+        ]
+        value = raw[:, 4 * DH :].astype(bf16)
+        rot_ref[:, 0, batch] = jnp.concatenate(turned + [value], axis=1).reshape(halves, rows, 6 * DH)
+        gain = gain_ref[...]
+        step = 128
+        parts = []
+        for start in range(0, total, step):
+            keys = start + step
+            mask = allowed_block(start, step, keys, length)
+            first = softmax_block(turned[0][start:keys], turned[2][:keys], mask)
+            second = softmax_block(turned[1][start:keys], turned[3][:keys], mask)
+            combined = (first - lam * second).astype(bf16)
+            attended = product(combined, value[:keys])
+            probs_ref[0, batch, 0, start:keys, :keys] = first
+            probs_ref[0, batch, 1, start:keys, :keys] = second
+            kept_ref[0, batch, start:keys] = attended
+            parts.append((attended * inverse_rms(attended) * gain).astype(bf16))
+        headed_ref[:, 0, batch] = jnp.concatenate(parts, axis=0).reshape(halves, rows, 2 * DH)
 
 
 def attend_back_kernel(
-    len_ref, lam_ref, rot_ref, grad_ref, cos_ref, sin_ref, gain_ref,
-    out_ref, head_ref, lam_out_ref, grad_key, grad_value,
+    lam_ref, rot_ref, probs_ref, kept_ref, grad_ref, cos_ref, sin_ref, gain_ref,
+    out_ref, head_ref, lam_out_ref, all_keys, all_values,
 ):
-    first_step = (pl.program_id(0) == 0) & (pl.program_id(1) == 0)
-
-    @pl.when(first_step)
+    @pl.when(pl.program_id(0) == 0)
     def _():
         head_ref[...] = jnp.zeros_like(head_ref)
         lam_out_ref[...] = jnp.zeros_like(lam_out_ref)
 
-    length = len_ref[pl.program_id(0), pl.program_id(1)]
-    lam = lam_ref[0]
-    halves, rows = rot_ref.shape[0], rot_ref.shape[3]
-    total = halves * rows
-    rot = rot_ref[:, 0, 0].reshape(total, 6 * DH)
-    grad_headed = grad_ref[:, 0, 0].reshape(total, 2 * DH).astype(f32)
-    cos_table, sin_table = cos_ref[...], sin_ref[...]
-    query = [rot[:, :DH], rot[:, DH : 2 * DH]]
-    key = [rot[:, 2 * DH : 3 * DH], rot[:, 3 * DH : 4 * DH]]
-    value = rot[:, 4 * DH :]
-    gain = gain_ref[...]
-    step = 128
-    grad_query = [[], []]
-    for start in reversed(range(0, total, step)):
-        keys = start + step
-        mask = allowed_block(start, step, keys, length)
-        first = softmax_block(query[0][start:keys], key[0][:keys], mask)
-        second = softmax_block(query[1][start:keys], key[1][:keys], mask)
-        combined = (first - lam * second).astype(bf16)
-        attended = product(combined, value[:keys])
-        inverse = inverse_rms(attended)
-        unit = attended * inverse
-        grad_head = grad_headed[start:keys]
-        head_ref[...] += jnp.sum(grad_head * unit, axis=0, keepdims=True)
-        grad_attended = norm_back(grad_head * gain, unit, inverse).astype(bf16)
-        grad_comb = against(grad_attended, value[:keys])
-        value_part = contract_rows(combined, grad_attended)
-        inner = [
-            jnp.sum(grad_comb * first, axis=-1, keepdims=True),
-            jnp.sum(grad_comb * second, axis=-1, keepdims=True),
+    for batch in range(rot_ref.shape[2]):
+        grad_key, grad_value = all_keys.at[batch], all_values.at[batch]
+        lam = lam_ref[0]
+        halves, rows = rot_ref.shape[0], rot_ref.shape[3]
+        total = halves * rows
+        rot = rot_ref[:, 0, batch].reshape(total, 6 * DH)
+        grad_headed = grad_ref[:, 0, batch].reshape(total, 2 * DH).astype(f32)
+        cos_table, sin_table = cos_ref[...], sin_ref[...]
+        query = [rot[:, :DH], rot[:, DH : 2 * DH]]
+        key = [rot[:, 2 * DH : 3 * DH], rot[:, 3 * DH : 4 * DH]]
+        value = rot[:, 4 * DH :]
+        gain = gain_ref[...]
+        step = 128
+        grad_query = [[], []]
+        for start in reversed(range(0, total, step)):
+            keys = start + step
+            first = probs_ref[0, batch, 0, start:keys, :keys]
+            second = probs_ref[0, batch, 1, start:keys, :keys]
+            combined = (first - lam * second).astype(bf16)
+            attended = kept_ref[0, batch, start:keys]
+            inverse = inverse_rms(attended)
+            unit = attended * inverse
+            grad_head = grad_headed[start:keys]
+            head_ref[...] += jnp.sum(grad_head * unit, axis=0, keepdims=True)
+            grad_attended = norm_back(grad_head * gain, unit, inverse).astype(bf16)
+            grad_comb = against(grad_attended, value[:keys])
+            value_part = contract_rows(combined, grad_attended)
+            inner = [
+                jnp.sum(grad_comb * first, axis=-1, keepdims=True),
+                jnp.sum(grad_comb * second, axis=-1, keepdims=True),
+            ]
+            lam_out_ref[...] -= jnp.sum(inner[1], axis=0, keepdims=True)
+            grad_scores = [
+                (first * (grad_comb - inner[0])).astype(bf16),
+                (-lam * second * (grad_comb - inner[1])).astype(bf16),
+            ]
+            if keys == total:
+                grad_value[...] = value_part
+            else:
+                grad_value[:keys] += value_part
+            for k in range(2):
+                key_part = contract_rows(grad_scores[k], query[k][start:keys])
+                cols = slice(k * DH, (k + 1) * DH)
+                if keys == total:
+                    grad_key[:, cols] = key_part
+                else:
+                    grad_key[:keys, cols] += key_part
+                grad_query[k].append(product(grad_scores[k], key[k][:keys]) * score_scale)
+        turned = [
+            turn(jnp.concatenate(grad_query[k][::-1], axis=0), cos_table, sin_table).astype(bf16)
+            for k in range(2)
+        ] + [
+            turn(grad_key[:, k * DH : (k + 1) * DH] * score_scale, cos_table, sin_table).astype(bf16)
+            for k in range(2)
         ]
-        lam_out_ref[...] -= jnp.sum(inner[1], axis=0, keepdims=True)
-        grad_scores = [
-            (first * (grad_comb - inner[0])).astype(bf16),
-            (-lam * second * (grad_comb - inner[1])).astype(bf16),
-        ]
-        if keys == total:
-            grad_value[...] = value_part
-        else:
-            grad_value[:keys] += value_part
-        for k in range(2):
-            key_part = contract_rows(grad_scores[k], query[k][start:keys])
-            cols = slice(k * DH, (k + 1) * DH)
-            if keys == total:
-                grad_key[:, cols] = key_part
-            else:
-                grad_key[:keys, cols] += key_part
-            grad_query[k].append(product(grad_scores[k], key[k][:keys]) * score_scale)
-    turned = [
-        turn(jnp.concatenate(grad_query[k][::-1], axis=0), cos_table, sin_table).astype(bf16)
-        for k in range(2)
-    ] + [
-        turn(grad_key[:, k * DH : (k + 1) * DH] * score_scale, cos_table, sin_table).astype(bf16)
-        for k in range(2)
-    ]
-    out_ref[:, 0, 0] = jnp.concatenate(
-        turned + [grad_value[...].astype(bf16)], axis=1
-    ).reshape(halves, rows, 6 * DH)
-
-
-def row_spec(halves, rows, cols):
-    return pl.BlockSpec((halves, 1, 1, rows, cols), lambda j, m: (0, j, m, 0, 0))
+        out_ref[:, 0, batch] = jnp.concatenate(
+            turned + [grad_value[...].astype(bf16)], axis=1
+        ).reshape(halves, rows, 6 * DH)
+
+
+def row_spec(halves, batches, rows, cols):
+    return pl.BlockSpec((halves, 1, batches, rows, cols), lambda j: (0, j, 0, 0, 0))
 
 
 def whole_spec(shape):
-    return pl.BlockSpec(shape, lambda j, m: (0,) * len(shape))
+    return pl.BlockSpec(shape, lambda j: (0,) * len(shape))
+
+
+def slot_spec(*shape):
+    return pl.BlockSpec((1,) + shape, lambda j: (j,) + (0,) * len(shape))
 
 
 def attend(lengths, lam, raw, cos_table, sin_table, gain, dims):
     halves, slots, batches, rows = dims
     smem = pl.BlockSpec(memory_space=pltpu.SMEM)
-    rot, headed = pl.pallas_call(
+    total = halves * rows
+    return pl.pallas_call(
         attend_kernel,
-        grid=(slots, batches),
+        grid=(slots,),
         in_specs=[
-            smem, smem, row_spec(halves, rows, 6 * DH),
+            smem, smem, row_spec(halves, batches, rows, 6 * DH),
             whole_spec(cos_table.shape), whole_spec(sin_table.shape), whole_spec(gain.shape),
         ],
-        out_specs=[row_spec(halves, rows, 6 * DH), row_spec(halves, rows, 2 * DH)],
+        out_specs=[
+            row_spec(halves, batches, rows, 6 * DH), row_spec(halves, batches, rows, 2 * DH),
+            slot_spec(batches, 2, total, total), slot_spec(batches, total, 2 * DH),
+        ],
         out_shape=[
             jax.ShapeDtypeStruct(dims + (6 * DH,), bf16),
             jax.ShapeDtypeStruct(dims + (2 * DH,), bf16),
+            jax.ShapeDtypeStruct((slots, batches, 2, total, total), f32),
+            jax.ShapeDtypeStruct((slots, batches, total, 2 * DH), f32),
         ],
         compiler_params=pltpu.CompilerParams(vmem_limit_bytes=48 * 1024 * 1024),
         cost_estimate=pl.CostEstimate(flops=1, bytes_accessed=1, transcendentals=0),
     )(lengths, lam, raw.reshape(dims + (6 * DH,)), cos_table, sin_table, gain)
-    return rot, headed
-
-
-def attend_back(lengths, lam, rot, grad_headed, cos_table, sin_table, gain, dims):
+
+
+def attend_back(lam, rot, probs, kept, grad_headed, cos_table, sin_table, gain, dims):
     halves, slots, batches, rows = dims
     smem = pl.BlockSpec(memory_space=pltpu.SMEM)
     return pl.pallas_call(
         attend_back_kernel,
-        grid=(slots, batches),
+        grid=(slots,),
         in_specs=[
-            smem, smem, row_spec(halves, rows, 6 * DH), row_spec(halves, rows, 2 * DH),
+            smem, row_spec(halves, batches, rows, 6 * DH), slot_spec(*probs.shape[1:]),
+            slot_spec(*kept.shape[1:]), row_spec(halves, batches, rows, 2 * DH),
             whole_spec(cos_table.shape), whole_spec(sin_table.shape), whole_spec(gain.shape),
         ],
         out_specs=[
-            row_spec(halves, rows, 6 * DH), whole_spec((1, 2 * DH)), whole_spec((1, 128)),
+            row_spec(halves, batches, rows, 6 * DH), whole_spec((1, 2 * DH)), whole_spec((1, 128)),
         ],
         out_shape=[
             jax.ShapeDtypeStruct(dims + (6 * DH,), bf16),
@@ -207,19 +219,19 @@
             jax.ShapeDtypeStruct((1, 128), f32),
         ],
         scratch_shapes=[
-            pltpu.VMEM((halves * rows, 2 * DH), f32),
-            pltpu.VMEM((halves * rows, 2 * DH), f32),
+            pltpu.VMEM((batches, halves * rows, 2 * DH), f32),
+            pltpu.VMEM((batches, halves * rows, 2 * DH), f32),
         ],
         compiler_params=pltpu.CompilerParams(vmem_limit_bytes=48 * 1024 * 1024),
         cost_estimate=pl.CostEstimate(flops=1, bytes_accessed=1, transcendentals=0),
-    )(lengths, lam, rot, grad_headed.reshape(dims + (2 * DH,)), cos_table, sin_table, gain)
-
-
-TILE = 256
+    )(lam, rot, probs, kept, grad_headed.reshape(dims + (2 * DH,)), cos_table, sin_table, gain)
+
+
+TILE = 512
 
 
 def tile_rows(rows):
-    return next(t for t in (TILE, 128, 64, 32, 16) if rows % t == 0)
+    return next(t for t in (TILE, 256, 128, 64, 32, 16) if rows % t == 0)
 
 
 def row_call(
@@ -313,20 +325,27 @@
 
 def gate_up_back_kernel(n_pieces, grad_ref, gate_ref, up_ref, down_ref, *refs):
     pieces, other, (gate_out, up_out, out_ref) = refs[:n_pieces], refs[n_pieces:-3], refs[-3:]
-    grad_hidden = against(grad_ref[...], down_ref[...])
-    gate = gate_ref[...]
-    share = jax.nn.sigmoid(gate)
-    grad_gate = grad_hidden * up_ref[...] * share * (1.0 + gate * (1.0 - share))
-    grad_gate = grad_gate.astype(bf16)
-    grad_up = (grad_hidden * (gate * share)).astype(bf16)
-    gate_out[...] = grad_gate
-    up_out[...] = grad_up
-    for start, gate_part, up_part in column_pieces(pieces, gate_ref.shape[1]):
-        cols = slice(start, start + gate_part.shape[1])
-        grad = product(grad_gate, gate_part) + product(grad_up, up_part)
-        if other:
-            grad += other[0][:, cols].astype(f32)
-        out_ref[:, cols] = grad.astype(bf16)
+    tile = grad_ref.shape[0]
+    block = min(tile, 256)
+    blocks = [slice(start, start + block) for start in range(0, tile, block)]
+    hidden = [against(grad_ref[at, :], down_ref[...]) for at in blocks]
+    grads = []
+    for at, grad_hidden in zip(blocks, hidden, strict=True):
+        gate = gate_ref[at, :]
+        share = jax.nn.sigmoid(gate)
+        grad_gate = grad_hidden * up_ref[at, :] * share * (1.0 + gate * (1.0 - share))
+        grad_gate = grad_gate.astype(bf16)
+        grad_up = (grad_hidden * (gate * share)).astype(bf16)
+        gate_out[at, :] = grad_gate
+        up_out[at, :] = grad_up
+        grads.append((grad_gate, grad_up))
+    for at, (grad_gate, grad_up) in zip(blocks, grads, strict=True):
+        for start, gate_part, up_part in column_pieces(pieces, gate_ref.shape[1]):
+            cols = slice(start, start + gate_part.shape[1])
+            grad = product(grad_gate, gate_part) + product(grad_up, up_part)
+            if other:
+                grad += other[0][at, cols].astype(f32)
+            out_ref[at, cols] = grad.astype(bf16)
 
 
 def place_units_kernel(depth, team, grad_ref, gate_ref, up_ref):
@@ -340,6 +359,23 @@
                 column = (z * team + source) * part
                 start = first + z * part
                 out_ref[:, column : column + part] = rows[:, start : start + part]
+
+
+def place_heads_kernel(grad_ref, *out_refs):
+    shard = out_refs[0].shape[0]
+    for head in range(H):
+        rows = grad_ref[head * shard : (head + 1) * shard, :].astype(f32)
+        for k, out_ref in enumerate(out_refs):
+            out_ref[:, head * 2 * DH : (head + 1) * 2 * DH] = rows[:, k * 2 * DH : (k + 1) * 2 * DH]
+
+
+def place_heads(grad, work):
+    return pl.pallas_call(
+        place_heads_kernel,
+        out_shape=[jax.ShapeDtypeStruct((grad.shape[0] // H, H * 2 * DH), f32)] * 3,
+        compiler_params=pltpu.CompilerParams(vmem_limit_bytes=40 * 1024 * 1024),
+        cost_estimate=pl.CostEstimate(flops=work, bytes_accessed=work // 300, transcendentals=0),
+    )(grad)
 
 
 def place_units(grad, depth, team):
@@ -619,7 +655,7 @@
         [(1, f32), (width, bf16), (6 * DH, f32)], [],
     )
     gate_up_ring = Gather(gate_up, depth)
-    rot, headed = attend(length_all, lam, raw, cos_table, sin_table, gain_mine, dims)
+    rot, headed, probs, kept = attend(length_all, lam, raw, cos_table, sin_table, gain_mine, dims)
     headed_own = exchange(headed.reshape(team * own_rows, 2 * DH), 0, 1)
     headed_own = after(headed_own, *gate_up_ring.first())
 
@@ -704,7 +740,7 @@
     grad_headed = after(grad_headed, grad_w_out)
     grad_w_out = over_chips(after(grad_w_out, *gate_up_back.second))
     grad_raw, grad_head, grad_lam = attend_back(
-        length_all, lam, rot, grad_headed, cos_table, -sin_table, gain_mine, dims
+        lam, rot, probs, kept, grad_headed, cos_table, -sin_table, gain_mine, dims
     )
     grad_raw = grad_raw.reshape(team * own_rows, 6 * DH)
     out_rows = after(out_rows, grad_raw)
@@ -714,18 +750,19 @@
     sent = after(sent, *gate_up_back.third)
     grad_w_gate_up = jnp.concatenate([v.astype(bf16).T for v in gate_up_back.total()], axis=1)
     grad_w_gate_up = exchange(grad_w_gate_up, 0, 0, TEAM)
-    grad_qkv = columns_call(normed_one, after(grad_raw, sent))
-    qkv_back = Scatter(*halves(jnp.split(grad_qkv, depth, axis=0)))
     grad_one, norm_sums = row_call(
         inputs_back_kernel, mine, [grad_raw, x_all, inverse_all], [qkv_w],
-        [after(across(sent), grad_qkv)], [], [(width, bf16)], sums=[((8, width), f32)],
+        [across(sent)], [], [(width, bf16)], sums=[((8, width), f32)],
     )
     grad_norm_attn = turned(jnp.sum(norm_sums, axis=0), axis=0, forth=False)
-    grad_one = over_chips(after(grad_one, grad_w_gate_up, *qkv_back.first))
+    grad_one = after(grad_one, grad_w_gate_up)
+    grad_qkv = columns_call(normed_one, after(grad_raw, grad_one))
+    grad_one = over_chips(grad_one)
+    grad_w_out = scatter_straight(jnp.split(grad_w_out, depth, axis=0))
+    grad_qkv = after(grad_qkv, grad_w_out)
+    qkv_back = Scatter(*halves(jnp.split(grad_qkv, depth, axis=0)))
     grad_w_gate, grad_w_up = place_units(grad_w_gate_up, depth, team)
     qkv_back.plain()
-    qkv_back.added(grad_w_gate_up)
-    grad_w_out = scatter_straight(jnp.split(grad_w_out, depth, axis=0))
     grad_lam = grad_lam[0, 0]
     grad_lambda = jnp.concatenate(
         [
@@ -750,9 +787,8 @@
     small_grads = exchange(small_grads, 0, 0, TEAM).reshape(team, depth, -1).sum(axis=0)
     small_grads = lax.all_to_all(small_grads, "z", 0, 0, tiled=True).sum(axis=0)
 
-    grad_qkv = exchange(by_core(jnp.concatenate(qkv_back.total(small_grads, grad_w_gate, grad_w_up, grad_w_out), axis=0)).astype(bf16), 0, 0).astype(f32)
-    grad_qkv = grad_qkv.reshape(H, shard, 3, 2 * DH).transpose(2, 1, 0, 3)
-    grad_qkv = grad_qkv.reshape(3, shard, width)
+    qkv_back.added(small_grads)
+    grad_qkv = exchange(by_core(jnp.concatenate(qkv_back.total(), axis=0)).astype(bf16), 0, 0)
 
     inverse_one = inverse_rms(x_own)
     grad_one = after(grad_one, small_grads, grad_w_gate, grad_w_up, grad_w_out)
@@ -761,6 +797,8 @@
     input_grad = (
         grad_resid + norm_back(grad_one * gain_attn, unit_one, inverse_one)
     ).astype(bf16)
+
+    grad_qkv = place_heads(grad_qkv, 20 * 10**9)
 
     return (
         output.reshape(inputs.shape),

time: 767 us -> 753 us (0.982)
  Pallas kernels: 254 us -> 238 us
  waiting for transfers between devices: 222 us -> 236 us
  starting transfers between devices: 104 us -> 92 us
  blocking collectives: 7.96 us -> 17.3 us
  local copies, waits for them, and re-layouts: 74.2 us -> 65.3 us
    ppermute x40, waiting for transfers between devices: 133 us -> 149 us  [permute(): return lax.ppermute(value, 'z', shift(depth, step))]
    pallas_call x2 -> x3, Pallas kernels: 43.4 us -> 30.9 us  [the longest x1 15.6 us: attend_back(): pl.pallas_call(attend_back_kernel, grid=(slots,), in_specs=[smem, row_spe...]
    all_to_all x0 -> x1, blocking collectives: none -> 9.32 us  [exchange(): lax.all_to_all(values, order, split_axis=split, concat_axis=joined, tiled...]
    ppermute x40, starting transfers between devices: 70.5 us -> 62.6 us  [permute(): return lax.ppermute(value, 'z', shift(depth, step))]
    all_to_all x7 -> x6, starting transfers between devices: 27.8 us -> 23.9 us  [exchange(): lax.all_to_all(values, order, split_axis=split, concat_axis=joined, tiled...]
    unnamed x111 -> x94, local copies, waits for them, and re-layouts: 21.7 us -> 17.8 us
    all_to_all x7 -> x6, waiting for transfers between devices: 37.5 us -> 40.9 us  [exchange(): lax.all_to_all(values, order, split_axis=split, concat_axis=joined, tiled...]
  transfers between devices with their start and end apart: 60 -> 59, of which waited for: 28 -> 30; matrix products, arithmetic and copies ran while one was open for 14% -> 14% of each run, Pallas kernels for 33% -> 31%
where the time goes in v3:
time: 753 us; the launch traced here: 743 us
  Pallas kernels  238 us (32%)
  waiting for transfers between devices  236 us (31%)
  starting transfers between devices  92 us (12%)
  local copies, waits for them, and re-layouts  65.3 us (9%)
  other arithmetic  62.4 us (8%)
  blocking collectives  17.3 us (2%)
  between operations  16.6 us (2%)
  matrix products  15.6 us (2%)
    ppermute x40, waiting for transfers between devices, permute(): return lax.ppermute(value, 'z', shift(depth, step))  149 us
    pallas_call x8, Pallas kernels, row_call(): pl.pallas_call(body_kernel, grid_spec=pltpu.PrefetchScalarGridSpec(num_sc...  133 us
    pallas_call x6, Pallas kernels, columns_call(): pl.pallas_call(columns_kernel, grid=(rows // tile,), in_specs=[pl.BlockSp...  71.6 us
    ppermute x40, starting transfers between devices, permute(): return lax.ppermute(value, 'z', shift(depth, step))  62.6 us
    all_to_all x6, waiting for transfers between devices, exchange(): lax.all_to_all(values, order, split_axis=split, concat_axis=joined, tiled...  40.9 us
    all_gather x3, waiting for transfers between devices, gather_rows(): return lax.all_gather(block, ROWS, axis=0, tiled=True)  25.5 us
    all_to_all x6, starting transfers between devices, exchange(): lax.all_to_all(values, order, split_axis=split, concat_axis=joined, tiled...  23.9 us
    unnamed x94, local copies, waits for them, and re-layouts  17.8 us
  transfers between devices with their start and end apart: 59, of which 30 were waited for; matrix products, arithmetic and copies ran while one was open for 14% of the time, Pallas kernels for 31%

profile of v3, /device:TPU:0, one launch (start us, length us, event | category | flops | bytes accessed | tf_op | source)
XLA Modules:
  0.0 743.1 jit_solution(4241450601578300791)
XLA Ops:
  21.0 12.1 %all-to-all-done = bf16[8,64,768]{2,1,0:T(8,128)(2,1)S(1)} async-done(((bf16[8,64,768]{2,1,0:T(8,128)(2,1)}), bf16[8,64,768]{2,1,0:T(8,128)(2,1)S(1)}, u32[]{:S(2)}, u32[]{:S(2)}) %all-to-all-start) | async-done | bytes 786464 | tf_op jit(solution)/shard_map/all_to_all | solution.py:554
  63.2 8.0 %all-gather = f32[8,1,210]{2,1,0:T(1,128)S(1)} all-gather(f32[1,1,210]{2,1,0:T(1,128)S(1)} %bitcast.174), channel_id=1, replica_groups=mesh['z'=4,'y'=2,'x'=2,'c'=2] {'y','x','c'}, dimensions={0}, use_global_device_ids=true | all-gather | bytes 7560 | tf_op jit(solution)/shard_map/all_gather | solution.py:613
  101.1 8.0 %collective-permute-done.10 = bf16[256,768]{1,0:T(8,128)(2,1)S(1)} collective-permute-done((bf16[256,768]{1,0:T(8,128)(2,1)}, bf16[256,768]{1,0:T(8,128)(2,1)S(1)}, u32[]{:S(2)}, u32[]{:S(2)}) %collective-permute-start.10) | collective-permute-done | bytes 393248 | tf_op jit(solution)/shard_map/ppermute | solution.py:450
  117.6 18.8 %shard_map.237 = (f32[3072,1]{1,0:T(8,128)}, bf16[3072,2048]{1,0:T(8,128)(2,1)}, f32[3072,768]{1,0:T(8,128)}) custom-call(s32[1]{0:T(128)} %constant.102.clone.1.first, bf16[3072,2048]{1,0:T(8,128)(2,1)} %all-gather.6.cloned.1.call-done.refs_0_.refs_1_, f32[1,2048]{1,0:T(1,128)} %fusion.29.refs_1_, ...), custom_call_target="tpu_custom_call" | custom-call | flops 1 | bytes 1 | tf_op jit(solution)/shard_map/pallas_call | solution.py:258
  136.4 14.0 %shard_map.238 = (bf16[2,4,2,192,768]{4,3,2,1,0:T(8,128)(2,1)}, bf16[2,4,2,192,256]{4,3,2,1,0:T(8,128)(2,1)S(1)}, f32[4,2,2,384,384]{4,3,2,1,0:T(8,128)}, f32[4,2,384,256]{3,2,1,0:T(8,128)S(1)}) custom-call(s32[4,2]{1,0:T(4,128)S(1)} %bitcast.132, f32[1]{0:T(128)} %bitcast.11.lam_ref, f32[2,4,2,192,768]{4,3,2,1,0:T(8,128)} %bitcast.147, ...), custom_call_target="tpu_custom_call" | custom-call | flops 1 | bytes 1 | tf_op jit(solution)/shard_map/pallas_call | solution.py:180
  157.9 8.3 %fusion = bf16[4,8,64,2048]{3,2,1,0:T(8,128)(2,1)} fusion(s32[]{:T(128)S(6)} %select_n.86, bf16[4,8,64,2048]{3,2,1,0:T(8,128)(2,1)} %all-gather.8.cloned.1.call-done), kind=kLoop, calls=%fused_computation.2 | loop fusion | flops 4194304 | bytes 16777220 | tf_op jit(solution)/shard_map/concatenate | solution.py:545
  166.2 11.3 %collective-permute-done.11.refs_2_.refs_5_ = bf16[1408,512]{1,0:T(8,128)(2,1)} collective-permute-done((bf16[1408,512]{1,0:T(8,128)(2,1)}, bf16[1408,512]{1,0:T(8,128)(2,1)}, u32[]{:S(2)}, u32[]{:S(2)}) %collective-permute-start.11) | collective-permute-done | bytes 1441824 | tf_op jit(solution)/shard_map/ppermute | solution.py:450
  179.4 8.2 %multiply_reduce_fusion.1 = (f32[384]{0:T(512)S(1)}, f32[384,2048]{1,0:T(8,128)S(1)}) fusion(bf16[384,2048]{0,1:T(8,128)(2,1)} %bitcast.142, bf16[2048,2048]{1,0:T(8,128)(2,1)} %bitcast.140, bf16[384,2048]{1,0:T(8,128)(2,1)} %bitcast.139), kind=kOutput, calls=%fused_computation.34 | convolution fusion | flops 3224370688 | bytes 14681600 | tf_op jit(solution)/shard_map/dot_general | solution.py:27
  201.9 15.8 %collective-permute-done.14.refs_4_.refs_7_ = bf16[704,512]{1,0:T(8,128)(2,1)} collective-permute-done((bf16[704,512]{1,0:T(8,128)(2,1)S(1)}, bf16[704,512]{1,0:T(8,128)(2,1)}, u32[]{:S(2)}, u32[]{:S(2)}) %collective-permute-start.14) | collective-permute-done | bytes 720928 | tf_op jit(solution)/shard_map/ppermute | solution.py:450
  217.7 14.3 %collective-permute-done.13.refs_3_.refs_6_ = bf16[704,512]{1,0:T(8,128)(2,1)} collective-permute-done((bf16[704,512]{1,0:T(8,128)(2,1)S(1)}, bf16[704,512]{1,0:T(8,128)(2,1)}, u32[]{:S(2)}, u32[]{:S(2)}) %collective-permute-start.13) | collective-permute-done | bytes 720928 | tf_op jit(solution)/shard_map/ppermute | solution.py:450
  236.1 25.4 %all-gather.10.cloned.1.call-done.refs_0_.right_ref = bf16[3072,2048]{1,0:T(8,128)(2,1)} async-done(((bf16[384,2048]{1,0:T(8,128)(2,1)}), bf16[3072,2048]{1,0:T(8,128)(2,1)}) %all-gather.10.cloned.1.call-update) | async-done | bytes 12582928 | tf_op jit(solution)/shard_map/all_gather | solution.py:550
  261.5 26.3 %shard_map.239 = (f32[3072,704]{1,0:T(8,128)}, f32[3072,704]{1,0:T(8,128)}, bf16[3072,704]{1,0:T(8,128)(2,1)}) custom-call(s32[1]{0:T(128)} %constant.102.clone.1.first, bf16[3072,2048]{1,0:T(8,128)(2,1)} %all-gather.10.cloned.1.call-done.refs_0_.right_ref, bf16[1408,512]{1,0:T(8,128)(2,1)} %bitcast.16.refs_1_.refs_4_, ...), custom_call_target="tpu_custom_call" | custom-call | flops 1 | bytes 1 | tf_op jit(solution)/shard_map/pallas_call | solution.py:258
  301.0 8.0 %collective-permute-done.18 = bf16[88,2048]{1,0:T(8,128)(2,1)S(1)} collective-permute-done((bf16[88,2048]{1,0:T(8,128)(2,1)S(1)}, bf16[88,2048]{1,0:T(8,128)(2,1)S(1)}, u32[]{:S(2)}, u32[]{:S(2)}) %collective-permute-start.18) | collective-permute-done | bytes 360480 | tf_op jit(solution)/shard_map/ppermute | solution.py:450
  314.5 8.8 %shard_map.240 = bf16[1536,2048]{1,0:T(8,128)(2,1)} custom-call(s32[1]{0:T(128)} %bitcast.24.first, bf16[3072,704]{1,0:T(8,128)(2,1)} %get-tuple-element.96.refs_0_.left_ref, bf16[704,2048]{1,0:T(8,128)(2,1)} %constant_dynamic-slice_fusion.2.refs_1_.refs_3_), custom_call_target="tpu_custom_call" | custom-call | flops 1 | bytes 1 | tf_op jit(solution)/shard_map/pallas_call | solution.py:258
  323.3 10.5 %collective-permute-done.19.refs_2_ = bf16[1536,2048]{1,0:T(8,128)(2,1)} collective-permute-done((bf16[1536,2048]{1,0:T(8,128)(2,1)}, bf16[1536,2048]{1,0:T(8,128)(2,1)}, u32[]{:S(2)}, u32[]{:S(2)}) %collective-permute-start.19) | collective-permute-done | bytes 6291488 | tf_op jit(solution)/shard_map/ppermute | solution.py:566
  333.8 10.2 %shard_map.241 = bf16[1536,2048]{1,0:T(8,128)(2,1)} custom-call(s32[1]{0:T(128)} %bitcast.23.first, bf16[3072,704]{1,0:T(8,128)(2,1)} %get-tuple-element.96.refs_0_.left_ref, bf16[704,2048]{1,0:T(8,128)(2,1)} %constant_dynamic-slice_fusion.2.refs_1_.refs_3_, bf16[1536,2048]{1,0:T(8,128)(2,1)} %collective-permute-done.19.refs_2_), custom_call_target="tpu_custom_call" | custom-call | flops 1 | bytes 1 | tf_op jit(solution)/shard_map/pallas_call | solution.py:258
  344.6 22.8 %shard_map.242 = (bf16[3072,704]{1,0:T(8,128)(2,1)}, bf16[3072,704]{1,0:T(8,128)(2,1)}, bf16[1536,2048]{1,0:T(8,128)(2,1)}) custom-call(s32[1]{0:T(128)} %bitcast.24.first, bf16[3072,2048]{1,0:T(8,128)(2,1)} %all-gather.12.cloned.1.call-done.refs_0_.right_ref, f32[3072,704]{1,0:T(8,128)} %get-tuple-element.104.refs_1_, ...), custom_call_target="tpu_custom_call" | custom-call | flops 1 | bytes 1 | tf_op jit(solution)/shard_map/pallas_call | solution.py:258
  367.5 14.1 %shard_map.243 = bf16[704,2048]{1,0:T(8,128)(2,1)} custom-call(bf16[3072,704]{1,0:T(8,128)(2,1)} %get-tuple-element.96.refs_0_.left_ref, bf16[3072,2048]{1,0:T(8,128)(2,1)} %all-gather.12.cloned.1.call-done.refs_0_.right_ref), custom_call_target="tpu_custom_call" | custom-call | flops 1 | bytes 1 | tf_op jit(solution)/shard_map/pallas_call | solution.py:428
  387.9 23.9 %shard_map.244 = (bf16[3072,704]{1,0:T(8,128)(2,1)}, bf16[3072,704]{1,0:T(8,128)(2,1)}, bf16[1536,2048]{1,0:T(8,128)(2,1)}) custom-call(s32[1]{0:T(128)} %bitcast.23.first, bf16[3072,2048]{1,0:T(8,128)(2,1)} %all-gather.12.cloned.1.call-done.refs_0_.right_ref, ...), custom_call_target="tpu_custom_call", output_to_operand_aliasing={{0}: (11, {}), {1}: (12, {})} | custom-call | flops 1 | bytes 1 | tf_op jit(solution)/shard_map/pallas_call | solution.py:258
  417.7 14.1 %shard_map.245 = bf16[704,2048]{1,0:T(8,128)(2,1)} custom-call(bf16[3072,704]{1,0:T(8,128)(2,1)} %get-tuple-element.115.left_ref, bf16[3072,2048]{1,0:T(8,128)(2,1)} %all-gather.10.cloned.1.call-done.refs_0_.right_ref), custom_call_target="tpu_custom_call" | custom-call | flops 1 | bytes 1 | tf_op jit(solution)/shard_map/pallas_call | solution.py:428
  438.5 14.5 %shard_map.246 = bf16[704,2048]{1,0:T(8,128)(2,1)} custom-call(bf16[3072,704]{1,0:T(8,128)(2,1)} %get-tuple-element.117.left_ref, bf16[3072,2048]{1,0:T(8,128)(2,1)} %all-gather.10.cloned.1.call-done.refs_0_.right_ref), custom_call_target="tpu_custom_call" | custom-call | flops 1 | bytes 1 | tf_op jit(solution)/shard_map/pallas_call | solution.py:428
  468.1 14.0 %collective-permute-done.28 = bf16[88,2048]{1,0:T(8,128)(2,1)} collective-permute-done((bf16[88,2048]{1,0:T(8,128)(2,1)}, bf16[88,2048]{1,0:T(8,128)(2,1)}, u32[]{:S(2)}, u32[]{:S(2)}) %collective-permute-start.28) | collective-permute-done | bytes 360480 | tf_op jit(solution)/shard_map/ppermute | solution.py:450
  495.1 7.4 convolution_convert_fusion
  518.0 15.8 %all-to-all-done.3 = bf16[384,8,256]{2,0,1:T(8,128)(2,1)S(1)} async-done(((bf16[384,8,256]{2,0,1:T(8,128)(2,1)}), bf16[384,8,256]{2,0,1:T(8,128)(2,1)S(1)}, u32[]{:S(2)}, u32[]{:S(2)}) %all-to-all-start.3) | async-done | bytes 1572896 | tf_op jit(solution)/shard_map/all_to_all | solution.py:554
  541.2 8.5 %collective-permute-done.33 = bf16[704,512]{1,0:T(8,128)(2,1)} collective-permute-done((bf16[704,512]{1,0:T(8,128)(2,1)}, bf16[704,512]{1,0:T(8,128)(2,1)}, u32[]{:S(2)}, u32[]{:S(2)}) %collective-permute-start.33) | collective-permute-done | bytes 720928 | tf_op jit(solution)/shard_map/ppermute | solution.py:450
  555.3 15.6 %shard_map.249 = (bf16[2,4,2,192,768]{4,3,2,1,0:T(8,128)(2,1)}, f32[1,256]{1,0:T(1,128)S(1)}, f32[1,128]{1,0:T(1,128)S(1)}) custom-call(f32[1]{0:T(128)} %bitcast.11.lam_ref, bf16[2,4,2,192,768]{4,3,2,1,0:T(8,128)(2,1)} %get-tuple-element.100.rot_ref, f32[4,2,2,384,384]{4,3,2,1,0:T(8,128)} %get-tuple-element.101.probs_ref, f32[4,2,384,256]{3,2,1,0:T(8,128)S(1)} %copy-done.1, ...), custom_call_target="tpu_custom_call" | custom-call | flops 1 | bytes 1 | tf_op jit(solution)/shard_map/pallas_call | solution.py:205
  570.9 9.0 %shard_map.250 = bf16[1536,2048]{1,0:T(8,128)(2,1)} custom-call(s32[1]{0:T(128)} %bitcast.24.first, bf16[3072,768]{1,0:T(8,128)(2,1)} %bitcast.135, bf16[2048,768]{1,0:T(8,128)(2,1)} %constant_dynamic-update-slice_fusion.refs_2_.refs_1_.refs_3_), custom_call_target="tpu_custom_call" | custom-call | flops 1 | bytes 1 | tf_op jit(solution)/shard_map/pallas_call | solution.py:258
  596.7 13.5 %shard_map.251 = (bf16[1536,2048]{1,0:T(8,128)(2,1)}, f32[8,2048]{1,0:T(8,128)}) custom-call(s32[1]{0:T(128)} %bitcast.23.first, bf16[3072,768]{1,0:T(8,128)(2,1)} %bitcast.136, bf16[3072,2048]{1,0:T(8,128)(2,1)} %all-gather.6.cloned.1.call-done.refs_0_.refs_1_, f32[3072,1]{1,0:T(8,128)} %get-tuple-element.126.refs_2_, ...), custom_call_target="tpu_custom_call" | custom-call | flops 1 | bytes 1 | tf_op jit(solution)/shard_map/pallas_call | solution.py:258
  623.5 15.6 %shard_map.253 = bf16[2048,768]{1,0:T(8,128)(2,1)} custom-call(bf16[3072,2048]{1,0:T(8,128)(2,1)} %get-tuple-element.143.left_ref, bf16[3072,768]{1,0:T(8,128)(2,1)} %bitcast.137), custom_call_target="tpu_custom_call" | custom-call | flops 1 | bytes 1 | tf_op jit(solution)/shard_map/pallas_call | solution.py:428
  650.9 9.3 %all_to_all.90 = f32[8,4,208]{2,1,0:T(4,128)S(1)} all-to-all(f32[8,4,208]{2,1,0:T(4,128)S(1)} %copy.97), channel_id=1, replica_groups=mesh['z'=4,'y'=2,'x'=2,'c'=2] {'y','x','c'}, dimensions={0} | all-to-all | bytes 53248 | tf_op jit(solution)/shard_map/all_to_all | solution.py:554
  678.4 13.4 %collective-permute-done.43 = bf16[256,768]{1,0:T(8,128)(2,1)} collective-permute-done((bf16[256,768]{1,0:T(8,128)(2,1)}, bf16[256,768]{1,0:T(8,128)(2,1)}, u32[]{:S(2)}, u32[]{:S(2)}) %collective-permute-start.43) | collective-permute-done | bytes 393248 | tf_op jit(solution)/shard_map/ppermute | solution.py:450
  691.9 7.7 %collective-permute-done.41 = bf16[256,768]{1,0:T(8,128)(2,1)} collective-permute-done((bf16[256,768]{1,0:T(8,128)(2,1)}, bf16[256,768]{1,0:T(8,128)(2,1)}, u32[]{:S(2)}, u32[]{:S(2)}) %collective-permute-start.41) | collective-permute-done | bytes 393248 | tf_op jit(solution)/shard_map/ppermute | solution.py:450
  (311 shorter events, 299.3 us)
Async XLA Ops:
  7.2 110.3 %all-gather.6.cloned.1.call-start = ((), (), s32[]{:S(2)}) async-start(), calls=%async_computation.12 | async-start | bytes 14155776 | tf_op jit(solution)/shard_map/all_gather | solution.py:550
  17.2 140.6 %all-gather.8.cloned.1.call-start = ((), (), s32[]{:S(2)}) async-start(), calls=%async_computation.13 | async-start | bytes 9437184 | tf_op jit(solution)/shard_map/all_gather | solution.py:626
  45.1 38.3 %collective-permute-start.4 = (bf16[512,768]{1,0:T(8,128)(2,1)S(1)}, bf16[512,768]{1,0:T(8,128)(2,1)}, u32[]{:S(2)}, u32[]{:S(2)}) collective-permute-start(bf16[512,768]{1,0:T(8,128)(2,1)S(1)} %bitcast.153), channel_id=1, source_target_pairs={{0,8},{8,16},{16,24},{24,0},{1,9},{9,17},{17,25},{25,1},{2,10},{10... | collective-permute-start | bytes 2359304 | tf_op jit(solution)/shard_map/ppermute | solution.py:450
  46.4 37.0 %collective-permute-start.3 = (bf16[512,768]{1,0:T(8,128)(2,1)S(1)}, bf16[512,768]{1,0:T(8,128)(2,1)}, u32[]{:S(2)}, u32[]{:S(2)}) collective-permute-start(bf16[512,768]{1,0:T(8,128)(2,1)S(1)} %bitcast.154), channel_id=1, source_target_pairs={{0,24},{8,0},{16,8},{24,16},{1,25},{9,1},{17,9},{25,17},{2,26},{10... | collective-permute-start | bytes 2359304 | tf_op jit(solution)/shard_map/ppermute | solution.py:450
  83.4 26.6 %all-to-all-start.1 = ((bf16[8,64,1408]{2,1,0:T(8,128)(2,1)}), bf16[8,64,1408]{2,1,0:T(8,128)(2,1)S(1)}, u32[]{:S(2)}, u32[]{:S(2)}) async-start(bf16[8,64,1408]{2,1,0:T(8,128)(2,1)} %bitcast.14), calls=%async_computation.1 | async-start | bytes 2883584 | tf_op jit(solution)/shard_map/all_to_all | solution.py:554
  111.5 54.7 %collective-permute-start.12 = (bf16[1408,512]{1,0:T(8,128)(2,1)}, bf16[1408,512]{1,0:T(8,128)(2,1)}, u32[]{:S(2)}, u32[]{:S(2)}) collective-permute-start(bf16[1408,512]{1,0:T(8,128)(2,1)} %bitcast.16.refs_1_.refs_4_), channel_id=1, source_target_pairs={{0,8},{8,16},{16,24},{24,0},{1,9},{9,17},{17,25},{25,1},{2,10},{10... | collective-permute-start | bytes 4325384 | tf_op jit(solution)/shard_map/ppermute | solution.py:450
  113.1 64.4 %collective-permute-start.11 = (bf16[1408,512]{1,0:T(8,128)(2,1)}, bf16[1408,512]{1,0:T(8,128)(2,1)}, u32[]{:S(2)}, u32[]{:S(2)}) collective-permute-start(bf16[1408,512]{1,0:T(8,128)(2,1)} %bitcast.16.refs_1_.refs_4_), channel_id=1, source_target_pairs={{0,24},{8,0},{16,8},{24,16},{1,25},{9,1},{17,9},{25,17},{2,26},{10... | collective-permute-start | bytes 4325384 | tf_op jit(solution)/shard_map/ppermute | solution.py:450
  153.6 24.6 %all-to-all-start.2 = ((bf16[8,384,256]{1,2,0:T(8,128)(2,1)}), bf16[8,384,256]{1,2,0:T(8,128)(2,1)S(1)}, u32[]{:S(2)}, u32[]{:S(2)}) async-start(bf16[8,384,256]{1,2,0:T(8,128)(2,1)} %copy.91), calls=%async_computation.2 | async-start | bytes 3145728 | tf_op jit(solution)/shard_map/all_to_all | solution.py:554
  157.7 103.8 %all-gather.10.cloned.1.call-start = ((), (), s32[]{:S(2)}) async-start(), calls=%async_computation.14 | async-start | bytes 14155776 | tf_op jit(solution)/shard_map/all_gather | solution.py:550
  190.0 154.6 %all-gather.12.cloned.1.call-start = ((), (), s32[]{:S(2)}) async-start(), calls=%async_computation.16 | async-start | bytes 14155776 | tf_op jit(solution)/shard_map/all_gather | solution.py:550
  195.4 218.8 %reduce-scatter.5.cloned.1.call-start = ((), (), s32[]{:S(2)}) async-start(), calls=%async_computation.15 | async-start | bytes 7864320 | tf_op jit(solution)/shard_map/reduce_scatter | solution.py:570
  198.3 33.8 %collective-permute-start.13 = (bf16[704,512]{1,0:T(8,128)(2,1)S(1)}, bf16[704,512]{1,0:T(8,128)(2,1)}, u32[]{:S(2)}, u32[]{:S(2)}) collective-permute-start(bf16[704,512]{1,0:T(8,128)(2,1)S(1)} %slice.202), channel_id=1, source_target_pairs={{0,24},{8,0},{16,8},{24,16},{1,25},{9,1},{17,9},{25,17},{2,26},{10... | collective-permute-start | bytes 2162696 | tf_op jit(solution)/shard_map/ppermute | solution.py:450
  232.1 55.8 %collective-permute-start.16 = (bf16[176,2048]{1,0:T(8,128)(2,1)}, bf16[176,2048]{1,0:T(8,128)(2,1)}, u32[]{:S(2)}, u32[]{:S(2)}) collective-permute-start(bf16[176,2048]{1,0:T(8,128)(2,1)} %param.23), channel_id=1, source_target_pairs={{0,8},{8,16},{16,24},{24,0},{1,9},{9,17},{17,25},{25,1},{2,10},{10... | collective-permute-start | bytes 2162696 | tf_op jit(solution)/shard_map/ppermute | solution.py:450
  232.8 55.1 %collective-permute-start.15 = (bf16[176,2048]{1,0:T(8,128)(2,1)}, bf16[176,2048]{1,0:T(8,128)(2,1)}, u32[]{:S(2)}, u32[]{:S(2)}) collective-permute-start(bf16[176,2048]{1,0:T(8,128)(2,1)} %param.23), channel_id=1, source_target_pairs={{0,24},{8,0},{16,8},{24,16},{1,25},{9,1},{17,9},{25,17},{2,26},{10... | collective-permute-start | bytes 2162696 | tf_op jit(solution)/shard_map/ppermute | solution.py:450
  344.1 144.2 %reduce-scatter.7.cloned.1.call-start = ((), (), s32[]{:S(2)}) async-start(), calls=%async_computation.17 | async-start | bytes 7864320 | tf_op jit(solution)/shard_map/reduce_scatter | solution.py:570
  383.9 27.9 %collective-permute-start.21 = (bf16[88,2048]{1,0:T(8,128)(2,1)S(1)}, bf16[88,2048]{1,0:T(8,128)(2,1)}, u32[]{:S(2)}, u32[]{:S(2)}) collective-permute-start(bf16[88,2048]{1,0:T(8,128)(2,1)S(1)} %get-tuple-element.251), channel_id=1, source_target_pairs={{0,8},{8,16},{16,24},{24,0},{1,9},{9,17},{17,25},{25,1},{2,10},{10... | collective-permute-start | bytes 1081352 | tf_op jit(solution)/shard_map/ppermute | solution.py:450
  385.4 26.4 %collective-permute-start.22 = (bf16[88,2048]{1,0:T(8,128)(2,1)S(1)}, bf16[88,2048]{1,0:T(8,128)(2,1)}, u32[]{:S(2)}, u32[]{:S(2)}) collective-permute-start(bf16[88,2048]{1,0:T(8,128)(2,1)S(1)} %get-tuple-element.252), channel_id=1, source_target_pairs={{0,24},{8,0},{16,8},{24,16},{1,25},{9,1},{17,9},{25,17},{2,26},{10... | collective-permute-start | bytes 1081352 | tf_op jit(solution)/shard_map/ppermute | solution.py:450
  436.9 51.4 %collective-permute-start.23 = (bf16[704,512]{1,0:T(8,128)(2,1)}, bf16[704,512]{1,0:T(8,128)(2,1)}, u32[]{:S(2)}, u32[]{:S(2)}) collective-permute-start(bf16[704,512]{1,0:T(8,128)(2,1)} %get-tuple-element.244), channel_id=1, source_target_pairs={{0,8},{8,16},{16,24},{24,0},{1,9},{9,17},{17,25},{25,1},{2,10},{10... | collective-permute-start | bytes 2162696 | tf_op jit(solution)/shard_map/ppermute | solution.py:450
  455.5 32.8 %collective-permute-start.24 = (bf16[704,512]{1,0:T(8,128)(2,1)}, bf16[704,512]{1,0:T(8,128)(2,1)}, u32[]{:S(2)}, u32[]{:S(2)}) collective-permute-start(bf16[704,512]{1,0:T(8,128)(2,1)} %get-tuple-element.246), channel_id=1, source_target_pairs={{0,24},{8,0},{16,8},{24,16},{1,25},{9,1},{17,9},{25,17},{2,26},{10... | collective-permute-start | bytes 2162696 | tf_op jit(solution)/shard_map/ppermute | solution.py:450
  459.8 28.5 %collective-permute-start.27 = (bf16[88,2048]{1,0:T(8,128)(2,1)}, bf16[88,2048]{1,0:T(8,128)(2,1)}, u32[]{:S(2)}, u32[]{:S(2)}) collective-permute-start(bf16[88,2048]{1,0:T(8,128)(2,1)} %get-tuple-element.248), channel_id=1, source_target_pairs={{0,8},{8,16},{16,24},{24,0},{1,9},{9,17},{17,25},{25,1},{2,10},{10... | collective-permute-start | bytes 1081352 | tf_op jit(solution)/shard_map/ppermute | solution.py:450
  508.5 25.3 %collective-permute-start.29 = (bf16[1024,2048]{1,0:T(8,128)(2,1)}, bf16[1024,2048]{1,0:T(8,128)(2,1)}, u32[]{:S(2)}, u32[]{:S(2)}) collective-permute-start(bf16[1024,2048]{1,0:T(8,128)(2,1)} %shard_map.247), channel_id=1, source_target_pairs={{0,1},{1,0},{2,3},{3,2},{4,5},{5,4},{6,7},{7,6},{8,9},{9,8},{10,11... | collective-permute-start | bytes 12582920 | tf_op jit(solution)/shard_map/ppermute | solution.py:566
  513.4 103.5 %reduce-scatter.11.cloned.1.call-start = ((), (), s32[]{:S(2)}) async-start(), calls=%async_computation.19 | async-start | bytes 5242880 | tf_op jit(solution)/shard_map/reduce_scatter | solution.py:570
  513.4 27.8 %collective-permute-start.34 = (bf16[704,512]{1,0:T(8,128)(2,1)}, bf16[704,512]{1,0:T(8,128)(2,1)}, u32[]{:S(2)}, u32[]{:S(2)}) collective-permute-start(bf16[704,512]{1,0:T(8,128)(2,1)} %get-tuple-element.243), channel_id=1, source_target_pairs={{0,24},{8,0},{16,8},{24,16},{1,25},{9,1},{17,9},{25,17},{2,26},{10... | collective-permute-start | bytes 2162696 | tf_op jit(solution)/shard_map/ppermute | solution.py:450
  516.8 32.8 %collective-permute-start.33 = (bf16[704,512]{1,0:T(8,128)(2,1)}, bf16[704,512]{1,0:T(8,128)(2,1)}, u32[]{:S(2)}, u32[]{:S(2)}) collective-permute-start(bf16[704,512]{1,0:T(8,128)(2,1)} %get-tuple-element.245), channel_id=1, source_target_pairs={{0,8},{8,16},{16,24},{24,0},{1,9},{9,17},{17,25},{25,1},{2,10},{10... | collective-permute-start | bytes 2162696 | tf_op jit(solution)/shard_map/ppermute | solution.py:450
  552.9 27.1 %collective-permute-start.31 = (bf16[704,512]{1,0:T(8,128)(2,1)S(1)}, bf16[704,512]{1,0:T(8,128)(2,1)S(1)}, u32[]{:S(2)}, u32[]{:S(2)}) collective-permute-start(bf16[704,512]{1,0:T(8,128)(2,1)S(1)} %add_convert_fusion.2), channel_id=1, source_target_pairs={{0,24},{8,0},{16,8},{24,16},{1,25},{9,1},{17,9},{25,17},{2,26},{10... | collective-permute-start | bytes 2162696 | tf_op jit(solution)/shard_map/ppermute | solution.py:450
  554.7 31.6 %collective-permute-start.30 = (bf16[704,512]{1,0:T(8,128)(2,1)S(1)}, bf16[704,512]{1,0:T(8,128)(2,1)S(1)}, u32[]{:S(2)}, u32[]{:S(2)}) collective-permute-start(bf16[704,512]{1,0:T(8,128)(2,1)S(1)} %add_convert_fusion.3), channel_id=1, source_target_pairs={{0,8},{8,16},{16,24},{24,0},{1,9},{9,17},{17,25},{25,1},{2,10},{10... | collective-permute-start | bytes 2162696 | tf_op jit(solution)/shard_map/ppermute | solution.py:450
  591.5 25.2 %all-to-all-start.4 = ((bf16[8,64,1408]{2,1,0:T(8,128)(2,1)}), bf16[8,64,1408]{2,1,0:T(8,128)(2,1)S(1)}, u32[]{:S(2)}, u32[]{:S(2)}) async-start(bf16[8,64,1408]{2,1,0:T(8,128)(2,1)} %bitcast.45), calls=%async_computation.6 | async-start | bytes 2883584 | tf_op jit(solution)/shard_map/all_to_all | solution.py:554
  595.1 131.1 %reduce-scatter.9.cloned.1.call-start = ((), (), s32[]{:S(2)}) async-start(), calls=%async_computation.18 | async-start | bytes 7864320 | tf_op jit(solution)/shard_map/reduce_scatter | solution.py:570
  646.4 26.7 %collective-permute-start.39 = (bf16[256,768]{1,0:T(8,128)(2,1)}, bf16[256,768]{1,0:T(8,128)(2,1)}, u32[]{:S(2)}, u32[]{:S(2)}) collective-permute-start(bf16[256,768]{1,0:T(8,128)(2,1)} %get-tuple-element.235), channel_id=1, source_target_pairs={{0,24},{8,0},{16,8},{24,16},{1,25},{9,1},{17,9},{25,17},{2,26},{10... | collective-permute-start | bytes 1179656 | tf_op jit(solution)/shard_map/ppermute | solution.py:450
  648.4 24.7 %collective-permute-start.38 = (bf16[256,768]{1,0:T(8,128)(2,1)}, bf16[256,768]{1,0:T(8,128)(2,1)}, u32[]{:S(2)}, u32[]{:S(2)}) collective-permute-start(bf16[256,768]{1,0:T(8,128)(2,1)} %get-tuple-element.236), channel_id=1, source_target_pairs={{0,8},{8,16},{16,24},{24,0},{1,9},{9,17},{17,25},{25,1},{2,10},{10... | collective-permute-start | bytes 1179656 | tf_op jit(solution)/shard_map/ppermute | solution.py:450
  675.6 24.1 %collective-permute-start.41 = (bf16[256,768]{1,0:T(8,128)(2,1)}, bf16[256,768]{1,0:T(8,128)(2,1)}, u32[]{:S(2)}, u32[]{:S(2)}) collective-permute-start(bf16[256,768]{1,0:T(8,128)(2,1)} %get-tuple-element.237), channel_id=1, source_target_pairs={{0,24},{8,0},{16,8},{24,16},{1,25},{9,1},{17,9},{25,17},{2,26},{10... | collective-permute-start | bytes 1179656 | tf_op jit(solution)/shard_map/ppermute | solution.py:450
  677.9 28.5 %collective-permute-start.40 = (bf16[256,768]{1,0:T(8,128)(2,1)}, bf16[256,768]{1,0:T(8,128)(2,1)}, u32[]{:S(2)}, u32[]{:S(2)}) collective-permute-start(bf16[256,768]{1,0:T(8,128)(2,1)} %get-tuple-element.238), channel_id=1, source_target_pairs={{0,8},{8,16},{16,24},{24,0},{1,9},{9,17},{17,25},{25,1},{2,10},{10... | collective-permute-start | bytes 1179656 | tf_op jit(solution)/shard_map/ppermute | solution.py:450
  (62 other events, 1047.2 us)
Sparse Core Ops, SparseCore 0:
  10.8 78.9 all-gather.5
  92.2 55.5 all-gather.7
  190.1 71.3 all-gather.9
  263.2 72.2 all-gather.11
  344.2 69.9 reduce-scatter.4
  417.1 70.2 reduce-scatter.6
  549.8 54.2 reduce-scatter.10
  616.9 69.2 reduce-scatter.8
